TPU v7x, 128 devices: a whole 4x4x4 slice. The times are simulated.
128 devices in a mesh: ha: 8 (over y, x_lo), ta: 16 (over z, x_hi, core).
Axes of the slice: x: 4 (x_hi: 2, x_lo: 2; x = x_hi * 2 + x_lo), y: 4, z: 4, core: 2. Of those that a mesh axis runs over, the one named last changes fastest.
Arguments:
- latent: bfloat16 [32, 64, 128, 512], P('ta', 'ha'), may hold values from -6 to 6
- w_first: bfloat16 [512, 512], replicated, may hold values from -0.25 to 0.25
- w_second: bfloat16 [512, 512], replicated, may hold values from -0.25 to 0.25
- kernel: bfloat16 [2, 3, 3, 128, 128], replicated, may hold values from -0.125 to 0.125
- cotangent: bfloat16 [32, 128, 256, 128], P('ta', 'ha'), may hold values from -6 to 6
Outputs:
- grad_latent: bfloat16 [32, 64, 128, 512], P('ta', 'ha')
- grad_first: float32 [512, 512], replicated
- grad_second: float32 [512, 512], replicated
- grad_kernel: float32 [2, 3, 3, 128, 128], replicated
All inputs are finite; a program needn't handle non-finite values.
Results may differ from a plain program's by a relative error of at most 0.012.
Values may be sent and summed in bfloat16 or wider, within the bound.
No kernel may reach another device: no remote copies, remote signals or barrier semaphores. Data moves between devices by JAX's collectives and lax.ppermute only.
A program may use at most 192 MiB of HBM per device.

v0:
```python
import functools
import jax
import jax.numpy as jnp
from jax import lax
from jax.experimental import pallas as pl
from jax.experimental.pallas import tpu as pltpu
from jax.sharding import PartitionSpec as P

BF, F32 = jnp.bfloat16, jnp.float32
ROWS = 16
MIB = 1 << 20


def in_hbm(*arrays):
    return [pltpu.with_memory_space_constraint(array, pltpu.HBM) for array in arrays]


def in_vmem(*arrays):
    return [pltpu.with_memory_space_constraint(array, pltpu.VMEM) for array in arrays]


def dot(a, b):
    return jnp.dot(a, b, preferred_element_type=F32)


CHUNK = 512


def forward_kernel(lat_h, w1_h, w2_h, k_h, cot_h, *refs):
    lat, act, slope, ft, taps, w1t, w2t, cot_a, cot_b, w1, w2, ker, sems = refs
    chunks = lat.shape[0] // CHUNK
    weights = [
        pltpu.make_async_copy(src, dst, sems.at[n])
        for n, (src, dst) in enumerate(((w1_h, w1), (w2_h, w2), (k_h, ker)))
    ]
    frames = [
        pltpu.make_async_copy(cot_h.at[n], dst.at[pl.ds(1, ROWS)], sems.at[3 + n])
        for n, dst in enumerate((cot_a, cot_b))
    ]

    def pixels(k):
        where = pl.ds(k * CHUNK, CHUNK)
        return pltpu.make_async_copy(lat_h.at[where], lat.at[where], sems.at[5 + k])

    weights[0].start()
    pixels(0).start()
    weights[1].start()
    for k in range(1, chunks):
        pixels(k).start()
    weights[2].start()
    for copy in frames:
        copy.start()
    weights[0].wait()
    pixels(0).wait()
    weights[1].wait()

    for k in range(chunks):
        if k:
            pixels(k).wait()
        here = slice(k * CHUNK, (k + 1) * CHUNK)
        x = lat[here]
        pre = dot(x, w1[...])
        sig = 0.5 * jnp.tanh(0.5 * pre) + 0.5
        hidden = pre * sig
        slope[here] = (sig + hidden * (1.0 - sig)).astype(BF)
        hidden = hidden.astype(BF)
        act[here] = hidden
        mixed = 0.5 * (x.astype(F32) + dot(hidden, w2[...]))
        ll, lh, hl, hh = (mixed[:, 128 * b : 128 * (b + 1)] for b in range(4))
        s, d, t, u = ll + lh, ll - lh, hl + hh, hl - hh
        for i in range(CHUNK // 128):
            px = slice(128 * i, 128 * (i + 1))
            for p, (m, n) in enumerate(((s, t), (d, u))):
                row = 2 * (k * CHUNK // 128 + i) + p
                frame, row = row // ROWS, row % ROWS
                lanes = slice(128 * row, 128 * (row + 1))
                ft[frame, 0:128, lanes] = (m[px] + n[px]).astype(BF).T
                ft[frame, 128:256, lanes] = (m[px] - n[px]).astype(BF).T
    w1t[...] = w1[...].T
    w2t[...] = w2[...].T
    weights[2].wait()
    for t in range(6):
        for q in range(2):
            col = 3 * (1 - q)
            taps[t, 128 * col : 128 * (col + 1), 128 * q : 128 * (q + 1)] = jnp.zeros((128, 128), BF)
        for dx in range(3):
            tap = ker[3 * t + dx].T
            for q in range(2):
                col = 2 - dx + q
                taps[t, 128 * col : 128 * (col + 1), 128 * q : 128 * (q + 1)] = tap
    for copy in frames:
        copy.wait()


def forward(latent, w1, w2, kernel, cotangent):
    n = latent.shape[0]
    frame = (ROWS + 2,) + cotangent.shape[2:]
    vmem = pl.BlockSpec(memory_space=pltpu.VMEM)
    shapes = [(n, 512), (n, 512), (n, 512), (2, 256, n), (6, 512, 256), (512, 512), (512, 512), frame, frame]
    return pl.pallas_call(
        forward_kernel,
        in_specs=[pl.BlockSpec(memory_space=pl.ANY)] * 5,
        out_specs=[vmem] * len(shapes),
        out_shape=[pltpu.VMEM(shape, BF) for shape in shapes],
        scratch_shapes=[
            pltpu.VMEM((512, 512), BF),
            pltpu.VMEM((512, 512), BF),
            pltpu.VMEM((18, 128, 128), BF),
            pltpu.SemaphoreType.DMA((5 + n // CHUNK,)),
        ],
        cost_estimate=pl.CostEstimate(flops=8 * n * 512 * 512, bytes_accessed=12 * MIB, transcendentals=n * 512),
        compiler_params=pltpu.CompilerParams(vmem_limit_bytes=16 * MIB),
    )(*in_hbm(latent, w1, w2, kernel.reshape(18, 128, 128), cotangent))


def border_kernel(first, second, _, __, cot_a, cot_b):
    odd = lax.axis_index("ha") % 2
    for upper, lower, here in ((second, first, odd == 0), (first, second, odd == 1)):

        @pl.when(here)
        def _():
            for n, cot in enumerate((cot_a, cot_b)):
                cot[0] = upper[n]
                cot[ROWS + 1] = lower[n]


def border(first, second, cot_a, cot_b):
    vmem = pl.BlockSpec(memory_space=pltpu.VMEM)
    return pl.pallas_call(
        border_kernel,
        in_specs=[vmem] * 4,
        out_specs=[vmem] * 2,
        out_shape=[pltpu.VMEM(cot_a.shape, BF)] * 2,
        input_output_aliases={2: 0, 3: 1},
        compiler_params=pltpu.CompilerParams(vmem_limit_bytes=4 * MIB),
    )(*in_vmem(first, second, cot_a, cot_b))


STEP = 4


def half_kernel(frame, *refs):
    refs = list(refs)
    take = lambda n: [refs.pop(0) for _ in range(n)]
    lat, act, slope, ft, taps, w1t, w2t = take(7)
    if frame == 0:
        cot_a, cot_b = take(2)
        gl_h, planes_b, gk, gw = take(4)
        planes_a, spread, gm, gp, gl, sem = take(6)
    else:
        planes_a, cot_b, sumk, sumw, _ = take(5)
        gl_h, keep, send = take(3)
        planes_b, spread, gm, gp, gl, sem, gk, gw = take(8)
    n_px = gm.shape[0]
    base = frame * n_px
    zero = jnp.zeros((8, 128), F32)
    for s in range(spread.shape[0]):
        spread[s, 0:8, :] = zero
        spread[s, 264:272, :] = zero

    def split(cells, planes, row, s):
        spread[s, 8:264, :] = cells.astype(F32)
        for c in range(4):
            planes[row, :, 128 * c : 128 * (c + 1)] = spread[s, pl.ds(7 + c, 128, stride=2), :].astype(BF)

    def split_all(cot, planes):
        def body(r, carry):
            for s in range(2):
                split(cot[2 * r + s], planes, 2 * r + s, s)
            return carry

        lax.fori_loop(0, ROWS // 2 + 1, body, 0)

    if frame == 0:
        split_all(cot_a, planes_a)
    split_all(cot_b, planes_b)

    def back(k, carry):
        y = k * STEP
        total = planes_a[pl.ds(y + 1, STEP), :, 128:384].reshape(STEP * 128, 256).astype(F32)
        for dt, planes in ((1, planes_a), (0, planes_b)):
            for dy in range(3):
                window = planes[pl.ds(y + 2 - dy, STEP)].reshape(STEP * 128, 512)
                total = total + dot(window, taps[3 * dt + dy])
        total = (0.5 * total).reshape(STEP // 2, 2, 128, 256)
        upper = total[:, 0].reshape(STEP * 64, 256)
        lower = total[:, 1].reshape(STEP * 64, 256)
        a, b, c, d = upper[:, :128], upper[:, 128:], lower[:, :128], lower[:, 128:]
        ab, am, cd, cm = a + b, a - b, c + d, c - d
        grad = jnp.concatenate([ab + cd, ab - cd, am + cm, am - cm], axis=1).astype(BF)
        start = pl.multiple_of(k * STEP * 64, STEP * 64)
        here = pl.ds(start, STEP * 64)
        gm[here] = grad
        hidden = (dot(grad, w2t[...]) * slope[pl.ds(base + start, STEP * 64)].astype(F32)).astype(BF)
        gp[here] = hidden
        gl[here] = (grad.astype(F32) + dot(hidden, w1t[...])).astype(BF)
        return carry

    lax.fori_loop(0, ROWS // STEP, back, 0)
    out = pltpu.make_async_copy(gl, gl_h.at[pl.ds(base, n_px)], sem)
    out.start()
    for dt, planes in ((1, planes_a), (0, planes_b)):
        cols = planes.reshape((ROWS + 2) * 128, 512)
        for dy in range(3):
            got = dot(ft[frame], cols[128 * (2 - dy) : 128 * (ROWS + 2 - dy)])
            for dx in range(3):
                col = 2 - dx
                both = got[0:128, 128 * col : 128 * (col + 1)] + got[128:256, 128 * (col + 1) : 128 * (col + 2)]
                where = slice(128 * (9 * dt + 3 * dy + dx), 128 * (9 * dt + 3 * dy + dx + 1))
                gk[where] = both if frame == 0 else sumk[where] + both
    for n, (left, right) in enumerate(((lat, gp), (act, gm))):
        for m in range(2):
            part = lax.dot_general(
                left[pl.ds(base, n_px), 256 * m : 256 * (m + 1)],
                right[...],
                (((0,), (0,)), ((), ())),
                preferred_element_type=F32,
            )
            where = slice(512 * n + 256 * m, 512 * n + 256 * (m + 1))
            gw[where] = part if frame == 0 else sumw[where] + part
    if frame == 1:
        ids = block_ids()
        for r in range(8):
            packed = (keep, send)[r // 4].at[r % 4]
            b = ids[r]
            for lane in range(4):
                packed[128 * lane : 128 * (lane + 1), :] = gw[
                    pl.ds(pl.multiple_of(b * 128, 128), 128), 128 * lane : 128 * (lane + 1)
                ].astype(BF)
            packed[512:800, :] = gk[pl.ds(pl.multiple_of(b * 288, 32), 288), :].astype(BF)
    out.wait()


def half(frame, rest, cells, sums=()):
    n = rest[0].shape[0]
    n_px = n // 2
    vmem = pl.BlockSpec(memory_space=pltpu.VMEM)
    any_ = pl.BlockSpec(memory_space=pl.ANY)
    ops = in_vmem(*rest, *cells)
    specs = [vmem] * len(ops)
    planes = (ROWS + 2, 128, 512)
    sum_shapes = [(2304, 128), (1024, 512)]
    scratch = [pltpu.VMEM(planes, BF), pltpu.VMEM((2, 272, 128), F32)]
    scratch += [pltpu.VMEM((n_px, 512), BF)] * 3 + [pltpu.SemaphoreType.DMA]
    shapes = [pltpu.HBM((n, 512), BF)]
    alias = {}
    if frame == 0:
        shapes += [pltpu.VMEM(planes, BF)] + [pltpu.VMEM(shape, F32) for shape in sum_shapes]
    else:
        grad, gk, gw = sums
        alias = {len(ops) + 2: 0}
        ops += in_vmem(gk, gw) + in_hbm(grad)
        specs += [vmem, vmem, any_]
        shapes += [pltpu.VMEM((4, 800, 128), BF)] * 2
        scratch += [pltpu.VMEM(shape, F32) for shape in sum_shapes]
    return pl.pallas_call(
        functools.partial(half_kernel, frame),
        in_specs=specs,
        out_specs=[any_] + [vmem] * (len(shapes) - 1),
        out_shape=shapes,
        input_output_aliases=alias,
        scratch_shapes=scratch,
        cost_estimate=pl.CostEstimate(flops=10 << 30, bytes_accessed=16 * MIB, transcendentals=0),
        compiler_params=pltpu.CompilerParams(vmem_limit_bytes=24 * MIB),
    )(*ops)


def unpack_kernel(own, near, far, last, other, first_h, second_h, gk_h, gw, gk, sems):
    copies = []
    ids = block_ids()
    for r in range(8):
        b = ids[r]
        piece = (own, near, far, last)[r] if r < 4 else other.at[r - 4]
        wide = pl.ds(pl.multiple_of(b * 128, 128), 128)
        low = pl.ds(pl.multiple_of(b * 288, 32), 288)
        for lane in range(4):
            cols = slice(128 * lane, 128 * (lane + 1))
            gw[wide, cols] = piece[cols, :].astype(F32)
        gk[low, :] = piece[512:800, :].astype(F32)
        copies.append(pltpu.make_async_copy(gk.at[low], gk_h.at[low], sems.at[0, r]))
        copies[-1].start()
        down = pl.ds(pl.multiple_of((b % 4) * 128, 128), 128)
        to_first = pltpu.make_async_copy(gw.at[wide], first_h.at[down], sems.at[1, r])
        to_second = pltpu.make_async_copy(gw.at[wide], second_h.at[down], sems.at[1, r])
        pl.when(b < 4)(to_first.start)
        pl.when(b >= 4)(to_second.start)
        copies.append(to_first)
    for copy in copies:
        copy.wait()


def unpack(*pieces):
    vmem = pl.BlockSpec(memory_space=pltpu.VMEM)
    sds = jax.ShapeDtypeStruct
    return pl.pallas_call(
        unpack_kernel,
        in_specs=[vmem] * 5,
        out_specs=[pl.BlockSpec(memory_space=pl.ANY)] * 3,
        out_shape=[sds((512, 512), F32), sds((512, 512), F32), sds((2304, 128), F32)],
        scratch_shapes=[
            pltpu.VMEM((1024, 512), F32),
            pltpu.VMEM((2304, 128), F32),
            pltpu.SemaphoreType.DMA((2, 8)),
        ],
        compiler_params=pltpu.CompilerParams(vmem_limit_bytes=16 << 20),
    )(*pieces)


BOTH = ("ha", "ta")


def coords(device):
    ha, ta = divmod(device, 16)
    return [(ta // 2 % 2) * 2 + ha % 2, ha // 2, ta // 4, ta % 2]


def device_at(x, y, z, core):
    return (y * 2 + x % 2) * 16 + z * 4 + (x // 2) * 2 + core


def along(axes, move):
    pairs = []
    for device in range(128):
        place = coords(device)
        axis = axes[place[3]]
        place[axis] = move(place[axis])
        pairs.append((device, device_at(*place)))
    return pairs


def step_by(count):
    return lambda place: (place + count) % 4


def rounded(value):
    return lax.reduce_precision(value, 8, 7).astype(BF)


def swap(value):
    return lax.ppermute(value, BOTH, [(i, i ^ 1) for i in range(128)])


def trade(near, far, last, axes):
    across = lax.ppermute(far, BOTH, along(axes, step_by(2)))
    before = lax.ppermute(near, BOTH, along(axes, step_by(1)))
    after = lax.ppermute(last, BOTH, along(axes, step_by(3)))
    return before, across, after


def add4(own, before, across, after):
    return rounded((own.astype(F32) + across.astype(F32)) + (before.astype(F32) + after.astype(F32)))


def place():
    ha, ta = lax.axis_index("ha"), lax.axis_index("ta")
    return (ta // 2 % 2) * 2 + ha % 2, ha // 2, ta // 4, ta % 2


def block_ids():
    x, y, _, core = place()
    ids = []
    for other in range(2):
        owner = core ^ other
        start = jnp.where(owner == 0, x, y)
        ids += [owner * 4 + (start + k) % 4 for k in range(4)]
    return ids


def add2(a, b):
    return rounded(a.astype(F32) + b.astype(F32))


def sum_all(keep, send):
    got = swap(send)
    parts = [add2(keep[k], got[k]) for k in range(4)]
    own = add4(parts[0], *trade(*parts[1:], (0, 1)))
    own = add4(own, *trade(own, own, own, (1, 2)))
    own = add4(own, *trade(own, own, own, (2, 0)))
    before, across, after = trade(own, own, own, (0, 1))
    other = swap(jnp.stack([own, after, across, before]))
    return own, after, across, before, other


def neighbour(value, axis, step):
    count = lax.axis_size(axis)
    return lax.ppermute(value, axis, [(i, i + step) for i in range(count) if 0 <= i + step < count])


def meetings(count):
    inner = [(i, i ^ 1) for i in range(count)]
    outer = [(i, i + 1 if i % 2 else i - 1) for i in range(1, count - 1)]
    return inner, outer


def shards(latent, w_first, w_second, kernel, cotangent):
    width = latent.shape[-1]
    flat = latent.reshape(-1, width)
    odd = lax.axis_index("ha") % 2
    top, bottom = cotangent[:, 0], cotangent[:, -1]
    meet = meetings(lax.axis_size("ha"))
    inner = lax.ppermute(jnp.where(odd == 1, top, bottom), "ha", meet[0])
    outer = lax.ppermute(jnp.where(odd == 1, bottom, top), "ha", meet[1])
    *rest, cot_a, cot_b = forward(flat, w_first, w_second, kernel, cotangent)
    cot_a, cot_b = border(inner, outer, cot_a, cot_b)
    later = neighbour(cot_a, "ta", -1)
    grad, planes, gk, gw = half(0, rest, (cot_a, cot_b))
    grad, keep, send = half(1, rest, (planes, later), (grad, gk, gw))
    first, second, gk = unpack(*sum_all(keep, send))
    return grad.reshape(latent.shape), first, second, gk.reshape(kernel.shape)


def solution(mesh):
    return jax.shard_map(
        shards,
        mesh=mesh,
        in_specs=(P("ta", "ha", None, None), P(), P(), P(), P("ta", "ha", None, None)),
        out_specs=(P("ta", "ha", None, None), P(), P(), P()),
        check_vma=False,
    )
```

profile of v0, /device:TPU:1, one launch (start us, length us, event | category | flops | bytes accessed | tf_op | source)
XLA Modules:
  0.0 98.9 jit_solution(4414768547806813395)
XLA Ops:
  0.6 1.0 %fusion.8 = (bf16[2,256,128]{2,1,0:T(8,128)(2,1)S(1)}, bf16[2,256,128]{2,1,0:T(8,128)(2,1)S(1)}) fusion(pred[]{:T(512)S(6)} %eq.6, bf16[2,16,256,128]{3,2,1,0:T(8,128)(2,1)} %cot_h.1), kind=kLoop, calls=%fused_computation.18 | loop fusion | flops 131072 | bytes 524289 | tf_op jit(solution)/shard_map/jit(_where)/select_n | solution.py:402
  1.6 0.7 collective-permute-start.1
  2.3 4.6 %collective-permute-start = (bf16[2,256,128]{2,1,0:T(8,128)(2,1)S(1)}, bf16[2,256,128]{2,1,0:T(8,128)(2,1)S(1)}, u32[]{:S(2)}, u32[]{:S(2)}) collective-permute-start(bf16[2,256,128]{2,1,0:T(8,128)(2,1)S(1)} %get-tuple-element.47), channel_id=1, source_target_pairs={{0,16},{16,0},{32,48},{48,32},{64,80},{80,64},{96,112},{112,96},{1... | collective-permute-start | bytes 393224 | tf_op jit(solution)/shard_map/ppermute | solution.py:401
  6.9 6.0 %shard_map.84 = (bf16[2048,512]{1,0:T(8,128)(2,1)S(1)}, bf16[2048,512]{1,0:T(8,128)(2,1)S(1)}, bf16[2048,512]{1,0:T(8,128)(2,1)S(1)}, bf16[2,256,2048]{2,1,0:T(8...) custom-call(bf16[2048,512]{1,0:T(8,128)(2,1)} %bitcast.37, ...), custom_call_target="tpu_custom_call" | custom-call | flops 4294967296 | bytes 12582912 | tf_op jit(solution)/shard_map/pallas_call | solution.py:100
  13.0 3.3 %collective-permute-start.2 = (bf16[18,256,128]{2,1,0:T(8,128)(2,1)S(1)}, bf16[18,256,128]{2,1,0:T(8,128)(2,1)S(1)}, u32[]{:S(2)}, u32[]{:S(2)}) collective-permute-start(bf16[18,256,128]{2,1,0:T(8,128)(2,1)S(1)} %get-tuple-element.34.refs_7_), channel_id=1, source_target_pairs={{1,0},{2,1},{3,2},{4,3},{5,4},{6,5},{7,6},{8,7},{9,8},{10,9},{11,1... | collective-permute-start | bytes 3538952 | tf_op jit(solution)/shard_map/ppermute | solution.py:386
  16.4 13.7 %shard_map.86 = (bf16[2048,512]{1,0:T(8,128)(2,1)}, bf16[18,128,512]{2,1,0:T(8,128)(2,1)S(1)}, f32[2304,128]{1,0:T(8,128)S(1)}, f32[1024,512]{1,0:T(8,128)S(1)}) custom-call(bf16[2048,512]{1,0:T(8,128)(2,1)S(1)} %get-tuple-element.25.refs_0_, bf16[2048,512]{1,0:T(8,128)(2,1)S(1)} %get-tuple-element.26.refs_1_, ...), custom_call_target="tpu_custom_call" | custom-call | flops 10737418240 | bytes 16777216 | tf_op jit(solution)/shard_map/pallas_call | solution.py:256
  30.0 2.6 %collective-permute-done.2.refs_8_ = bf16[18,256,128]{2,1,0:T(8,128)(2,1)S(1)} collective-permute-done((bf16[18,256,128]{2,1,0:T(8,128)(2,1)S(1)}, bf16[18,256,128]{2,1,0:T(8,128)(2,1)S(1)}, u32[]{:S(2)}, u32[]{:S(2)}) %collective-permute-start.2) | collective-permute-done | bytes 1179680 | tf_op jit(solution)/shard_map/ppermute | solution.py:386
  32.7 13.4 %shard_map.87 = (bf16[2048,512]{1,0:T(8,128)(2,1)}, bf16[4,800,128]{2,1,0:T(8,128)(2,1)S(1)}, bf16[4,800,128]{2,1,0:T(8,128)(2,1)S(1)}) custom-call(bf16[2048,512]{1,0:T(8,128)(2,1)S(1)} %get-tuple-element.25.refs_0_, bf16[2048,512]{1,0:T(8,128)(2,1)S(1)} %get-tuple-element.26.refs_1_, ...), custom_call_target="tpu_custom_call", output_to_operand_aliasing={{0}: (11, {})} | custom-call | flops 10737418240 | bytes 16777216 | tf_op jit(solution)/shard_map/pallas_call | solution.py:256
  46.2 2.3 %collective-permute-done.3 = bf16[4,800,128]{2,1,0:T(8,128)(2,1)S(1)} collective-permute-done((bf16[4,800,128]{2,1,0:T(8,128)(2,1)S(1)}, bf16[4,800,128]{2,1,0:T(8,128)(2,1)S(1)}, u32[]{:S(2)}, u32[]{:S(2)}) %collective-permute-start.3) | collective-permute-done | bytes 819232 | tf_op jit(solution)/shard_map/ppermute | solution.py:340
  48.7 2.7 %collective-permute-start.4 = (bf16[800,128]{1,0:T(8,128)(2,1)S(1)}, bf16[800,128]{1,0:T(8,128)(2,1)S(1)}, u32[]{:S(2)}, u32[]{:S(2)}) collective-permute-start(bf16[800,128]{1,0:T(8,128)(2,1)S(1)} %get-tuple-element.48), channel_id=1, source_target_pairs={{0,2},{1,65},{2,0},{3,67},{4,6},{5,69},{6,4},{7,71},{8,10},{9,73},... | collective-permute-start | bytes 614408 | tf_op jit(solution)/shard_map/ppermute | solution.py:344
  51.4 1.1 %collective-permute-start.6 = (bf16[800,128]{1,0:T(8,128)(2,1)S(1)}, bf16[800,128]{1,0:T(8,128)(2,1)S(1)}, u32[]{:S(2)}, u32[]{:S(2)}) collective-permute-start(bf16[800,128]{1,0:T(8,128)(2,1)S(1)} %get-tuple-element.49), channel_id=1, source_target_pairs={{0,18},{1,97},{2,16},{3,99},{4,22},{5,101},{6,20},{7,103},{8,26},{... | collective-permute-start | bytes 614408 | tf_op jit(solution)/shard_map/ppermute | solution.py:346
  52.4 0.4 collective-permute-start.5
  52.8 2.3 %collective-permute-done.4 = bf16[800,128]{1,0:T(8,128)(2,1)S(1)} collective-permute-done((bf16[800,128]{1,0:T(8,128)(2,1)S(1)}, bf16[800,128]{1,0:T(8,128)(2,1)S(1)}, u32[]{:S(2)}, u32[]{:S(2)}) %collective-permute-start.4) | collective-permute-done | bytes 204832 | tf_op jit(solution)/shard_map/ppermute | solution.py:344
  55.2 1.1 %collective-permute-done.6 = bf16[800,128]{1,0:T(8,128)(2,1)S(1)} collective-permute-done((bf16[800,128]{1,0:T(8,128)(2,1)S(1)}, bf16[800,128]{1,0:T(8,128)(2,1)S(1)}, u32[]{:S(2)}, u32[]{:S(2)}) %collective-permute-start.6) | collective-permute-done | bytes 204832 | tf_op jit(solution)/shard_map/ppermute | solution.py:346
  56.3 2.3 %collective-permute-done.5 = bf16[800,128]{1,0:T(8,128)(2,1)S(1)} collective-permute-done((bf16[800,128]{1,0:T(8,128)(2,1)S(1)}, bf16[800,128]{1,0:T(8,128)(2,1)S(1)}, u32[]{:S(2)}, u32[]{:S(2)}) %collective-permute-start.5) | collective-permute-done | bytes 204832 | tf_op jit(solution)/shard_map/ppermute | solution.py:345
  58.7 3.5 %collective-permute-start.9 = (bf16[800,128]{1,0:T(8,128)(2,1)S(1)}, bf16[800,128]{1,0:T(8,128)(2,1)S(1)}, u32[]{:S(2)}, u32[]{:S(2)}) collective-permute-start(bf16[800,128]{1,0:T(8,128)(2,1)S(1)} %fusion.2), channel_id=1, source_target_pairs={{0,96},{1,13},{2,98},{3,15},{4,100},{5,1},{6,102},{7,3},{8,104},{9... | collective-permute-start | bytes 614408 | tf_op jit(solution)/shard_map/ppermute | solution.py:346
  62.2 1.6 %collective-permute-start.7 = (bf16[800,128]{1,0:T(8,128)(2,1)S(1)}, bf16[800,128]{1,0:T(8,128)(2,1)S(1)}, u32[]{:S(2)}, u32[]{:S(2)}) collective-permute-start(bf16[800,128]{1,0:T(8,128)(2,1)S(1)} %fusion.2), channel_id=1, source_target_pairs={{0,64},{1,9},{2,66},{3,11},{4,68},{5,13},{6,70},{7,15},{8,72},{9,1... | collective-permute-start | bytes 614408 | tf_op jit(solution)/shard_map/ppermute | solution.py:344
  63.8 1.1 %collective-permute-done.9 = bf16[800,128]{1,0:T(8,128)(2,1)S(1)} collective-permute-done((bf16[800,128]{1,0:T(8,128)(2,1)S(1)}, bf16[800,128]{1,0:T(8,128)(2,1)S(1)}, u32[]{:S(2)}, u32[]{:S(2)}) %collective-permute-start.9) | collective-permute-done | bytes 204832 | tf_op jit(solution)/shard_map/ppermute | solution.py:346
  64.9 5.6 %collective-permute-done.8 = bf16[800,128]{1,0:T(8,128)(2,1)S(1)} collective-permute-done((bf16[800,128]{1,0:T(8,128)(2,1)S(1)}, bf16[800,128]{1,0:T(8,128)(2,1)S(1)}, u32[]{:S(2)}, u32[]{:S(2)}) %collective-permute-start.8) | collective-permute-done | bytes 204832 | tf_op jit(solution)/shard_map/ppermute | solution.py:345
  70.7 0.5 collective-permute-start.12
  71.2 1.0 %collective-permute-start.11 = (bf16[800,128]{1,0:T(8,128)(2,1)S(1)}, bf16[800,128]{1,0:T(8,128)(2,1)S(1)}, u32[]{:S(2)}, u32[]{:S(2)}) collective-permute-start(bf16[800,128]{1,0:T(8,128)(2,1)S(1)} %reduce-precision_convert_fusion.1), channel_id=1, source_target_pairs={{0,4},{1,17},{2,6},{3,19},{4,8},{5,21},{6,10},{7,23},{8,12},{9,25}... | collective-permute-start | bytes 614408 | tf_op jit(solution)/shard_map/ppermute | solution.py:345
  72.2 1.5 %collective-permute-start.10 = (bf16[800,128]{1,0:T(8,128)(2,1)S(1)}, bf16[800,128]{1,0:T(8,128)(2,1)S(1)}, u32[]{:S(2)}, u32[]{:S(2)}) collective-permute-start(bf16[800,128]{1,0:T(8,128)(2,1)S(1)} %reduce-precision_convert_fusion.1), channel_id=1, source_target_pairs={{0,8},{1,3},{2,10},{3,1},{4,12},{5,7},{6,14},{7,5},{8,0},{9,11},{1... | collective-permute-start | bytes 614408 | tf_op jit(solution)/shard_map/ppermute | solution.py:344
  73.7 1.9 %collective-permute-done.12 = bf16[800,128]{1,0:T(8,128)(2,1)S(1)} collective-permute-done((bf16[800,128]{1,0:T(8,128)(2,1)S(1)}, bf16[800,128]{1,0:T(8,128)(2,1)S(1)}, u32[]{:S(2)}, u32[]{:S(2)}) %collective-permute-start.12) | collective-permute-done | bytes 204832 | tf_op jit(solution)/shard_map/ppermute | solution.py:346
  75.6 3.5 %collective-permute-done.11 = bf16[800,128]{1,0:T(8,128)(2,1)S(1)} collective-permute-done((bf16[800,128]{1,0:T(8,128)(2,1)S(1)}, bf16[800,128]{1,0:T(8,128)(2,1)S(1)}, u32[]{:S(2)}, u32[]{:S(2)}) %collective-permute-start.11) | collective-permute-done | bytes 204832 | tf_op jit(solution)/shard_map/ppermute | solution.py:345
  79.3 0.5 collective-permute-start.15
  79.8 3.0 %collective-permute-start.14 = (bf16[800,128]{1,0:T(8,128)(2,1)S(1)}, bf16[800,128]{1,0:T(8,128)(2,1)S(1)}, u32[]{:S(2)}, u32[]{:S(2)}) collective-permute-start(bf16[800,128]{1,0:T(8,128)(2,1)S(1)} %reduce-precision_convert_fusion.own), channel_id=1, source_target_pairs={{0,2},{1,65},{2,0},{3,67},{4,6},{5,69},{6,4},{7,71},{8,10},{9,73},... | collective-permute-start | bytes 614408 | tf_op jit(solution)/shard_map/ppermute | solution.py:344
  82.8 0.5 collective-permute-start.13
  83.3 1.9 %collective-permute-done.15.last = bf16[800,128]{1,0:T(8,128)(2,1)S(1)} collective-permute-done((bf16[800,128]{1,0:T(8,128)(2,1)S(1)}, bf16[800,128]{1,0:T(8,128)(2,1)S(1)}, u32[]{:S(2)}, u32[]{:S(2)}) %collective-permute-start.15) | collective-permute-done | bytes 204832 | tf_op jit(solution)/shard_map/ppermute | solution.py:345
  85.2 2.9 %collective-permute-done.14.far = bf16[800,128]{1,0:T(8,128)(2,1)S(1)} collective-permute-done((bf16[800,128]{1,0:T(8,128)(2,1)S(1)}, bf16[800,128]{1,0:T(8,128)(2,1)S(1)}, u32[]{:S(2)}, u32[]{:S(2)}) %collective-permute-start.14) | collective-permute-done | bytes 204832 | tf_op jit(solution)/shard_map/ppermute | solution.py:344
  88.2 6.6 %collective-permute-start.16 = (bf16[4,800,128]{2,1,0:T(8,128)(2,1)S(1)}, bf16[4,800,128]{2,1,0:T(8,128)(2,1)S(1)}, u32[]{:S(2)}, u32[]{:S(2)}) collective-permute-start(bf16[4,800,128]{2,1,0:T(8,128)(2,1)S(1)} %pad_maximum_fusion), channel_id=1, source_target_pairs={{0,1},{1,0},{2,3},{3,2},{4,5},{5,4},{6,7},{7,6},{8,9},{9,8},{10,11... | collective-permute-start | bytes 2457608 | tf_op jit(solution)/shard_map/ppermute | solution.py:340
  94.8 2.0 %collective-permute-done.16.other = bf16[4,800,128]{2,1,0:T(8,128)(2,1)S(1)} collective-permute-done((bf16[4,800,128]{2,1,0:T(8,128)(2,1)S(1)}, bf16[4,800,128]{2,1,0:T(8,128)(2,1)S(1)}, u32[]{:S(2)}, u32[]{:S(2)}) %collective-permute-start.16) | collective-permute-done | bytes 819232 | tf_op jit(solution)/shard_map/ppermute | solution.py:340
  96.8 1.9 %shard_map.88 = (f32[512,512]{1,0:T(8,128)}, f32[512,512]{1,0:T(8,128)}, f32[2304,128]{1,0:T(8,128)}) custom-call(bf16[800,128]{1,0:T(8,128)(2,1)S(1)} %reduce-precision_convert_fusion.own, bf16[800,128]{1,0:T(8,128)(2,1)S(1)} %collective-permute-done.13.near, bf16[800,128]{1,0:T(8,128)(2,1)S(1)} %collective-permute-done.14.far, ...), custom_call_target="tpu_custom_call" | custom-call | tf_op jit(solution)/shard_map/pallas_call | solution.py:295
  (13 shorter events, 0.8 us)
Async XLA Ops:
  1.6 11.3 %collective-permute-start.1 = (bf16[2,256,128]{2,1,0:T(8,128)(2,1)S(1)}, bf16[2,256,128]{2,1,0:T(8,128)(2,1)S(1)}, u32[]{:S(2)}, u32[]{:S(2)}) collective-permute-start(bf16[2,256,128]{2,1,0:T(8,128)(2,1)S(1)} %get-tuple-element.46), channel_id=1, source_target_pairs={{16,32},{32,16},{48,64},{64,48},{80,96},{96,80},{17,33},{33,17},{4... | collective-permute-start | bytes 393224 | tf_op jit(solution)/shard_map/ppermute | solution.py:402
  2.3 10.7 %collective-permute-start = (bf16[2,256,128]{2,1,0:T(8,128)(2,1)S(1)}, bf16[2,256,128]{2,1,0:T(8,128)(2,1)S(1)}, u32[]{:S(2)}, u32[]{:S(2)}) collective-permute-start(bf16[2,256,128]{2,1,0:T(8,128)(2,1)S(1)} %get-tuple-element.47), channel_id=1, source_target_pairs={{0,16},{16,0},{32,48},{48,32},{64,80},{80,64},{96,112},{112,96},{1... | collective-permute-start | bytes 393224 | tf_op jit(solution)/shard_map/ppermute | solution.py:401
  13.0 19.7 %collective-permute-start.2 = (bf16[18,256,128]{2,1,0:T(8,128)(2,1)S(1)}, bf16[18,256,128]{2,1,0:T(8,128)(2,1)S(1)}, u32[]{:S(2)}, u32[]{:S(2)}) collective-permute-start(bf16[18,256,128]{2,1,0:T(8,128)(2,1)S(1)} %get-tuple-element.34.refs_7_), channel_id=1, source_target_pairs={{1,0},{2,1},{3,2},{4,3},{5,4},{6,5},{7,6},{8,7},{9,8},{10,9},{11,1... | collective-permute-start | bytes 3538952 | tf_op jit(solution)/shard_map/ppermute | solution.py:386
  46.1 2.4 %collective-permute-start.3 = (bf16[4,800,128]{2,1,0:T(8,128)(2,1)S(1)}, bf16[4,800,128]{2,1,0:T(8,128)(2,1)S(1)}, u32[]{:S(2)}, u32[]{:S(2)}) collective-permute-start(bf16[4,800,128]{2,1,0:T(8,128)(2,1)S(1)} %get-tuple-element.42), channel_id=1, source_target_pairs={{0,1},{1,0},{2,3},{3,2},{4,5},{5,4},{6,7},{7,6},{8,9},{9,8},{10,11... | collective-permute-start | bytes 2457608 | tf_op jit(solution)/shard_map/ppermute | solution.py:340
  48.7 6.5 %collective-permute-start.4 = (bf16[800,128]{1,0:T(8,128)(2,1)S(1)}, bf16[800,128]{1,0:T(8,128)(2,1)S(1)}, u32[]{:S(2)}, u32[]{:S(2)}) collective-permute-start(bf16[800,128]{1,0:T(8,128)(2,1)S(1)} %get-tuple-element.48), channel_id=1, source_target_pairs={{0,2},{1,65},{2,0},{3,67},{4,6},{5,69},{6,4},{7,71},{8,10},{9,73},... | collective-permute-start | bytes 614408 | tf_op jit(solution)/shard_map/ppermute | solution.py:344
  51.4 4.9 %collective-permute-start.6 = (bf16[800,128]{1,0:T(8,128)(2,1)S(1)}, bf16[800,128]{1,0:T(8,128)(2,1)S(1)}, u32[]{:S(2)}, u32[]{:S(2)}) collective-permute-start(bf16[800,128]{1,0:T(8,128)(2,1)S(1)} %get-tuple-element.49), channel_id=1, source_target_pairs={{0,18},{1,97},{2,16},{3,99},{4,22},{5,101},{6,20},{7,103},{8,26},{... | collective-permute-start | bytes 614408 | tf_op jit(solution)/shard_map/ppermute | solution.py:346
  52.4 6.1 %collective-permute-start.5 = (bf16[800,128]{1,0:T(8,128)(2,1)S(1)}, bf16[800,128]{1,0:T(8,128)(2,1)S(1)}, u32[]{:S(2)}, u32[]{:S(2)}) collective-permute-start(bf16[800,128]{1,0:T(8,128)(2,1)S(1)} %get-tuple-element.50), channel_id=1, source_target_pairs={{0,16},{1,33},{2,18},{3,35},{4,20},{5,37},{6,22},{7,39},{8,24},{9,... | collective-permute-start | bytes 614408 | tf_op jit(solution)/shard_map/ppermute | solution.py:345
  58.7 6.2 %collective-permute-start.9 = (bf16[800,128]{1,0:T(8,128)(2,1)S(1)}, bf16[800,128]{1,0:T(8,128)(2,1)S(1)}, u32[]{:S(2)}, u32[]{:S(2)}) collective-permute-start(bf16[800,128]{1,0:T(8,128)(2,1)S(1)} %fusion.2), channel_id=1, source_target_pairs={{0,96},{1,13},{2,98},{3,15},{4,100},{5,1},{6,102},{7,3},{8,104},{9... | collective-permute-start | bytes 614408 | tf_op jit(solution)/shard_map/ppermute | solution.py:346
  62.2 8.3 %collective-permute-start.8 = (bf16[800,128]{1,0:T(8,128)(2,1)S(1)}, bf16[800,128]{1,0:T(8,128)(2,1)S(1)}, u32[]{:S(2)}, u32[]{:S(2)}) collective-permute-start(bf16[800,128]{1,0:T(8,128)(2,1)S(1)} %fusion.2), channel_id=1, source_target_pairs={{0,32},{1,5},{2,34},{3,7},{4,36},{5,9},{6,38},{7,11},{8,40},{9,13}... | collective-permute-start | bytes 614408 | tf_op jit(solution)/shard_map/ppermute | solution.py:345
  62.2 8.3 %collective-permute-start.7 = (bf16[800,128]{1,0:T(8,128)(2,1)S(1)}, bf16[800,128]{1,0:T(8,128)(2,1)S(1)}, u32[]{:S(2)}, u32[]{:S(2)}) collective-permute-start(bf16[800,128]{1,0:T(8,128)(2,1)S(1)} %fusion.2), channel_id=1, source_target_pairs={{0,64},{1,9},{2,66},{3,11},{4,68},{5,13},{6,70},{7,15},{8,72},{9,1... | collective-permute-start | bytes 614408 | tf_op jit(solution)/shard_map/ppermute | solution.py:344
  70.7 5.0 %collective-permute-start.12 = (bf16[800,128]{1,0:T(8,128)(2,1)S(1)}, bf16[800,128]{1,0:T(8,128)(2,1)S(1)}, u32[]{:S(2)}, u32[]{:S(2)}) collective-permute-start(bf16[800,128]{1,0:T(8,128)(2,1)S(1)} %reduce-precision_convert_fusion.1), channel_id=1, source_target_pairs={{0,12},{1,19},{2,14},{3,17},{4,0},{5,23},{6,2},{7,21},{8,4},{9,27}... | collective-permute-start | bytes 614408 | tf_op jit(solution)/shard_map/ppermute | solution.py:346
  71.2 8.0 %collective-permute-start.11 = (bf16[800,128]{1,0:T(8,128)(2,1)S(1)}, bf16[800,128]{1,0:T(8,128)(2,1)S(1)}, u32[]{:S(2)}, u32[]{:S(2)}) collective-permute-start(bf16[800,128]{1,0:T(8,128)(2,1)S(1)} %reduce-precision_convert_fusion.1), channel_id=1, source_target_pairs={{0,4},{1,17},{2,6},{3,19},{4,8},{5,21},{6,10},{7,23},{8,12},{9,25}... | collective-permute-start | bytes 614408 | tf_op jit(solution)/shard_map/ppermute | solution.py:345
  72.2 7.0 %collective-permute-start.10 = (bf16[800,128]{1,0:T(8,128)(2,1)S(1)}, bf16[800,128]{1,0:T(8,128)(2,1)S(1)}, u32[]{:S(2)}, u32[]{:S(2)}) collective-permute-start(bf16[800,128]{1,0:T(8,128)(2,1)S(1)} %reduce-precision_convert_fusion.1), channel_id=1, source_target_pairs={{0,8},{1,3},{2,10},{3,1},{4,12},{5,7},{6,14},{7,5},{8,0},{9,11},{1... | collective-permute-start | bytes 614408 | tf_op jit(solution)/shard_map/ppermute | solution.py:344
  79.3 5.9 %collective-permute-start.15 = (bf16[800,128]{1,0:T(8,128)(2,1)S(1)}, bf16[800,128]{1,0:T(8,128)(2,1)S(1)}, u32[]{:S(2)}, u32[]{:S(2)}) collective-permute-start(bf16[800,128]{1,0:T(8,128)(2,1)S(1)} %reduce-precision_convert_fusion.own), channel_id=1, source_target_pairs={{0,16},{1,33},{2,18},{3,35},{4,20},{5,37},{6,22},{7,39},{8,24},{9,... | collective-permute-start | bytes 614408 | tf_op jit(solution)/shard_map/ppermute | solution.py:345
  79.8 8.3 %collective-permute-start.14 = (bf16[800,128]{1,0:T(8,128)(2,1)S(1)}, bf16[800,128]{1,0:T(8,128)(2,1)S(1)}, u32[]{:S(2)}, u32[]{:S(2)}) collective-permute-start(bf16[800,128]{1,0:T(8,128)(2,1)S(1)} %reduce-precision_convert_fusion.own), channel_id=1, source_target_pairs={{0,2},{1,65},{2,0},{3,67},{4,6},{5,69},{6,4},{7,71},{8,10},{9,73},... | collective-permute-start | bytes 614408 | tf_op jit(solution)/shard_map/ppermute | solution.py:344
  82.8 5.3 %collective-permute-start.13 = (bf16[800,128]{1,0:T(8,128)(2,1)S(1)}, bf16[800,128]{1,0:T(8,128)(2,1)S(1)}, u32[]{:S(2)}, u32[]{:S(2)}) collective-permute-start(bf16[800,128]{1,0:T(8,128)(2,1)S(1)} %reduce-precision_convert_fusion.own), channel_id=1, source_target_pairs={{0,18},{1,97},{2,16},{3,99},{4,22},{5,101},{6,20},{7,103},{8,26},{... | collective-permute-start | bytes 614408 | tf_op jit(solution)/shard_map/ppermute | solution.py:346
  88.2 8.5 %collective-permute-start.16 = (bf16[4,800,128]{2,1,0:T(8,128)(2,1)S(1)}, bf16[4,800,128]{2,1,0:T(8,128)(2,1)S(1)}, u32[]{:S(2)}, u32[]{:S(2)}) collective-permute-start(bf16[4,800,128]{2,1,0:T(8,128)(2,1)S(1)} %pad_maximum_fusion), channel_id=1, source_target_pairs={{0,1},{1,0},{2,3},{3,2},{4,5},{5,4},{6,7},{7,6},{8,9},{9,8},{10,11... | collective-permute-start | bytes 2457608 | tf_op jit(solution)/shard_map/ppermute | solution.py:340
where the time goes:
time: 99 us; the launch traced here: 98.9 us
  Pallas kernels  35.1 us (35%)
  starting transfers between devices  31.5 us (32%)
  waiting for transfers between devices  29.7 us (30%)
  other arithmetic  1.63 us (2%)
    pallas_call x2, Pallas kernels, half(): pl.pallas_call(functools.partial(half_kernel, frame), in_specs=specs, out...  27.1 us
    ppermute x4, waiting for transfers between devices, trade(): before = lax.ppermute(near, BOTH, along(axes, step_by(1)))  13.4 us
    ppermute x4, starting transfers between devices, trade(): across = lax.ppermute(far, BOTH, along(axes, step_by(2)))  8.77 us
    ppermute x2, starting transfers between devices, swap(): return lax.ppermute(value, BOTH, [(i, i ^ 1) for i in range(128)])  6.65 us
    pallas_call x1, Pallas kernels, forward(): pl.pallas_call(forward_kernel, in_specs=[pl.BlockSpec(memory_space=pl.ANY...  6 us
    ppermute x4, starting transfers between devices, trade(): after = lax.ppermute(last, BOTH, along(axes, step_by(3)))  5.58 us
    ppermute x4, waiting for transfers between devices, trade(): across = lax.ppermute(far, BOTH, along(axes, step_by(2)))  5.25 us
    ppermute x1, starting transfers between devices, shards(): inner = lax.ppermute(jnp.where(odd == 1, top, bottom), 'ha', meet[0])  4.63 us
  transfers between devices with their start and end apart: 17, of which 12 were waited for; matrix products, arithmetic and copies ran while one was open for 0% of the time, Pallas kernels for 20%

commit v1 on v0

--- a/solution.py
+++ b/solution.py
@@ -23,7 +23,7 @@
     return jnp.dot(a, b, preferred_element_type=F32)
 
 
-CHUNK = 512
+CHUNK = 1024
 
 
 def forward_kernel(lat_h, w1_h, w2_h, k_h, cot_h, *refs):
@@ -136,133 +136,192 @@
     )(*in_vmem(first, second, cot_a, cot_b))
 
 
-STEP = 4
-
-
-def half_kernel(frame, *refs):
-    refs = list(refs)
-    take = lambda n: [refs.pop(0) for _ in range(n)]
-    lat, act, slope, ft, taps, w1t, w2t = take(7)
-    if frame == 0:
-        cot_a, cot_b = take(2)
-        gl_h, planes_b, gk, gw = take(4)
-        planes_a, spread, gm, gp, gl, sem = take(6)
-    else:
-        planes_a, cot_b, sumk, sumw, _ = take(5)
-        gl_h, keep, send = take(3)
-        planes_b, spread, gm, gp, gl, sem, gk, gw = take(8)
-    n_px = gm.shape[0]
-    base = frame * n_px
+STEP = 8
+
+
+def split(cells, planes, spread, row, s):
+    spread[s, 8:264, :] = cells[row].astype(F32)
+    for c in range(4):
+        planes[row, :, 128 * c : 128 * (c + 1)] = spread[s, pl.ds(7 + c, 128, stride=2), :].astype(BF)
+
+
+def split_all(cells, planes, spread):
     zero = jnp.zeros((8, 128), F32)
-    for s in range(spread.shape[0]):
+    for s in range(2):
         spread[s, 0:8, :] = zero
         spread[s, 264:272, :] = zero
 
-    def split(cells, planes, row, s):
-        spread[s, 8:264, :] = cells.astype(F32)
-        for c in range(4):
-            planes[row, :, 128 * c : 128 * (c + 1)] = spread[s, pl.ds(7 + c, 128, stride=2), :].astype(BF)
-
-    def split_all(cot, planes):
-        def body(r, carry):
-            for s in range(2):
-                split(cot[2 * r + s], planes, 2 * r + s, s)
-            return carry
-
-        lax.fori_loop(0, ROWS // 2 + 1, body, 0)
-
-    if frame == 0:
-        split_all(cot_a, planes_a)
-    split_all(cot_b, planes_b)
+    def body(r, carry):
+        for s in range(2):
+            split(cells, planes, spread, 2 * r + s, s)
+        return carry
+
+    lax.fori_loop(0, ROWS // 2 + 1, body, 0)
+
+
+def conv(taps, dt, planes, y):
+    total = 0.0
+    for dy in range(3):
+        window = planes[pl.ds(y + 2 - dy, STEP)].reshape(STEP * 128, 512)
+        total = total + dot(window, taps[3 * dt + dy])
+    return total
+
+
+def own_cells(planes, y):
+    return planes[pl.ds(y + 1, STEP), :, 128:384].reshape(STEP * 128, 256).astype(F32)
+
+
+def analyze(total):
+    total = (0.5 * total).reshape(STEP // 2, 2, 128, 256)
+    upper = total[:, 0].reshape(STEP * 64, 256)
+    lower = total[:, 1].reshape(STEP * 64, 256)
+    a, b, c, d = upper[:, :128], upper[:, 128:], lower[:, :128], lower[:, 128:]
+    ab, am, cd, cm = a + b, a - b, c + d, c - d
+    return jnp.concatenate([ab + cd, ab - cd, am + cm, am - cm], axis=1).astype(BF)
+
+
+def rows_of(k, count):
+    return pl.ds(pl.multiple_of(k * count, count), count)
+
+
+def add_taps(gk, ft, dt, planes, before):
+    cols = planes.reshape((ROWS + 2) * 128, 512)
+    for dy in range(3):
+        got = dot(ft, cols[128 * (2 - dy) : 128 * (ROWS + 2 - dy)])
+        for dx in range(3):
+            col = 2 - dx
+            both = got[0:128, 128 * col : 128 * (col + 1)] + got[128:256, 128 * (col + 1) : 128 * (col + 2)]
+            where = slice(128 * (9 * dt + 3 * dy + dx), 128 * (9 * dt + 3 * dy + dx + 1))
+            gk[where] = both if before is None else before[where] + both
+
+
+def add_weights(gw, pairs, before):
+    for n, (left, right) in enumerate(pairs):
+        for m in range(2):
+            part = lax.dot_general(
+                left[:, 256 * m : 256 * (m + 1)], right[...], (((0,), (0,)), ((), ())), preferred_element_type=F32
+            )
+            where = slice(512 * n + 256 * m, 512 * n + 256 * (m + 1))
+            gw[where] = part if before is None else before[where] + part
+
+
+def early_kernel(lat, act, slope, ft, taps, w1t, w2t, cot_a, cot_b, gl_h, part, gk, gw, *scratch):
+    planes_a, planes_b, spread, gm, gp, gl, sem = scratch
+    n_px = gm.shape[0]
+    mine = pl.ds(0, n_px)
+    split_all(cot_a, planes_a, spread)
+    split_all(cot_b, planes_b, spread)
 
     def back(k, carry):
         y = k * STEP
-        total = planes_a[pl.ds(y + 1, STEP), :, 128:384].reshape(STEP * 128, 256).astype(F32)
-        for dt, planes in ((1, planes_a), (0, planes_b)):
-            for dy in range(3):
-                window = planes[pl.ds(y + 2 - dy, STEP)].reshape(STEP * 128, 512)
-                total = total + dot(window, taps[3 * dt + dy])
-        total = (0.5 * total).reshape(STEP // 2, 2, 128, 256)
-        upper = total[:, 0].reshape(STEP * 64, 256)
-        lower = total[:, 1].reshape(STEP * 64, 256)
-        a, b, c, d = upper[:, :128], upper[:, 128:], lower[:, :128], lower[:, 128:]
-        ab, am, cd, cm = a + b, a - b, c + d, c - d
-        grad = jnp.concatenate([ab + cd, ab - cd, am + cm, am - cm], axis=1).astype(BF)
-        start = pl.multiple_of(k * STEP * 64, STEP * 64)
-        here = pl.ds(start, STEP * 64)
-        gm[here] = grad
-        hidden = (dot(grad, w2t[...]) * slope[pl.ds(base + start, STEP * 64)].astype(F32)).astype(BF)
-        gp[here] = hidden
-        gl[here] = (grad.astype(F32) + dot(hidden, w1t[...])).astype(BF)
+        total = own_cells(planes_a, y) + conv(taps, 1, planes_a, y) + conv(taps, 0, planes_b, y)
+        gm[rows_of(k, STEP * 64)] = analyze(total)
         return carry
 
+    def ahead(k, carry):
+        y = k * STEP
+        part[rows_of(k, STEP * 128)] = own_cells(planes_b, y) + conv(taps, 1, planes_b, y)
+        return carry
+
     lax.fori_loop(0, ROWS // STEP, back, 0)
-    out = pltpu.make_async_copy(gl, gl_h.at[pl.ds(base, n_px)], sem)
+    lax.fori_loop(0, ROWS // STEP, ahead, 0)
+    gp[...] = (dot(gm[...], w2t[...]) * slope[mine].astype(F32)).astype(BF)
+    gl[...] = (gm[...].astype(F32) + dot(gp[...], w1t[...])).astype(BF)
+    out = pltpu.make_async_copy(gl, gl_h.at[mine], sem)
     out.start()
-    for dt, planes in ((1, planes_a), (0, planes_b)):
-        cols = planes.reshape((ROWS + 2) * 128, 512)
-        for dy in range(3):
-            got = dot(ft[frame], cols[128 * (2 - dy) : 128 * (ROWS + 2 - dy)])
-            for dx in range(3):
-                col = 2 - dx
-                both = got[0:128, 128 * col : 128 * (col + 1)] + got[128:256, 128 * (col + 1) : 128 * (col + 2)]
-                where = slice(128 * (9 * dt + 3 * dy + dx), 128 * (9 * dt + 3 * dy + dx + 1))
-                gk[where] = both if frame == 0 else sumk[where] + both
-    for n, (left, right) in enumerate(((lat, gp), (act, gm))):
-        for m in range(2):
-            part = lax.dot_general(
-                left[pl.ds(base, n_px), 256 * m : 256 * (m + 1)],
-                right[...],
-                (((0,), (0,)), ((), ())),
-                preferred_element_type=F32,
-            )
-            where = slice(512 * n + 256 * m, 512 * n + 256 * (m + 1))
-            gw[where] = part if frame == 0 else sumw[where] + part
-    if frame == 1:
-        ids = block_ids()
-        for r in range(8):
-            packed = (keep, send)[r // 4].at[r % 4]
-            b = ids[r]
-            for lane in range(4):
-                packed[128 * lane : 128 * (lane + 1), :] = gw[
-                    pl.ds(pl.multiple_of(b * 128, 128), 128), 128 * lane : 128 * (lane + 1)
-                ].astype(BF)
-            packed[512:800, :] = gk[pl.ds(pl.multiple_of(b * 288, 32), 288), :].astype(BF)
+    add_taps(gk, ft[0], 1, planes_a, None)
+    add_taps(gk, ft[0], 0, planes_b, None)
+    add_taps(gk, ft[1], 1, planes_b, gk)
+    add_weights(gw, ((lat.at[mine], gp), (act.at[mine], gm)), None)
     out.wait()
 
 
-def half(frame, rest, cells, sums=()):
-    n = rest[0].shape[0]
-    n_px = n // 2
-    vmem = pl.BlockSpec(memory_space=pltpu.VMEM)
-    any_ = pl.BlockSpec(memory_space=pl.ANY)
-    ops = in_vmem(*rest, *cells)
-    specs = [vmem] * len(ops)
-    planes = (ROWS + 2, 128, 512)
-    sum_shapes = [(2304, 128), (1024, 512)]
-    scratch = [pltpu.VMEM(planes, BF), pltpu.VMEM((2, 272, 128), F32)]
-    scratch += [pltpu.VMEM((n_px, 512), BF)] * 3 + [pltpu.SemaphoreType.DMA]
-    shapes = [pltpu.HBM((n, 512), BF)]
-    alias = {}
-    if frame == 0:
-        shapes += [pltpu.VMEM(planes, BF)] + [pltpu.VMEM(shape, F32) for shape in sum_shapes]
-    else:
-        grad, gk, gw = sums
-        alias = {len(ops) + 2: 0}
-        ops += in_vmem(gk, gw) + in_hbm(grad)
-        specs += [vmem, vmem, any_]
-        shapes += [pltpu.VMEM((4, 800, 128), BF)] * 2
-        scratch += [pltpu.VMEM(shape, F32) for shape in sum_shapes]
-    return pl.pallas_call(
-        functools.partial(half_kernel, frame),
-        in_specs=specs,
-        out_specs=[any_] + [vmem] * (len(shapes) - 1),
-        out_shape=shapes,
-        input_output_aliases=alias,
-        scratch_shapes=scratch,
+def late_kernel(lat, act, slope, ft, taps, w2t, cells, part, sumk, sumw, gm, gp, keep, send, *scratch):
+    planes, spread, gk, gw = scratch
+    n_px = gm.shape[0]
+    mine = pl.ds(n_px, n_px)
+    split_all(cells, planes, spread)
+
+    def back(k, carry):
+        total = part[rows_of(k, STEP * 128)] + conv(taps, 0, planes, k * STEP)
+        gm[rows_of(k, STEP * 64)] = analyze(total)
+        return carry
+
+    lax.fori_loop(0, ROWS // STEP, back, 0)
+    gp[...] = (dot(gm[...], w2t[...]) * slope[mine].astype(F32)).astype(BF)
+    gk[128 * 9 :] = sumk[128 * 9 :]
+    add_taps(gk, ft[1], 0, planes, sumk)
+    add_weights(gw, ((lat.at[mine], gp), (act.at[mine], gm)), sumw)
+    ids = block_ids()
+    for r in range(8):
+        packed = (keep, send)[r // 4].at[r % 4]
+        b = ids[r]
+        for lane in range(4):
+            packed[128 * lane : 128 * (lane + 1), :] = gw[
+                pl.ds(pl.multiple_of(b * 128, 128), 128), 128 * lane : 128 * (lane + 1)
+            ].astype(BF)
+        packed[512:800, :] = gk[pl.ds(pl.multiple_of(b * 288, 32), 288), :].astype(BF)
+
+
+def last_kernel(gm, gp, w1t, _, gl_h, gl, sem):
+    n_px = gm.shape[0]
+    gl[...] = (gm[...].astype(F32) + dot(gp[...], w1t[...])).astype(BF)
+    out = pltpu.make_async_copy(gl, gl_h.at[pl.ds(n_px, n_px)], sem)
+    out.start()
+    out.wait()
+
+
+VMEM_SPEC = pl.BlockSpec(memory_space=pltpu.VMEM)
+ANY_SPEC = pl.BlockSpec(memory_space=pl.ANY)
+PLANES = (ROWS + 2, 128, 512)
+SUMS = [(2304, 128), (1024, 512)]
+SPREAD = (2, 272, 128)
+
+
+def early(lat, act, slope, ft, taps, w1t, w2t, cot_a, cot_b):
+    n_px = lat.shape[0] // 2
+    sums = [pltpu.VMEM(shape, F32) for shape in SUMS]
+    ops = in_vmem(lat, act, slope, ft, taps, w1t, w2t, cot_a, cot_b)
+    return pl.pallas_call(
+        early_kernel,
+        in_specs=[VMEM_SPEC] * len(ops),
+        out_specs=[ANY_SPEC] + [VMEM_SPEC] * 3,
+        out_shape=[pltpu.HBM(lat.shape, BF), pltpu.VMEM((ROWS * 128, 256), F32)] + sums,
+        scratch_shapes=[pltpu.VMEM(PLANES, BF)] * 2
+        + [pltpu.VMEM(SPREAD, F32)]
+        + [pltpu.VMEM((n_px, 512), BF)] * 3
+        + [pltpu.SemaphoreType.DMA],
         cost_estimate=pl.CostEstimate(flops=10 << 30, bytes_accessed=16 * MIB, transcendentals=0),
         compiler_params=pltpu.CompilerParams(vmem_limit_bytes=24 * MIB),
     )(*ops)
+
+
+def late(lat, act, slope, ft, taps, w2t, cells, part, gk, gw):
+    half = (lat.shape[0] // 2, 512)
+    ops = in_vmem(lat, act, slope, ft, taps, w2t, cells, part, gk, gw)
+    return pl.pallas_call(
+        late_kernel,
+        in_specs=[VMEM_SPEC] * len(ops),
+        out_specs=[VMEM_SPEC] * 4,
+        out_shape=[pltpu.VMEM(half, BF)] * 2 + [pltpu.VMEM((4, 800, 128), BF)] * 2,
+        scratch_shapes=[pltpu.VMEM(PLANES, BF), pltpu.VMEM(SPREAD, F32)]
+        + [pltpu.VMEM(shape, F32) for shape in SUMS],
+        cost_estimate=pl.CostEstimate(flops=6 << 30, bytes_accessed=16 * MIB, transcendentals=0),
+        compiler_params=pltpu.CompilerParams(vmem_limit_bytes=24 * MIB),
+    )(*ops)
+
+
+def last(gm, gp, w1t, grad):
+    return pl.pallas_call(
+        last_kernel,
+        in_specs=[VMEM_SPEC] * 3 + [ANY_SPEC],
+        out_specs=ANY_SPEC,
+        out_shape=pltpu.HBM(grad.shape, BF),
+        input_output_aliases={3: 0},
+        scratch_shapes=[pltpu.VMEM(gm.shape, BF), pltpu.SemaphoreType.DMA],
+        cost_estimate=pl.CostEstimate(flops=1 << 29, bytes_accessed=4 * MIB, transcendentals=0),
+        compiler_params=pltpu.CompilerParams(vmem_limit_bytes=8 * MIB),
+    )(*in_vmem(gm, gp, w1t), *in_hbm(grad))
 
 
 def unpack_kernel(own, near, far, last, other, first_h, second_h, gk_h, gw, gk, sems):
@@ -370,8 +429,7 @@
     return rounded(a.astype(F32) + b.astype(F32))
 
 
-def sum_all(keep, send):
-    got = swap(send)
+def sum_all(keep, got):
     parts = [add2(keep[k], got[k]) for k in range(4)]
     own = add4(parts[0], *trade(*parts[1:], (0, 1)))
     own = add4(own, *trade(own, own, own, (1, 2)))
@@ -403,9 +461,13 @@
     *rest, cot_a, cot_b = forward(flat, w_first, w_second, kernel, cotangent)
     cot_a, cot_b = border(inner, outer, cot_a, cot_b)
     later = neighbour(cot_a, "ta", -1)
-    grad, planes, gk, gw = half(0, rest, (cot_a, cot_b))
-    grad, keep, send = half(1, rest, (planes, later), (grad, gk, gw))
-    first, second, gk = unpack(*sum_all(keep, send))
+    lat, act, slope, ft, taps, w1t, w2t = rest
+    grad, part, gk, gw = early(*rest, cot_a, cot_b)
+    gm, gp, keep, send = late(lat, act, slope, ft, taps, w2t, later, part, gk, gw)
+    got = swap(send)
+    grad = last(gm, gp, w1t, grad)
+    got, grad = lax.optimization_barrier((got, grad))
+    first, second, gk = unpack(*sum_all(keep, got))
     return grad.reshape(latent.shape), first, second, gk.reshape(kernel.shape)
 
 

time: 99 us -> 91.5 us (0.924)
  Pallas kernels: 35.1 us -> 29.8 us
  waiting for transfers between devices: 29.7 us -> 27 us
    pallas_call x2 -> x3, Pallas kernels: 27.1 us -> 22.3 us  [the longest x1 14.6 us: early(): pl.pallas_call(early_kernel, in_specs=[VMEM_SPEC] * len(ops), out_specs=[...]
    ppermute x2, waiting for transfers between devices: 4.28 us -> 2.58 us  [swap(): return lax.ppermute(value, BOTH, [(i, i ^ 1) for i in range(128)])]
  transfers between devices with their start and end apart: 17 -> 17, of which waited for: 12 -> 13; matrix products, arithmetic and copies ran while one was open for 0% -> 0% of each run, Pallas kernels for 20% -> 24%
where the time goes in v1:
time: 91.5 us; the launch traced here: 91.3 us
  starting transfers between devices  32 us (35%)
  Pallas kernels  29.8 us (33%)
  waiting for transfers between devices  27 us (30%)
  other arithmetic  1.63 us (2%)
  between operations  0.93 us (1%)
    pallas_call x1, Pallas kernels, early(): pl.pallas_call(early_kernel, in_specs=[VMEM_SPEC] * len(ops), out_specs=[...  14.6 us
    ppermute x4, waiting for transfers between devices, trade(): before = lax.ppermute(near, BOTH, along(axes, step_by(1)))  13 us
    ppermute x4, starting transfers between devices, trade(): across = lax.ppermute(far, BOTH, along(axes, step_by(2)))  8.66 us
    ppermute x2, starting transfers between devices, swap(): return lax.ppermute(value, BOTH, [(i, i ^ 1) for i in range(128)])  6.68 us
    pallas_call x1, Pallas kernels, late(): pl.pallas_call(late_kernel, in_specs=[VMEM_SPEC] * len(ops), out_specs=[V...  6.07 us
    ppermute x4, starting transfers between devices, trade(): after = lax.ppermute(last, BOTH, along(axes, step_by(3)))  5.78 us
    pallas_call x1, Pallas kernels, forward(): pl.pallas_call(forward_kernel, in_specs=[pl.BlockSpec(memory_space=pl.ANY...  5.5 us
    ppermute x4, waiting for transfers between devices, trade(): across = lax.ppermute(far, BOTH, along(axes, step_by(2)))  5.26 us
  transfers between devices with their start and end apart: 17, of which 13 were waited for; matrix products, arithmetic and copies ran while one was open for 0% of the time, Pallas kernels for 24%

profile of v1, /device:TPU:1, one launch (start us, length us, event | category | flops | bytes accessed | tf_op | source)
XLA Modules:
  0.0 91.3 jit_solution(7773811426202585135)
XLA Ops:
  0.6 1.0 %fusion.8 = (bf16[2,256,128]{2,1,0:T(8,128)(2,1)S(1)}, bf16[2,256,128]{2,1,0:T(8,128)(2,1)S(1)}) fusion(pred[]{:T(512)S(6)} %eq.6, bf16[2,16,256,128]{3,2,1,0:T(8,128)(2,1)} %cot_h.1), kind=kLoop, calls=%fused_computation.18 | loop fusion | flops 131072 | bytes 524289 | tf_op jit(solution)/shard_map/jit(_where)/select_n | solution.py:460
  1.6 0.7 collective-permute-start.1
  2.3 4.6 %collective-permute-start = (bf16[2,256,128]{2,1,0:T(8,128)(2,1)S(1)}, bf16[2,256,128]{2,1,0:T(8,128)(2,1)S(1)}, u32[]{:S(2)}, u32[]{:S(2)}) collective-permute-start(bf16[2,256,128]{2,1,0:T(8,128)(2,1)S(1)} %get-tuple-element.53), channel_id=1, source_target_pairs={{0,16},{16,0},{32,48},{48,32},{64,80},{80,64},{96,112},{112,96},{1... | collective-permute-start | bytes 393224 | tf_op jit(solution)/shard_map/ppermute | solution.py:459
  6.9 5.5 %shard_map.84 = (bf16[2048,512]{1,0:T(8,128)(2,1)S(1)}, bf16[2048,512]{1,0:T(8,128)(2,1)S(1)}, bf16[2048,512]{1,0:T(8,128)(2,1)S(1)}, bf16[2,256,2048]{2,1,0:T(8...) custom-call(bf16[2048,512]{1,0:T(8,128)(2,1)} %bitcast.38, ...), custom_call_target="tpu_custom_call" | custom-call | flops 4294967296 | bytes 12582912 | tf_op jit(solution)/shard_map/pallas_call | solution.py:100
  12.6 3.6 %collective-permute-start.2 = (bf16[18,256,128]{2,1,0:T(8,128)(2,1)S(1)}, bf16[18,256,128]{2,1,0:T(8,128)(2,1)S(1)}, u32[]{:S(2)}, u32[]{:S(2)}) collective-permute-start(bf16[18,256,128]{2,1,0:T(8,128)(2,1)S(1)} %get-tuple-element.36.cot_a), channel_id=1, source_target_pairs={{1,0},{2,1},{3,2},{4,3},{5,4},{6,5},{7,6},{8,7},{9,8},{10,9},{11,1... | collective-permute-start | bytes 3538952 | tf_op jit(solution)/shard_map/ppermute | solution.py:444
  16.2 14.6 %shard_map.86 = (bf16[2048,512]{1,0:T(8,128)(2,1)}, f32[2048,256]{1,0:T(8,128)S(1)}, f32[2304,128]{1,0:T(8,128)S(1)}, f32[1024,512]{1,0:T(8,128)S(1)}) custom-call(bf16[2048,512]{1,0:T(8,128)(2,1)S(1)} %get-tuple-element.28.lat, bf16[2048,512]{1,0:T(8,128)(2,1)S(1)} %get-tuple-element.29.act, bf16[2048,512]{1,0:T(8,128)(2,1)S(1)} %get-tuple-element.30.slope, ...), custom_call_target="tpu_custom_call" | custom-call | flops 10737418240 | bytes 16777216 | tf_op jit(solution)/shard_map/pallas_call | solution.py:285
  30.8 1.7 %collective-permute-done.2.cells = bf16[18,256,128]{2,1,0:T(8,128)(2,1)S(1)} collective-permute-done((bf16[18,256,128]{2,1,0:T(8,128)(2,1)S(1)}, bf16[18,256,128]{2,1,0:T(8,128)(2,1)S(1)}, u32[]{:S(2)}, u32[]{:S(2)}) %collective-permute-start.2) | collective-permute-done | bytes 1179680 | tf_op jit(solution)/shard_map/ppermute | solution.py:444
  32.5 6.1 %shard_map.87 = (bf16[1024,512]{1,0:T(8,128)(2,1)S(1)}, bf16[1024,512]{1,0:T(8,128)(2,1)S(1)}, bf16[4,800,128]{2,1,0:T(8,128)(2,1)S(1)}, bf16[4,800,128]{2,1,0:T(8,128)(2,1)S(1)}) custom-call(bf16[2048,512]{1,0:T(8,128)(2,1)S(1)} %get-tuple-element.28.lat, bf16[2048,512]{1,0:T(8,128)(2,1)S(1)} %get-tuple-element.29.act, ...), custom_call_target="tpu_custom_call" | custom-call | flops 6442450944 | bytes 16777216 | tf_op jit(solution)/shard_map/pallas_call | solution.py:302
  38.7 1.7 %shard_map.88 = bf16[2048,512]{1,0:T(8,128)(2,1)} custom-call(bf16[1024,512]{1,0:T(8,128)(2,1)S(1)} %get-tuple-element.43.gm, bf16[1024,512]{1,0:T(8,128)(2,1)S(1)} %get-tuple-element.44.gp, bf16[512,512]{1,0:T(8,128)(2,1)S(1)} %get-tuple-element.37.w1t, bf16[2048,512]{1,0:T(8,128)(2,1)} %get-tuple-element.45._), custom_call_target="tpu_custom_call", output_to_operand_aliasing={{}: (3, {})} | custom-call | flops 536870912 | bytes 4194304 | tf_op jit(solution)/shard_map/pallas_call | solution.py:315
  40.4 0.6 collective-permute-done.3
  41.2 2.7 %collective-permute-start.4 = (bf16[800,128]{1,0:T(8,128)(2,1)S(1)}, bf16[800,128]{1,0:T(8,128)(2,1)S(1)}, u32[]{:S(2)}, u32[]{:S(2)}) collective-permute-start(bf16[800,128]{1,0:T(8,128)(2,1)S(1)} %get-tuple-element.54), channel_id=1, source_target_pairs={{0,2},{1,65},{2,0},{3,67},{4,6},{5,69},{6,4},{7,71},{8,10},{9,73},... | collective-permute-start | bytes 614408 | tf_op jit(solution)/shard_map/ppermute | solution.py:403
  43.9 1.1 %collective-permute-start.6 = (bf16[800,128]{1,0:T(8,128)(2,1)S(1)}, bf16[800,128]{1,0:T(8,128)(2,1)S(1)}, u32[]{:S(2)}, u32[]{:S(2)}) collective-permute-start(bf16[800,128]{1,0:T(8,128)(2,1)S(1)} %get-tuple-element.55), channel_id=1, source_target_pairs={{0,18},{1,97},{2,16},{3,99},{4,22},{5,101},{6,20},{7,103},{8,26},{... | collective-permute-start | bytes 614408 | tf_op jit(solution)/shard_map/ppermute | solution.py:405
  45.4 2.3 %collective-permute-done.4 = bf16[800,128]{1,0:T(8,128)(2,1)S(1)} collective-permute-done((bf16[800,128]{1,0:T(8,128)(2,1)S(1)}, bf16[800,128]{1,0:T(8,128)(2,1)S(1)}, u32[]{:S(2)}, u32[]{:S(2)}) %collective-permute-start.4) | collective-permute-done | bytes 204832 | tf_op jit(solution)/shard_map/ppermute | solution.py:403
  47.7 1.1 %collective-permute-done.6 = bf16[800,128]{1,0:T(8,128)(2,1)S(1)} collective-permute-done((bf16[800,128]{1,0:T(8,128)(2,1)S(1)}, bf16[800,128]{1,0:T(8,128)(2,1)S(1)}, u32[]{:S(2)}, u32[]{:S(2)}) %collective-permute-start.6) | collective-permute-done | bytes 204832 | tf_op jit(solution)/shard_map/ppermute | solution.py:405
  48.8 2.2 %collective-permute-done.5 = bf16[800,128]{1,0:T(8,128)(2,1)S(1)} collective-permute-done((bf16[800,128]{1,0:T(8,128)(2,1)S(1)}, bf16[800,128]{1,0:T(8,128)(2,1)S(1)}, u32[]{:S(2)}, u32[]{:S(2)}) %collective-permute-start.5) | collective-permute-done | bytes 204832 | tf_op jit(solution)/shard_map/ppermute | solution.py:404
  51.1 3.9 %collective-permute-start.9 = (bf16[800,128]{1,0:T(8,128)(2,1)S(1)}, bf16[800,128]{1,0:T(8,128)(2,1)S(1)}, u32[]{:S(2)}, u32[]{:S(2)}) collective-permute-start(bf16[800,128]{1,0:T(8,128)(2,1)S(1)} %fusion.2), channel_id=1, source_target_pairs={{0,96},{1,13},{2,98},{3,15},{4,100},{5,1},{6,102},{7,3},{8,104},{9... | collective-permute-start | bytes 614408 | tf_op jit(solution)/shard_map/ppermute | solution.py:405
  55.0 1.5 %collective-permute-start.7 = (bf16[800,128]{1,0:T(8,128)(2,1)S(1)}, bf16[800,128]{1,0:T(8,128)(2,1)S(1)}, u32[]{:S(2)}, u32[]{:S(2)}) collective-permute-start(bf16[800,128]{1,0:T(8,128)(2,1)S(1)} %fusion.2), channel_id=1, source_target_pairs={{0,64},{1,9},{2,66},{3,11},{4,68},{5,13},{6,70},{7,15},{8,72},{9,1... | collective-permute-start | bytes 614408 | tf_op jit(solution)/shard_map/ppermute | solution.py:403
  56.5 1.2 %collective-permute-done.9 = bf16[800,128]{1,0:T(8,128)(2,1)S(1)} collective-permute-done((bf16[800,128]{1,0:T(8,128)(2,1)S(1)}, bf16[800,128]{1,0:T(8,128)(2,1)S(1)}, u32[]{:S(2)}, u32[]{:S(2)}) %collective-permute-start.9) | collective-permute-done | bytes 204832 | tf_op jit(solution)/shard_map/ppermute | solution.py:405
  57.7 5.3 %collective-permute-done.8 = bf16[800,128]{1,0:T(8,128)(2,1)S(1)} collective-permute-done((bf16[800,128]{1,0:T(8,128)(2,1)S(1)}, bf16[800,128]{1,0:T(8,128)(2,1)S(1)}, u32[]{:S(2)}, u32[]{:S(2)}) %collective-permute-start.8) | collective-permute-done | bytes 204832 | tf_op jit(solution)/shard_map/ppermute | solution.py:404
  63.2 0.4 collective-permute-start.12
  63.6 1.1 %collective-permute-start.11 = (bf16[800,128]{1,0:T(8,128)(2,1)S(1)}, bf16[800,128]{1,0:T(8,128)(2,1)S(1)}, u32[]{:S(2)}, u32[]{:S(2)}) collective-permute-start(bf16[800,128]{1,0:T(8,128)(2,1)S(1)} %reduce-precision_convert_fusion.1), channel_id=1, source_target_pairs={{0,4},{1,17},{2,6},{3,19},{4,8},{5,21},{6,10},{7,23},{8,12},{9,25}... | collective-permute-start | bytes 614408 | tf_op jit(solution)/shard_map/ppermute | solution.py:404
  64.7 1.4 %collective-permute-start.10 = (bf16[800,128]{1,0:T(8,128)(2,1)S(1)}, bf16[800,128]{1,0:T(8,128)(2,1)S(1)}, u32[]{:S(2)}, u32[]{:S(2)}) collective-permute-start(bf16[800,128]{1,0:T(8,128)(2,1)S(1)} %reduce-precision_convert_fusion.1), channel_id=1, source_target_pairs={{0,8},{1,3},{2,10},{3,1},{4,12},{5,7},{6,14},{7,5},{8,0},{9,11},{1... | collective-permute-start | bytes 614408 | tf_op jit(solution)/shard_map/ppermute | solution.py:403
  66.1 2.0 %collective-permute-done.12 = bf16[800,128]{1,0:T(8,128)(2,1)S(1)} collective-permute-done((bf16[800,128]{1,0:T(8,128)(2,1)S(1)}, bf16[800,128]{1,0:T(8,128)(2,1)S(1)}, u32[]{:S(2)}, u32[]{:S(2)}) %collective-permute-start.12) | collective-permute-done | bytes 204832 | tf_op jit(solution)/shard_map/ppermute | solution.py:405
  68.1 3.5 %collective-permute-done.11 = bf16[800,128]{1,0:T(8,128)(2,1)S(1)} collective-permute-done((bf16[800,128]{1,0:T(8,128)(2,1)S(1)}, bf16[800,128]{1,0:T(8,128)(2,1)S(1)}, u32[]{:S(2)}, u32[]{:S(2)}) %collective-permute-start.11) | collective-permute-done | bytes 204832 | tf_op jit(solution)/shard_map/ppermute | solution.py:404
  71.7 0.5 collective-permute-start.15
  72.2 3.0 %collective-permute-start.14 = (bf16[800,128]{1,0:T(8,128)(2,1)S(1)}, bf16[800,128]{1,0:T(8,128)(2,1)S(1)}, u32[]{:S(2)}, u32[]{:S(2)}) collective-permute-start(bf16[800,128]{1,0:T(8,128)(2,1)S(1)} %reduce-precision_convert_fusion.own), channel_id=1, source_target_pairs={{0,2},{1,65},{2,0},{3,67},{4,6},{5,69},{6,4},{7,71},{8,10},{9,73},... | collective-permute-start | bytes 614408 | tf_op jit(solution)/shard_map/ppermute | solution.py:403
  75.2 0.4 collective-permute-start.13
  75.6 2.0 %collective-permute-done.15.last = bf16[800,128]{1,0:T(8,128)(2,1)S(1)} collective-permute-done((bf16[800,128]{1,0:T(8,128)(2,1)S(1)}, bf16[800,128]{1,0:T(8,128)(2,1)S(1)}, u32[]{:S(2)}, u32[]{:S(2)}) %collective-permute-start.15) | collective-permute-done | bytes 204832 | tf_op jit(solution)/shard_map/ppermute | solution.py:404
  77.6 2.9 %collective-permute-done.14.far = bf16[800,128]{1,0:T(8,128)(2,1)S(1)} collective-permute-done((bf16[800,128]{1,0:T(8,128)(2,1)S(1)}, bf16[800,128]{1,0:T(8,128)(2,1)S(1)}, u32[]{:S(2)}, u32[]{:S(2)}) %collective-permute-start.14) | collective-permute-done | bytes 204832 | tf_op jit(solution)/shard_map/ppermute | solution.py:403
  80.7 6.6 %collective-permute-start.16 = (bf16[4,800,128]{2,1,0:T(8,128)(2,1)S(1)}, bf16[4,800,128]{2,1,0:T(8,128)(2,1)S(1)}, u32[]{:S(2)}, u32[]{:S(2)}) collective-permute-start(bf16[4,800,128]{2,1,0:T(8,128)(2,1)S(1)} %pad_maximum_fusion), channel_id=1, source_target_pairs={{0,1},{1,0},{2,3},{3,2},{4,5},{5,4},{6,7},{7,6},{8,9},{9,8},{10,11... | collective-permute-start | bytes 2457608 | tf_op jit(solution)/shard_map/ppermute | solution.py:399
  87.3 2.0 %collective-permute-done.16.other = bf16[4,800,128]{2,1,0:T(8,128)(2,1)S(1)} collective-permute-done((bf16[4,800,128]{2,1,0:T(8,128)(2,1)S(1)}, bf16[4,800,128]{2,1,0:T(8,128)(2,1)S(1)}, u32[]{:S(2)}, u32[]{:S(2)}) %collective-permute-start.16) | collective-permute-done | bytes 819232 | tf_op jit(solution)/shard_map/ppermute | solution.py:399
  89.2 1.9 %shard_map.89 = (f32[512,512]{1,0:T(8,128)}, f32[512,512]{1,0:T(8,128)}, f32[2304,128]{1,0:T(8,128)}) custom-call(bf16[800,128]{1,0:T(8,128)(2,1)S(1)} %reduce-precision_convert_fusion.own, bf16[800,128]{1,0:T(8,128)(2,1)S(1)} %collective-permute-done.13.near, bf16[800,128]{1,0:T(8,128)(2,1)S(1)} %collective-permute-done.14.far, ...), custom_call_target="tpu_custom_call" | custom-call | tf_op jit(solution)/shard_map/pallas_call | solution.py:354
  (14 shorter events, 1.2 us)
Async XLA Ops:
  1.6 10.8 %collective-permute-start.1 = (bf16[2,256,128]{2,1,0:T(8,128)(2,1)S(1)}, bf16[2,256,128]{2,1,0:T(8,128)(2,1)S(1)}, u32[]{:S(2)}, u32[]{:S(2)}) collective-permute-start(bf16[2,256,128]{2,1,0:T(8,128)(2,1)S(1)} %get-tuple-element.52), channel_id=1, source_target_pairs={{16,32},{32,16},{48,64},{64,48},{80,96},{96,80},{17,33},{33,17},{4... | collective-permute-start | bytes 393224 | tf_op jit(solution)/shard_map/ppermute | solution.py:460
  2.3 10.2 %collective-permute-start = (bf16[2,256,128]{2,1,0:T(8,128)(2,1)S(1)}, bf16[2,256,128]{2,1,0:T(8,128)(2,1)S(1)}, u32[]{:S(2)}, u32[]{:S(2)}) collective-permute-start(bf16[2,256,128]{2,1,0:T(8,128)(2,1)S(1)} %get-tuple-element.53), channel_id=1, source_target_pairs={{0,16},{16,0},{32,48},{48,32},{64,80},{80,64},{96,112},{112,96},{1... | collective-permute-start | bytes 393224 | tf_op jit(solution)/shard_map/ppermute | solution.py:459
  12.6 20.0 %collective-permute-start.2 = (bf16[18,256,128]{2,1,0:T(8,128)(2,1)S(1)}, bf16[18,256,128]{2,1,0:T(8,128)(2,1)S(1)}, u32[]{:S(2)}, u32[]{:S(2)}) collective-permute-start(bf16[18,256,128]{2,1,0:T(8,128)(2,1)S(1)} %get-tuple-element.36.cot_a), channel_id=1, source_target_pairs={{1,0},{2,1},{3,2},{4,3},{5,4},{6,5},{7,6},{8,7},{9,8},{10,9},{11,1... | collective-permute-start | bytes 3538952 | tf_op jit(solution)/shard_map/ppermute | solution.py:444
  38.6 2.4 %collective-permute-start.3 = (bf16[4,800,128]{2,1,0:T(8,128)(2,1)S(1)}, bf16[4,800,128]{2,1,0:T(8,128)(2,1)S(1)}, u32[]{:S(2)}, u32[]{:S(2)}) collective-permute-start(bf16[4,800,128]{2,1,0:T(8,128)(2,1)S(1)} %get-tuple-element.42), channel_id=1, source_target_pairs={{0,1},{1,0},{2,3},{3,2},{4,5},{5,4},{6,7},{7,6},{8,9},{9,8},{10,11... | collective-permute-start | bytes 2457608 | tf_op jit(solution)/shard_map/ppermute | solution.py:399
  41.2 6.5 %collective-permute-start.4 = (bf16[800,128]{1,0:T(8,128)(2,1)S(1)}, bf16[800,128]{1,0:T(8,128)(2,1)S(1)}, u32[]{:S(2)}, u32[]{:S(2)}) collective-permute-start(bf16[800,128]{1,0:T(8,128)(2,1)S(1)} %get-tuple-element.54), channel_id=1, source_target_pairs={{0,2},{1,65},{2,0},{3,67},{4,6},{5,69},{6,4},{7,71},{8,10},{9,73},... | collective-permute-start | bytes 614408 | tf_op jit(solution)/shard_map/ppermute | solution.py:403
  43.9 4.9 %collective-permute-start.6 = (bf16[800,128]{1,0:T(8,128)(2,1)S(1)}, bf16[800,128]{1,0:T(8,128)(2,1)S(1)}, u32[]{:S(2)}, u32[]{:S(2)}) collective-permute-start(bf16[800,128]{1,0:T(8,128)(2,1)S(1)} %get-tuple-element.55), channel_id=1, source_target_pairs={{0,18},{1,97},{2,16},{3,99},{4,22},{5,101},{6,20},{7,103},{8,26},{... | collective-permute-start | bytes 614408 | tf_op jit(solution)/shard_map/ppermute | solution.py:405
  45.0 6.0 %collective-permute-start.5 = (bf16[800,128]{1,0:T(8,128)(2,1)S(1)}, bf16[800,128]{1,0:T(8,128)(2,1)S(1)}, u32[]{:S(2)}, u32[]{:S(2)}) collective-permute-start(bf16[800,128]{1,0:T(8,128)(2,1)S(1)} %get-tuple-element.56), channel_id=1, source_target_pairs={{0,16},{1,33},{2,18},{3,35},{4,20},{5,37},{6,22},{7,39},{8,24},{9,... | collective-permute-start | bytes 614408 | tf_op jit(solution)/shard_map/ppermute | solution.py:404
  51.1 6.6 %collective-permute-start.9 = (bf16[800,128]{1,0:T(8,128)(2,1)S(1)}, bf16[800,128]{1,0:T(8,128)(2,1)S(1)}, u32[]{:S(2)}, u32[]{:S(2)}) collective-permute-start(bf16[800,128]{1,0:T(8,128)(2,1)S(1)} %fusion.2), channel_id=1, source_target_pairs={{0,96},{1,13},{2,98},{3,15},{4,100},{5,1},{6,102},{7,3},{8,104},{9... | collective-permute-start | bytes 614408 | tf_op jit(solution)/shard_map/ppermute | solution.py:405
  55.0 8.0 %collective-permute-start.8 = (bf16[800,128]{1,0:T(8,128)(2,1)S(1)}, bf16[800,128]{1,0:T(8,128)(2,1)S(1)}, u32[]{:S(2)}, u32[]{:S(2)}) collective-permute-start(bf16[800,128]{1,0:T(8,128)(2,1)S(1)} %fusion.2), channel_id=1, source_target_pairs={{0,32},{1,5},{2,34},{3,7},{4,36},{5,9},{6,38},{7,11},{8,40},{9,13}... | collective-permute-start | bytes 614408 | tf_op jit(solution)/shard_map/ppermute | solution.py:404
  55.0 8.0 %collective-permute-start.7 = (bf16[800,128]{1,0:T(8,128)(2,1)S(1)}, bf16[800,128]{1,0:T(8,128)(2,1)S(1)}, u32[]{:S(2)}, u32[]{:S(2)}) collective-permute-start(bf16[800,128]{1,0:T(8,128)(2,1)S(1)} %fusion.2), channel_id=1, source_target_pairs={{0,64},{1,9},{2,66},{3,11},{4,68},{5,13},{6,70},{7,15},{8,72},{9,1... | collective-permute-start | bytes 614408 | tf_op jit(solution)/shard_map/ppermute | solution.py:403
  63.2 5.0 %collective-permute-start.12 = (bf16[800,128]{1,0:T(8,128)(2,1)S(1)}, bf16[800,128]{1,0:T(8,128)(2,1)S(1)}, u32[]{:S(2)}, u32[]{:S(2)}) collective-permute-start(bf16[800,128]{1,0:T(8,128)(2,1)S(1)} %reduce-precision_convert_fusion.1), channel_id=1, source_target_pairs={{0,12},{1,19},{2,14},{3,17},{4,0},{5,23},{6,2},{7,21},{8,4},{9,27}... | collective-permute-start | bytes 614408 | tf_op jit(solution)/shard_map/ppermute | solution.py:405
  63.6 8.0 %collective-permute-start.11 = (bf16[800,128]{1,0:T(8,128)(2,1)S(1)}, bf16[800,128]{1,0:T(8,128)(2,1)S(1)}, u32[]{:S(2)}, u32[]{:S(2)}) collective-permute-start(bf16[800,128]{1,0:T(8,128)(2,1)S(1)} %reduce-precision_convert_fusion.1), channel_id=1, source_target_pairs={{0,4},{1,17},{2,6},{3,19},{4,8},{5,21},{6,10},{7,23},{8,12},{9,25}... | collective-permute-start | bytes 614408 | tf_op jit(solution)/shard_map/ppermute | solution.py:404
  64.7 6.9 %collective-permute-start.10 = (bf16[800,128]{1,0:T(8,128)(2,1)S(1)}, bf16[800,128]{1,0:T(8,128)(2,1)S(1)}, u32[]{:S(2)}, u32[]{:S(2)}) collective-permute-start(bf16[800,128]{1,0:T(8,128)(2,1)S(1)} %reduce-precision_convert_fusion.1), channel_id=1, source_target_pairs={{0,8},{1,3},{2,10},{3,1},{4,12},{5,7},{6,14},{7,5},{8,0},{9,11},{1... | collective-permute-start | bytes 614408 | tf_op jit(solution)/shard_map/ppermute | solution.py:403
  71.7 5.9 %collective-permute-start.15 = (bf16[800,128]{1,0:T(8,128)(2,1)S(1)}, bf16[800,128]{1,0:T(8,128)(2,1)S(1)}, u32[]{:S(2)}, u32[]{:S(2)}) collective-permute-start(bf16[800,128]{1,0:T(8,128)(2,1)S(1)} %reduce-precision_convert_fusion.own), channel_id=1, source_target_pairs={{0,16},{1,33},{2,18},{3,35},{4,20},{5,37},{6,22},{7,39},{8,24},{9,... | collective-permute-start | bytes 614408 | tf_op jit(solution)/shard_map/ppermute | solution.py:404
  72.2 8.4 %collective-permute-start.14 = (bf16[800,128]{1,0:T(8,128)(2,1)S(1)}, bf16[800,128]{1,0:T(8,128)(2,1)S(1)}, u32[]{:S(2)}, u32[]{:S(2)}) collective-permute-start(bf16[800,128]{1,0:T(8,128)(2,1)S(1)} %reduce-precision_convert_fusion.own), channel_id=1, source_target_pairs={{0,2},{1,65},{2,0},{3,67},{4,6},{5,69},{6,4},{7,71},{8,10},{9,73},... | collective-permute-start | bytes 614408 | tf_op jit(solution)/shard_map/ppermute | solution.py:403
  75.2 5.3 %collective-permute-start.13 = (bf16[800,128]{1,0:T(8,128)(2,1)S(1)}, bf16[800,128]{1,0:T(8,128)(2,1)S(1)}, u32[]{:S(2)}, u32[]{:S(2)}) collective-permute-start(bf16[800,128]{1,0:T(8,128)(2,1)S(1)} %reduce-precision_convert_fusion.own), channel_id=1, source_target_pairs={{0,18},{1,97},{2,16},{3,99},{4,22},{5,101},{6,20},{7,103},{8,26},{... | collective-permute-start | bytes 614408 | tf_op jit(solution)/shard_map/ppermute | solution.py:405
  80.7 8.6 %collective-permute-start.16 = (bf16[4,800,128]{2,1,0:T(8,128)(2,1)S(1)}, bf16[4,800,128]{2,1,0:T(8,128)(2,1)S(1)}, u32[]{:S(2)}, u32[]{:S(2)}) collective-permute-start(bf16[4,800,128]{2,1,0:T(8,128)(2,1)S(1)} %pad_maximum_fusion), channel_id=1, source_target_pairs={{0,1},{1,0},{2,3},{3,2},{4,5},{5,4},{6,7},{7,6},{8,9},{9,8},{10,11... | collective-permute-start | bytes 2457608 | tf_op jit(solution)/shard_map/ppermute | solution.py:399

commit v2 on v1

--- a/solution.py
+++ b/solution.py
@@ -23,62 +23,45 @@
     return jnp.dot(a, b, preferred_element_type=F32)
 
 
-CHUNK = 1024
-
-
-def forward_kernel(lat_h, w1_h, w2_h, k_h, cot_h, *refs):
-    lat, act, slope, ft, taps, w1t, w2t, cot_a, cot_b, w1, w2, ker, sems = refs
-    chunks = lat.shape[0] // CHUNK
-    weights = [
-        pltpu.make_async_copy(src, dst, sems.at[n])
-        for n, (src, dst) in enumerate(((w1_h, w1), (w2_h, w2), (k_h, ker)))
-    ]
-    frames = [
-        pltpu.make_async_copy(cot_h.at[n], dst.at[pl.ds(1, ROWS)], sems.at[3 + n])
-        for n, dst in enumerate((cot_a, cot_b))
-    ]
-
-    def pixels(k):
-        where = pl.ds(k * CHUNK, CHUNK)
-        return pltpu.make_async_copy(lat_h.at[where], lat.at[where], sems.at[5 + k])
-
-    weights[0].start()
-    pixels(0).start()
-    weights[1].start()
-    for k in range(1, chunks):
-        pixels(k).start()
-    weights[2].start()
-    for copy in frames:
+def project(x, w1, w2, act, slope, ft):
+    pre = dot(x, w1[...])
+    sig = 0.5 * jnp.tanh(0.5 * pre) + 0.5
+    hidden = pre * sig
+    slope[...] = (sig + hidden * (1.0 - sig)).astype(BF)
+    hidden = hidden.astype(BF)
+    act[...] = hidden
+    mixed = 0.5 * (x.astype(F32) + dot(hidden, w2[...]))
+    ll, lh, hl, hh = (mixed[:, 128 * b : 128 * (b + 1)] for b in range(4))
+    s, d, t, u = ll + lh, ll - lh, hl + hh, hl - hh
+    for i in range(x.shape[0] // 128):
+        px = slice(128 * i, 128 * (i + 1))
+        for p, (m, n) in enumerate(((s, t), (d, u))):
+            row = 2 * i + p
+            lanes = slice(128 * row, 128 * (row + 1))
+            ft[0:128, lanes] = (m[px] + n[px]).astype(BF).T
+            ft[128:256, lanes] = (m[px] - n[px]).astype(BF).T
+
+
+def first_kernel(lat_h, w1_h, w2_h, k_h, cot_h, lat, w1, w2, ker, cot_a, cot_b, act, slope, ft, sems):
+    n_px = act.shape[0]
+    pairs = [(w1_h, w1), (lat_h.at[pl.ds(0, n_px)], lat.at[pl.ds(0, n_px)]), (w2_h, w2)]
+    pairs += [(cot_h.at[n], dst.at[pl.ds(1, ROWS)]) for n, dst in enumerate((cot_a, cot_b))]
+    pairs += [(lat_h.at[pl.ds(n_px, n_px)], lat.at[pl.ds(n_px, n_px)]), (k_h, ker)]
+    copies = [pltpu.make_async_copy(src, dst, sems.at[n]) for n, (src, dst) in enumerate(pairs)]
+    for copy in copies:
         copy.start()
-    weights[0].wait()
-    pixels(0).wait()
-    weights[1].wait()
-
-    for k in range(chunks):
-        if k:
-            pixels(k).wait()
-        here = slice(k * CHUNK, (k + 1) * CHUNK)
-        x = lat[here]
-        pre = dot(x, w1[...])
-        sig = 0.5 * jnp.tanh(0.5 * pre) + 0.5
-        hidden = pre * sig
-        slope[here] = (sig + hidden * (1.0 - sig)).astype(BF)
-        hidden = hidden.astype(BF)
-        act[here] = hidden
-        mixed = 0.5 * (x.astype(F32) + dot(hidden, w2[...]))
-        ll, lh, hl, hh = (mixed[:, 128 * b : 128 * (b + 1)] for b in range(4))
-        s, d, t, u = ll + lh, ll - lh, hl + hh, hl - hh
-        for i in range(CHUNK // 128):
-            px = slice(128 * i, 128 * (i + 1))
-            for p, (m, n) in enumerate(((s, t), (d, u))):
-                row = 2 * (k * CHUNK // 128 + i) + p
-                frame, row = row // ROWS, row % ROWS
-                lanes = slice(128 * row, 128 * (row + 1))
-                ft[frame, 0:128, lanes] = (m[px] + n[px]).astype(BF).T
-                ft[frame, 128:256, lanes] = (m[px] - n[px]).astype(BF).T
+    for copy in copies[:3]:
+        copy.wait()
+    project(lat[0:n_px], w1, w2, act, slope, ft)
+    for copy in copies[3:]:
+        copy.wait()
+
+
+def second_kernel(lat, w1, w2, ker, _, act, slope, ft, taps, w1t, w2t):
+    n_px = act.shape[0]
+    project(lat[n_px : 2 * n_px], w1, w2, act, slope, ft)
     w1t[...] = w1[...].T
     w2t[...] = w2[...].T
-    weights[2].wait()
     for t in range(6):
         for q in range(2):
             col = 3 * (1 - q)
@@ -88,29 +71,42 @@
             for q in range(2):
                 col = 2 - dx + q
                 taps[t, 128 * col : 128 * (col + 1), 128 * q : 128 * (q + 1)] = tap
-    for copy in frames:
-        copy.wait()
-
-
-def forward(latent, w1, w2, kernel, cotangent):
+
+
+VMEM_SPEC = pl.BlockSpec(memory_space=pltpu.VMEM)
+ANY_SPEC = pl.BlockSpec(memory_space=pl.ANY)
+
+
+def frame_shapes(n_px):
+    return [(n_px, 512), (n_px, 512), (256, 2 * n_px)]
+
+
+def first(latent, w1, w2, kernel, cotangent):
     n = latent.shape[0]
     frame = (ROWS + 2,) + cotangent.shape[2:]
-    vmem = pl.BlockSpec(memory_space=pltpu.VMEM)
-    shapes = [(n, 512), (n, 512), (n, 512), (2, 256, n), (6, 512, 256), (512, 512), (512, 512), frame, frame]
-    return pl.pallas_call(
-        forward_kernel,
-        in_specs=[pl.BlockSpec(memory_space=pl.ANY)] * 5,
-        out_specs=[vmem] * len(shapes),
+    shapes = [(n, 512), (512, 512), (512, 512), (18, 128, 128), frame, frame] + frame_shapes(n // 2)
+    return pl.pallas_call(
+        first_kernel,
+        in_specs=[ANY_SPEC] * 5,
+        out_specs=[VMEM_SPEC] * len(shapes),
         out_shape=[pltpu.VMEM(shape, BF) for shape in shapes],
-        scratch_shapes=[
-            pltpu.VMEM((512, 512), BF),
-            pltpu.VMEM((512, 512), BF),
-            pltpu.VMEM((18, 128, 128), BF),
-            pltpu.SemaphoreType.DMA((5 + n // CHUNK,)),
-        ],
-        cost_estimate=pl.CostEstimate(flops=8 * n * 512 * 512, bytes_accessed=12 * MIB, transcendentals=n * 512),
+        scratch_shapes=[pltpu.SemaphoreType.DMA((7,))],
+        cost_estimate=pl.CostEstimate(flops=4 * n * 512 * 512, bytes_accessed=8 * MIB, transcendentals=n * 256),
         compiler_params=pltpu.CompilerParams(vmem_limit_bytes=16 * MIB),
     )(*in_hbm(latent, w1, w2, kernel.reshape(18, 128, 128), cotangent))
+
+
+def second(lat, w1, w2, ker, after):
+    n = lat.shape[0]
+    shapes = frame_shapes(n // 2) + [(6, 512, 256), (512, 512), (512, 512)]
+    return pl.pallas_call(
+        second_kernel,
+        in_specs=[VMEM_SPEC] * 4 + [ANY_SPEC],
+        out_specs=[VMEM_SPEC] * len(shapes),
+        out_shape=[pltpu.VMEM(shape, BF) for shape in shapes],
+        cost_estimate=pl.CostEstimate(flops=4 * n * 512 * 512, bytes_accessed=8 * MIB, transcendentals=n * 256),
+        compiler_params=pltpu.CompilerParams(vmem_limit_bytes=16 * MIB),
+    )(*in_vmem(lat, w1, w2, ker, after))
 
 
 def border_kernel(first, second, _, __, cot_a, cot_b):
@@ -187,7 +183,7 @@
 def add_taps(gk, ft, dt, planes, before):
     cols = planes.reshape((ROWS + 2) * 128, 512)
     for dy in range(3):
-        got = dot(ft, cols[128 * (2 - dy) : 128 * (ROWS + 2 - dy)])
+        got = dot(ft[...], cols[128 * (2 - dy) : 128 * (ROWS + 2 - dy)])
         for dx in range(3):
             col = 2 - dx
             both = got[0:128, 128 * col : 128 * (col + 1)] + got[128:256, 128 * (col + 1) : 128 * (col + 2)]
@@ -205,7 +201,7 @@
             gw[where] = part if before is None else before[where] + part
 
 
-def early_kernel(lat, act, slope, ft, taps, w1t, w2t, cot_a, cot_b, gl_h, part, gk, gw, *scratch):
+def early_kernel(lat, act, slope, ft_a, ft_b, taps, w1t, w2t, cot_a, cot_b, gl_h, part, gk, gw, *scratch):
     planes_a, planes_b, spread, gm, gp, gl, sem = scratch
     n_px = gm.shape[0]
     mine = pl.ds(0, n_px)
@@ -225,14 +221,14 @@
 
     lax.fori_loop(0, ROWS // STEP, back, 0)
     lax.fori_loop(0, ROWS // STEP, ahead, 0)
-    gp[...] = (dot(gm[...], w2t[...]) * slope[mine].astype(F32)).astype(BF)
+    gp[...] = (dot(gm[...], w2t[...]) * slope[...].astype(F32)).astype(BF)
     gl[...] = (gm[...].astype(F32) + dot(gp[...], w1t[...])).astype(BF)
     out = pltpu.make_async_copy(gl, gl_h.at[mine], sem)
     out.start()
-    add_taps(gk, ft[0], 1, planes_a, None)
-    add_taps(gk, ft[0], 0, planes_b, None)
-    add_taps(gk, ft[1], 1, planes_b, gk)
-    add_weights(gw, ((lat.at[mine], gp), (act.at[mine], gm)), None)
+    add_taps(gk, ft_a, 1, planes_a, None)
+    add_taps(gk, ft_a, 0, planes_b, None)
+    add_taps(gk, ft_b, 1, planes_b, gk)
+    add_weights(gw, ((lat.at[mine], gp), (act, gm)), None)
     out.wait()
 
 
@@ -248,10 +244,10 @@
         return carry
 
     lax.fori_loop(0, ROWS // STEP, back, 0)
-    gp[...] = (dot(gm[...], w2t[...]) * slope[mine].astype(F32)).astype(BF)
+    gp[...] = (dot(gm[...], w2t[...]) * slope[...].astype(F32)).astype(BF)
     gk[128 * 9 :] = sumk[128 * 9 :]
-    add_taps(gk, ft[1], 0, planes, sumk)
-    add_weights(gw, ((lat.at[mine], gp), (act.at[mine], gm)), sumw)
+    add_taps(gk, ft, 0, planes, sumk)
+    add_weights(gw, ((lat.at[mine], gp), (act, gm)), sumw)
     ids = block_ids()
     for r in range(8):
         packed = (keep, send)[r // 4].at[r % 4]
@@ -271,17 +267,15 @@
     out.wait()
 
 
-VMEM_SPEC = pl.BlockSpec(memory_space=pltpu.VMEM)
-ANY_SPEC = pl.BlockSpec(memory_space=pl.ANY)
 PLANES = (ROWS + 2, 128, 512)
 SUMS = [(2304, 128), (1024, 512)]
 SPREAD = (2, 272, 128)
 
 
-def early(lat, act, slope, ft, taps, w1t, w2t, cot_a, cot_b):
+def early(lat, *rest):
     n_px = lat.shape[0] // 2
     sums = [pltpu.VMEM(shape, F32) for shape in SUMS]
-    ops = in_vmem(lat, act, slope, ft, taps, w1t, w2t, cot_a, cot_b)
+    ops = in_vmem(lat, *rest)
     return pl.pallas_call(
         early_kernel,
         in_specs=[VMEM_SPEC] * len(ops),
@@ -324,23 +318,27 @@
     )(*in_vmem(gm, gp, w1t), *in_hbm(grad))
 
 
-def unpack_kernel(own, near, far, last, other, first_h, second_h, gk_h, gw, gk, sems):
+def unpack_kernel(side, *refs):
+    if side:
+        (other, *_), refs = refs[:4], refs[4:]
+        pieces = [other.at[r] for r in range(4)]
+    else:
+        pieces, refs = refs[:4], refs[4:]
+    first_h, second_h, gk_h, gw, gk, sems = refs
     copies = []
-    ids = block_ids()
-    for r in range(8):
-        b = ids[r]
-        piece = (own, near, far, last)[r] if r < 4 else other.at[r - 4]
-        wide = pl.ds(pl.multiple_of(b * 128, 128), 128)
+    ids = block_ids()[4 * side : 4 * side + 4]
+    for r in range(4):
+        b, piece = ids[r], pieces[r]
+        down = pl.ds(pl.multiple_of((b % 4) * 128, 128), 128)
         low = pl.ds(pl.multiple_of(b * 288, 32), 288)
         for lane in range(4):
             cols = slice(128 * lane, 128 * (lane + 1))
-            gw[wide, cols] = piece[cols, :].astype(F32)
-        gk[low, :] = piece[512:800, :].astype(F32)
-        copies.append(pltpu.make_async_copy(gk.at[low], gk_h.at[low], sems.at[0, r]))
+            gw[r, :, cols] = piece[cols, :].astype(F32)
+        gk[r] = piece[512:800, :].astype(F32)
+        copies.append(pltpu.make_async_copy(gk.at[r], gk_h.at[low], sems.at[0, r]))
         copies[-1].start()
-        down = pl.ds(pl.multiple_of((b % 4) * 128, 128), 128)
-        to_first = pltpu.make_async_copy(gw.at[wide], first_h.at[down], sems.at[1, r])
-        to_second = pltpu.make_async_copy(gw.at[wide], second_h.at[down], sems.at[1, r])
+        to_first = pltpu.make_async_copy(gw.at[r], first_h.at[down], sems.at[1, r])
+        to_second = pltpu.make_async_copy(gw.at[r], second_h.at[down], sems.at[1, r])
         pl.when(b < 4)(to_first.start)
         pl.when(b >= 4)(to_second.start)
         copies.append(to_first)
@@ -348,21 +346,21 @@
         copy.wait()
 
 
-def unpack(*pieces):
-    vmem = pl.BlockSpec(memory_space=pltpu.VMEM)
-    sds = jax.ShapeDtypeStruct
-    return pl.pallas_call(
-        unpack_kernel,
-        in_specs=[vmem] * 5,
-        out_specs=[pl.BlockSpec(memory_space=pl.ANY)] * 3,
-        out_shape=[sds((512, 512), F32), sds((512, 512), F32), sds((2304, 128), F32)],
+def unpack(side, pieces, outs=()):
+    return pl.pallas_call(
+        functools.partial(unpack_kernel, side),
+        in_specs=[VMEM_SPEC] * len(pieces) + [ANY_SPEC] * len(outs),
+        out_specs=[ANY_SPEC] * 3,
+        out_shape=[pltpu.HBM(shape, F32) for shape in ((512, 512), (512, 512), (2304, 128))],
+        input_output_aliases={1 + n: n for n in range(len(outs))},
         scratch_shapes=[
-            pltpu.VMEM((1024, 512), F32),
-            pltpu.VMEM((2304, 128), F32),
-            pltpu.SemaphoreType.DMA((2, 8)),
+            pltpu.VMEM((4, 128, 512), F32),
+            pltpu.VMEM((4, 288, 128), F32),
+            pltpu.SemaphoreType.DMA((2, 4)),
         ],
-        compiler_params=pltpu.CompilerParams(vmem_limit_bytes=16 << 20),
-    )(*pieces)
+        cost_estimate=pl.CostEstimate(flops=1 << 20, bytes_accessed=3 * MIB, transcendentals=0),
+        compiler_params=pltpu.CompilerParams(vmem_limit_bytes=8 * MIB),
+    )(*pieces, *in_hbm(*outs))
 
 
 BOTH = ("ha", "ta")
@@ -416,11 +414,11 @@
 
 
 def block_ids():
-    x, y, _, core = place()
+    _, y, z, core = place()
     ids = []
     for other in range(2):
         owner = core ^ other
-        start = jnp.where(owner == 0, x, y)
+        start = jnp.where(owner == 0, z, y)
         ids += [owner * 4 + (start + k) % 4 for k in range(4)]
     return ids
 
@@ -431,12 +429,13 @@
 
 def sum_all(keep, got):
     parts = [add2(keep[k], got[k]) for k in range(4)]
-    own = add4(parts[0], *trade(*parts[1:], (0, 1)))
-    own = add4(own, *trade(own, own, own, (1, 2)))
-    own = add4(own, *trade(own, own, own, (2, 0)))
-    before, across, after = trade(own, own, own, (0, 1))
+    own = add4(parts[0], *trade(*parts[1:], (2, 1)))
+    own = add4(own, *trade(own, own, own, (1, 0)))
+    own = add4(own, *trade(own, own, own, (0, 2)))
+    before, across, after = trade(own, own, own, (2, 1))
     other = swap(jnp.stack([own, after, across, before]))
-    return own, after, across, before, other
+    outs = unpack(0, (own, after, across, before))
+    return unpack(1, (other,), outs)
 
 
 def neighbour(value, axis, step):
@@ -458,17 +457,17 @@
     meet = meetings(lax.axis_size("ha"))
     inner = lax.ppermute(jnp.where(odd == 1, top, bottom), "ha", meet[0])
     outer = lax.ppermute(jnp.where(odd == 1, bottom, top), "ha", meet[1])
-    *rest, cot_a, cot_b = forward(flat, w_first, w_second, kernel, cotangent)
+    lat, w1, w2, ker, cot_a, cot_b, act_a, slope_a, ft_a = first(flat, w_first, w_second, kernel, cotangent)
     cot_a, cot_b = border(inner, outer, cot_a, cot_b)
     later = neighbour(cot_a, "ta", -1)
-    lat, act, slope, ft, taps, w1t, w2t = rest
-    grad, part, gk, gw = early(*rest, cot_a, cot_b)
-    gm, gp, keep, send = late(lat, act, slope, ft, taps, w2t, later, part, gk, gw)
+    act_b, slope_b, ft_b, taps, w1t, w2t = second(lat, w1, w2, ker, cot_b)
+    grad, part, gk, gw = early(lat, act_a, slope_a, ft_a, ft_b, taps, w1t, w2t, cot_a, cot_b)
+    gm, gp, keep, send = late(lat, act_b, slope_b, ft_b, taps, w2t, later, part, gk, gw)
     got = swap(send)
     grad = last(gm, gp, w1t, grad)
     got, grad = lax.optimization_barrier((got, grad))
-    first, second, gk = unpack(*sum_all(keep, got))
-    return grad.reshape(latent.shape), first, second, gk.reshape(kernel.shape)
+    grad_first, grad_second, gk = sum_all(keep, got)
+    return grad.reshape(latent.shape), grad_first, grad_second, gk.reshape(kernel.shape)
 
 
 def solution(mesh):

time: 91.5 us -> 87.8 us (0.960)
  waiting for transfers between devices: 27 us -> 19.3 us
  starting transfers between devices: 32 us -> 35.4 us
    ppermute x4, starting transfers between devices: 8.66 us -> 13 us  [trade(): across = lax.ppermute(far, BOTH, along(axes, step_by(2)))]
    ppermute x4, starting transfers between devices: 5.78 us -> 9.61 us  [trade(): after = lax.ppermute(last, BOTH, along(axes, step_by(3)))]
    ppermute x4, waiting for transfers between devices: 13 us -> 10.4 us  [trade(): before = lax.ppermute(near, BOTH, along(axes, step_by(1)))]
    ppermute x1, starting transfers between devices: 4.63 us -> 2.12 us  [shards(): inner = lax.ppermute(jnp.where(odd == 1, top, bottom), 'ha', meet[0])]
    ppermute x4, waiting for transfers between devices: 5.26 us -> 3.25 us  [trade(): across = lax.ppermute(far, BOTH, along(axes, step_by(2)))]
    ppermute x1, waiting for transfers between devices: 1.75 us -> 0.01 us  [neighbour(): lax.ppermute(value, axis, [(i, i + step) for i in range(count) if 0 <= i...]
    ppermute x2, starting transfers between devices: 6.68 us -> 4.99 us  [swap(): return lax.ppermute(value, BOTH, [(i, i ^ 1) for i in range(128)])]
    ppermute x2, waiting for transfers between devices: 2.58 us -> 1.31 us  [swap(): return lax.ppermute(value, BOTH, [(i, i ^ 1) for i in range(128)])]
  transfers between devices with their start and end apart: 17 -> 17, of which waited for: 13 -> 12; matrix products, arithmetic and copies ran while one was open for 0% -> 0% of each run, Pallas kernels for 24% -> 26%
where the time goes in v2:
time: 87.8 us; the launch traced here: 87.6 us
  starting transfers between devices  35.4 us (40%)
  Pallas kernels  30.3 us (35%)
  waiting for transfers between devices  19.3 us (22%)
  other arithmetic  1.64 us (2%)
  between operations  0.96 us (1%)
    pallas_call x1, Pallas kernels, early(): pl.pallas_call(early_kernel, in_specs=[VMEM_SPEC] * len(ops), out_specs=[...  14.6 us
    ppermute x4, starting transfers between devices, trade(): across = lax.ppermute(far, BOTH, along(axes, step_by(2)))  13 us
    ppermute x4, waiting for transfers between devices, trade(): before = lax.ppermute(near, BOTH, along(axes, step_by(1)))  10.4 us
    ppermute x4, starting transfers between devices, trade(): after = lax.ppermute(last, BOTH, along(axes, step_by(3)))  9.61 us
    pallas_call x1, Pallas kernels, late(): pl.pallas_call(late_kernel, in_specs=[VMEM_SPEC] * len(ops), out_specs=[V...  6.07 us
    ppermute x2, starting transfers between devices, swap(): return lax.ppermute(value, BOTH, [(i, i ^ 1) for i in range(128)])  4.99 us
    ppermute x4, waiting for transfers between devices, trade(): after = lax.ppermute(last, BOTH, along(axes, step_by(3)))  4.39 us
    pallas_call x1, Pallas kernels, first(): pl.pallas_call(first_kernel, in_specs=[ANY_SPEC] * 5, out_specs=[VMEM_SPE...  3.42 us
  transfers between devices with their start and end apart: 17, of which 12 were waited for; matrix products, arithmetic and copies ran while one was open for 0% of the time, Pallas kernels for 26%

profile of v2, /device:TPU:1, one launch (start us, length us, event | category | flops | bytes accessed | tf_op | source)
XLA Modules:
  0.0 87.6 jit_solution(17127863628541039011)
XLA Ops:
  0.6 1.0 %fusion.8 = (bf16[2,256,128]{2,1,0:T(8,128)(2,1)S(1)}, bf16[2,256,128]{2,1,0:T(8,128)(2,1)S(1)}) fusion(pred[]{:T(512)S(6)} %eq.6, bf16[2,16,256,128]{3,2,1,0:T(8,128)(2,1)} %cot_h.1), kind=kLoop, calls=%fused_computation.18 | loop fusion | flops 131072 | bytes 524289 | tf_op jit(solution)/shard_map/jit(_where)/select_n | solution.py:459
  1.6 2.1 %collective-permute-start = (bf16[2,256,128]{2,1,0:T(8,128)(2,1)S(1)}, bf16[2,256,128]{2,1,0:T(8,128)(2,1)S(1)}, u32[]{:S(2)}, u32[]{:S(2)}) collective-permute-start(bf16[2,256,128]{2,1,0:T(8,128)(2,1)S(1)} %get-tuple-element.71), channel_id=1, source_target_pairs={{0,16},{16,0},{32,48},{48,32},{64,80},{80,64},{96,112},{112,96},{1... | collective-permute-start | bytes 393224 | tf_op jit(solution)/shard_map/ppermute | solution.py:458
  3.8 0.7 collective-permute-start.1
  4.4 3.4 %shard_map.84 = (bf16[2048,512]{1,0:T(8,128)(2,1)S(1)}, bf16[512,512]{1,0:T(8,128)(2,1)S(1)}, bf16[512,512]{1,0:T(8,128)(2,1)S(1)}, bf16[18,128,128]{2,1,0:T(8,1...) custom-call(bf16[2048,512]{1,0:T(8,128)(2,1)} %bitcast.39, ...), custom_call_target="tpu_custom_call" | custom-call | flops 2147483648 | bytes 8388608 | tf_op jit(solution)/shard_map/pallas_call | solution.py:88
  7.9 3.0 %collective-permute-start.2 = (bf16[18,256,128]{2,1,0:T(8,128)(2,1)S(1)}, bf16[18,256,128]{2,1,0:T(8,128)(2,1)S(1)}, u32[]{:S(2)}, u32[]{:S(2)}) collective-permute-start(bf16[18,256,128]{2,1,0:T(8,128)(2,1)S(1)} %get-tuple-element.49.cot_a), channel_id=1, source_target_pairs={{1,0},{2,1},{3,2},{4,3},{5,4},{6,5},{7,6},{8,7},{9,8},{10,9},{11,1... | collective-permute-start | bytes 3538952 | tf_op jit(solution)/shard_map/ppermute | solution.py:443
  11.0 2.0 %shard_map.86 = (bf16[1024,512]{1,0:T(8,128)(2,1)S(1)}, bf16[1024,512]{1,0:T(8,128)(2,1)S(1)}, bf16[256,2048]{1,0:T(8,128)(2,1)S(1)}, bf16[6,512,256]{2,1,0:T(8,...) custom-call(bf16[2048,512]{1,0:T(8,128)(2,1)S(1)} %get-tuple-element.37.lat, ...), custom_call_target="tpu_custom_call" | custom-call | flops 2147483648 | bytes 8388608 | tf_op jit(solution)/shard_map/pallas_call | solution.py:102
  13.0 14.6 %shard_map.87 = (bf16[2048,512]{1,0:T(8,128)(2,1)}, f32[2048,256]{1,0:T(8,128)S(1)}, f32[2304,128]{1,0:T(8,128)S(1)}, f32[1024,512]{1,0:T(8,128)S(1)}) custom-call(bf16[2048,512]{1,0:T(8,128)(2,1)S(1)} %get-tuple-element.37.lat, bf16[1024,512]{1,0:T(8,128)(2,1)S(1)} %get-tuple-element.50.act, bf16[1024,512]{1,0:T(8,128)(2,1)S(1)} %get-tuple-element.51.slope, ...), custom_call_target="tpu_custom_call" | custom-call | flops 10737418240 | bytes 16777216 | tf_op jit(solution)/shard_map/pallas_call | solution.py:279
  27.6 6.1 %shard_map.88 = (bf16[1024,512]{1,0:T(8,128)(2,1)S(1)}, bf16[1024,512]{1,0:T(8,128)(2,1)S(1)}, bf16[4,800,128]{2,1,0:T(8,128)(2,1)S(1)}, bf16[4,800,128]{2,1,0:T(8,128)(2,1)S(1)}) custom-call(bf16[2048,512]{1,0:T(8,128)(2,1)S(1)} %get-tuple-element.37.lat, bf16[1024,512]{1,0:T(8,128)(2,1)S(1)} %get-tuple-element.44.act, ...), custom_call_target="tpu_custom_call" | custom-call | flops 6442450944 | bytes 16777216 | tf_op jit(solution)/shard_map/pallas_call | solution.py:296
  34.0 1.7 %shard_map.89 = bf16[2048,512]{1,0:T(8,128)(2,1)} custom-call(bf16[1024,512]{1,0:T(8,128)(2,1)S(1)} %get-tuple-element.58.gm, bf16[1024,512]{1,0:T(8,128)(2,1)S(1)} %get-tuple-element.59.gp, bf16[512,512]{1,0:T(8,128)(2,1)S(1)} %get-tuple-element.53.w1t, bf16[2048,512]{1,0:T(8,128)(2,1)} %get-tuple-element.60._), custom_call_target="tpu_custom_call", output_to_operand_aliasing={{}: (3, {})} | custom-call | flops 536870912 | bytes 4194304 | tf_op jit(solution)/shard_map/pallas_call | solution.py:309
  35.7 0.6 collective-permute-done.3
  36.5 6.6 %collective-permute-start.4 = (bf16[800,128]{1,0:T(8,128)(2,1)S(1)}, bf16[800,128]{1,0:T(8,128)(2,1)S(1)}, u32[]{:S(2)}, u32[]{:S(2)}) collective-permute-start(bf16[800,128]{1,0:T(8,128)(2,1)S(1)} %get-tuple-element.72), channel_id=1, source_target_pairs={{0,8},{1,65},{2,10},{3,67},{4,12},{5,69},{6,14},{7,71},{8,0},{9,73... | collective-permute-start | bytes 614408 | tf_op jit(solution)/shard_map/ppermute | solution.py:401
  43.5 2.3 %collective-permute-start.6 = (bf16[800,128]{1,0:T(8,128)(2,1)S(1)}, bf16[800,128]{1,0:T(8,128)(2,1)S(1)}, u32[]{:S(2)}, u32[]{:S(2)}) collective-permute-start(bf16[800,128]{1,0:T(8,128)(2,1)S(1)} %get-tuple-element.73), channel_id=1, source_target_pairs={{0,12},{1,97},{2,14},{3,99},{4,0},{5,101},{6,2},{7,103},{8,4},{9,1... | collective-permute-start | bytes 614408 | tf_op jit(solution)/shard_map/ppermute | solution.py:403
  45.8 0.5 collective-permute-done.4
  46.2 2.7 %collective-permute-done.5 = bf16[800,128]{1,0:T(8,128)(2,1)S(1)} collective-permute-done((bf16[800,128]{1,0:T(8,128)(2,1)S(1)}, bf16[800,128]{1,0:T(8,128)(2,1)S(1)}, u32[]{:S(2)}, u32[]{:S(2)}) %collective-permute-start.5) | collective-permute-done | bytes 204832 | tf_op jit(solution)/shard_map/ppermute | solution.py:402
  49.1 2.5 %collective-permute-start.7 = (bf16[800,128]{1,0:T(8,128)(2,1)S(1)}, bf16[800,128]{1,0:T(8,128)(2,1)S(1)}, u32[]{:S(2)}, u32[]{:S(2)}) collective-permute-start(bf16[800,128]{1,0:T(8,128)(2,1)S(1)} %fusion.2), channel_id=1, source_target_pairs={{0,64},{1,3},{2,66},{3,1},{4,68},{5,7},{6,70},{7,5},{8,72},{9,11},... | collective-permute-start | bytes 614408 | tf_op jit(solution)/shard_map/ppermute | solution.py:401
  52.0 2.3 %collective-permute-start.9 = (bf16[800,128]{1,0:T(8,128)(2,1)S(1)}, bf16[800,128]{1,0:T(8,128)(2,1)S(1)}, u32[]{:S(2)}, u32[]{:S(2)}) collective-permute-start(bf16[800,128]{1,0:T(8,128)(2,1)S(1)} %fusion.2), channel_id=1, source_target_pairs={{0,96},{1,19},{2,98},{3,17},{4,100},{5,23},{6,102},{7,21},{8,104},... | collective-permute-start | bytes 614408 | tf_op jit(solution)/shard_map/ppermute | solution.py:403
  54.3 1.0 %collective-permute-done.7 = bf16[800,128]{1,0:T(8,128)(2,1)S(1)} collective-permute-done((bf16[800,128]{1,0:T(8,128)(2,1)S(1)}, bf16[800,128]{1,0:T(8,128)(2,1)S(1)}, u32[]{:S(2)}, u32[]{:S(2)}) %collective-permute-start.7) | collective-permute-done | bytes 204832 | tf_op jit(solution)/shard_map/ppermute | solution.py:401
  55.2 2.5 %collective-permute-done.8 = bf16[800,128]{1,0:T(8,128)(2,1)S(1)} collective-permute-done((bf16[800,128]{1,0:T(8,128)(2,1)S(1)}, bf16[800,128]{1,0:T(8,128)(2,1)S(1)}, u32[]{:S(2)}, u32[]{:S(2)}) %collective-permute-start.8) | collective-permute-done | bytes 204832 | tf_op jit(solution)/shard_map/ppermute | solution.py:402
  57.9 3.7 %collective-permute-start.10 = (bf16[800,128]{1,0:T(8,128)(2,1)S(1)}, bf16[800,128]{1,0:T(8,128)(2,1)S(1)}, u32[]{:S(2)}, u32[]{:S(2)}) collective-permute-start(bf16[800,128]{1,0:T(8,128)(2,1)S(1)} %reduce-precision_convert_fusion.1), channel_id=1, source_target_pairs={{0,2},{1,9},{2,0},{3,11},{4,6},{5,13},{6,4},{7,15},{8,10},{9,1},{1... | collective-permute-start | bytes 614408 | tf_op jit(solution)/shard_map/ppermute | solution.py:401
  61.5 0.6 collective-permute-start.11
  62.2 2.0 %collective-permute-start.12 = (bf16[800,128]{1,0:T(8,128)(2,1)S(1)}, bf16[800,128]{1,0:T(8,128)(2,1)S(1)}, u32[]{:S(2)}, u32[]{:S(2)}) collective-permute-start(bf16[800,128]{1,0:T(8,128)(2,1)S(1)} %reduce-precision_convert_fusion.1), channel_id=1, source_target_pairs={{0,18},{1,13},{2,16},{3,15},{4,22},{5,1},{6,20},{7,3},{8,26},{9,5}... | collective-permute-start | bytes 614408 | tf_op jit(solution)/shard_map/ppermute | solution.py:403
  64.2 0.5 collective-permute-done.10
  64.7 3.0 %collective-permute-done.11 = bf16[800,128]{1,0:T(8,128)(2,1)S(1)} collective-permute-done((bf16[800,128]{1,0:T(8,128)(2,1)S(1)}, bf16[800,128]{1,0:T(8,128)(2,1)S(1)}, u32[]{:S(2)}, u32[]{:S(2)}) %collective-permute-start.11) | collective-permute-done | bytes 204832 | tf_op jit(solution)/shard_map/ppermute | solution.py:402
  67.9 3.0 %collective-permute-start.13 = (bf16[800,128]{1,0:T(8,128)(2,1)S(1)}, bf16[800,128]{1,0:T(8,128)(2,1)S(1)}, u32[]{:S(2)}, u32[]{:S(2)}) collective-permute-start(bf16[800,128]{1,0:T(8,128)(2,1)S(1)} %reduce-precision_convert_fusion.refs_0_), channel_id=1, source_target_pairs={{0,12},{1,97},{2,14},{3,99},{4,0},{5,101},{6,2},{7,103},{8,4},{9,1... | collective-permute-start | bytes 614408 | tf_op jit(solution)/shard_map/ppermute | solution.py:403
  71.1 0.5 collective-permute-start.15
  71.6 4.2 %collective-permute-done.13.refs_1_ = bf16[800,128]{1,0:T(8,128)(2,1)S(1)} collective-permute-done((bf16[800,128]{1,0:T(8,128)(2,1)S(1)}, bf16[800,128]{1,0:T(8,128)(2,1)S(1)}, u32[]{:S(2)}, u32[]{:S(2)}) %collective-permute-start.13) | collective-permute-done | bytes 204832 | tf_op jit(solution)/shard_map/ppermute | solution.py:403
  75.9 1.3 %collective-permute-done.14.refs_2_ = bf16[800,128]{1,0:T(8,128)(2,1)S(1)} collective-permute-done((bf16[800,128]{1,0:T(8,128)(2,1)S(1)}, bf16[800,128]{1,0:T(8,128)(2,1)S(1)}, u32[]{:S(2)}, u32[]{:S(2)}) %collective-permute-start.14) | collective-permute-done | bytes 204832 | tf_op jit(solution)/shard_map/ppermute | solution.py:401
  77.2 2.2 %collective-permute-done.15.refs_3_ = bf16[800,128]{1,0:T(8,128)(2,1)S(1)} collective-permute-done((bf16[800,128]{1,0:T(8,128)(2,1)S(1)}, bf16[800,128]{1,0:T(8,128)(2,1)S(1)}, u32[]{:S(2)}, u32[]{:S(2)}) %collective-permute-start.15) | collective-permute-done | bytes 204832 | tf_op jit(solution)/shard_map/ppermute | solution.py:402
  79.5 4.7 %collective-permute-start.16 = (bf16[4,800,128]{2,1,0:T(8,128)(2,1)S(1)}, bf16[4,800,128]{2,1,0:T(8,128)(2,1)S(1)}, u32[]{:S(2)}, u32[]{:S(2)}) collective-permute-start(bf16[4,800,128]{2,1,0:T(8,128)(2,1)S(1)} %pad_maximum_fusion), channel_id=1, source_target_pairs={{0,1},{1,0},{2,3},{3,2},{4,5},{5,4},{6,7},{7,6},{8,9},{9,8},{10,11... | collective-permute-start | bytes 2457608 | tf_op jit(solution)/shard_map/ppermute | solution.py:397
  84.2 1.3 %shard_map.90 = (f32[512,512]{1,0:T(8,128)}, f32[512,512]{1,0:T(8,128)}, f32[2304,128]{1,0:T(8,128)}) custom-call(bf16[800,128]{1,0:T(8,128)(2,1)S(1)} %reduce-precision_convert_fusion.refs_0_, bf16[800,128]{1,0:T(8,128)(2,1)S(1)} %collective-permute-done.13.refs_1_, bf16[800,128]{1,0:T(8,128)(2,1)S(1)} %collective-permute-done.14.refs_2_, ...), custom_call_target="tpu_custom_call" | custom-call | flops 1048576 | bytes 3145728 | tf_op jit(solution)/shard_map/pallas_call | solution.py:350
  85.5 0.7 collective-permute-done.16.refs_0_
  86.2 1.3 %shard_map.91 = (f32[512,512]{1,0:T(8,128)}, f32[512,512]{1,0:T(8,128)}, f32[2304,128]{1,0:T(8,128)}) custom-call(bf16[4,800,128]{2,1,0:T(8,128)(2,1)S(1)} %collective-permute-done.16.refs_0_, f32[512,512]{1,0:T(8,128)} %get-tuple-element.64.refs_1_, ...), custom_call_target="tpu_custom_call", output_to_operand_aliasing={{0}: (1, {}), {1}: (2, {}), {2}: (3, {})} | custom-call | flops 1048576 | bytes 3145728 | tf_op jit(solution)/shard_map/pallas_call | solution.py:350
  (16 shorter events, 2.1 us)
Async XLA Ops:
  1.6 6.2 %collective-permute-start = (bf16[2,256,128]{2,1,0:T(8,128)(2,1)S(1)}, bf16[2,256,128]{2,1,0:T(8,128)(2,1)S(1)}, u32[]{:S(2)}, u32[]{:S(2)}) collective-permute-start(bf16[2,256,128]{2,1,0:T(8,128)(2,1)S(1)} %get-tuple-element.71), channel_id=1, source_target_pairs={{0,16},{16,0},{32,48},{48,32},{64,80},{80,64},{96,112},{112,96},{1... | collective-permute-start | bytes 393224 | tf_op jit(solution)/shard_map/ppermute | solution.py:458
  3.8 4.1 %collective-permute-start.1 = (bf16[2,256,128]{2,1,0:T(8,128)(2,1)S(1)}, bf16[2,256,128]{2,1,0:T(8,128)(2,1)S(1)}, u32[]{:S(2)}, u32[]{:S(2)}) collective-permute-start(bf16[2,256,128]{2,1,0:T(8,128)(2,1)S(1)} %get-tuple-element.70), channel_id=1, source_target_pairs={{16,32},{32,16},{48,64},{64,48},{80,96},{96,80},{17,33},{33,17},{4... | collective-permute-start | bytes 393224 | tf_op jit(solution)/shard_map/ppermute | solution.py:459
  7.9 19.7 %collective-permute-start.2 = (bf16[18,256,128]{2,1,0:T(8,128)(2,1)S(1)}, bf16[18,256,128]{2,1,0:T(8,128)(2,1)S(1)}, u32[]{:S(2)}, u32[]{:S(2)}) collective-permute-start(bf16[18,256,128]{2,1,0:T(8,128)(2,1)S(1)} %get-tuple-element.49.cot_a), channel_id=1, source_target_pairs={{1,0},{2,1},{3,2},{4,3},{5,4},{6,5},{7,6},{8,7},{9,8},{10,9},{11,1... | collective-permute-start | bytes 3538952 | tf_op jit(solution)/shard_map/ppermute | solution.py:443
  33.7 2.6 %collective-permute-start.3 = (bf16[4,800,128]{2,1,0:T(8,128)(2,1)S(1)}, bf16[4,800,128]{2,1,0:T(8,128)(2,1)S(1)}, u32[]{:S(2)}, u32[]{:S(2)}) collective-permute-start(bf16[4,800,128]{2,1,0:T(8,128)(2,1)S(1)} %get-tuple-element.57), channel_id=1, source_target_pairs={{0,1},{1,0},{2,3},{3,2},{4,5},{5,4},{6,7},{7,6},{8,9},{9,8},{10,11... | collective-permute-start | bytes 2457608 | tf_op jit(solution)/shard_map/ppermute | solution.py:397
  36.5 9.8 %collective-permute-start.4 = (bf16[800,128]{1,0:T(8,128)(2,1)S(1)}, bf16[800,128]{1,0:T(8,128)(2,1)S(1)}, u32[]{:S(2)}, u32[]{:S(2)}) collective-permute-start(bf16[800,128]{1,0:T(8,128)(2,1)S(1)} %get-tuple-element.72), channel_id=1, source_target_pairs={{0,8},{1,65},{2,10},{3,67},{4,12},{5,69},{6,14},{7,71},{8,0},{9,73... | collective-permute-start | bytes 614408 | tf_op jit(solution)/shard_map/ppermute | solution.py:401
  43.1 5.8 %collective-permute-start.5 = (bf16[800,128]{1,0:T(8,128)(2,1)S(1)}, bf16[800,128]{1,0:T(8,128)(2,1)S(1)}, u32[]{:S(2)}, u32[]{:S(2)}) collective-permute-start(bf16[800,128]{1,0:T(8,128)(2,1)S(1)} %get-tuple-element.74), channel_id=1, source_target_pairs={{0,4},{1,33},{2,6},{3,35},{4,8},{5,37},{6,10},{7,39},{8,12},{9,41}... | collective-permute-start | bytes 614408 | tf_op jit(solution)/shard_map/ppermute | solution.py:402
  43.5 5.4 %collective-permute-start.6 = (bf16[800,128]{1,0:T(8,128)(2,1)S(1)}, bf16[800,128]{1,0:T(8,128)(2,1)S(1)}, u32[]{:S(2)}, u32[]{:S(2)}) collective-permute-start(bf16[800,128]{1,0:T(8,128)(2,1)S(1)} %get-tuple-element.73), channel_id=1, source_target_pairs={{0,12},{1,97},{2,14},{3,99},{4,0},{5,101},{6,2},{7,103},{8,4},{9,1... | collective-permute-start | bytes 614408 | tf_op jit(solution)/shard_map/ppermute | solution.py:403
  49.1 6.2 %collective-permute-start.7 = (bf16[800,128]{1,0:T(8,128)(2,1)S(1)}, bf16[800,128]{1,0:T(8,128)(2,1)S(1)}, u32[]{:S(2)}, u32[]{:S(2)}) collective-permute-start(bf16[800,128]{1,0:T(8,128)(2,1)S(1)} %fusion.2), channel_id=1, source_target_pairs={{0,64},{1,3},{2,66},{3,1},{4,68},{5,7},{6,70},{7,5},{8,72},{9,11},... | collective-permute-start | bytes 614408 | tf_op jit(solution)/shard_map/ppermute | solution.py:401
  51.6 6.1 %collective-permute-start.8 = (bf16[800,128]{1,0:T(8,128)(2,1)S(1)}, bf16[800,128]{1,0:T(8,128)(2,1)S(1)}, u32[]{:S(2)}, u32[]{:S(2)}) collective-permute-start(bf16[800,128]{1,0:T(8,128)(2,1)S(1)} %fusion.2), channel_id=1, source_target_pairs={{0,32},{1,17},{2,34},{3,19},{4,36},{5,21},{6,38},{7,23},{8,40},{9,... | collective-permute-start | bytes 614408 | tf_op jit(solution)/shard_map/ppermute | solution.py:402
  52.0 5.7 %collective-permute-start.9 = (bf16[800,128]{1,0:T(8,128)(2,1)S(1)}, bf16[800,128]{1,0:T(8,128)(2,1)S(1)}, u32[]{:S(2)}, u32[]{:S(2)}) collective-permute-start(bf16[800,128]{1,0:T(8,128)(2,1)S(1)} %fusion.2), channel_id=1, source_target_pairs={{0,96},{1,19},{2,98},{3,17},{4,100},{5,23},{6,102},{7,21},{8,104},... | collective-permute-start | bytes 614408 | tf_op jit(solution)/shard_map/ppermute | solution.py:403
  57.9 6.8 %collective-permute-start.10 = (bf16[800,128]{1,0:T(8,128)(2,1)S(1)}, bf16[800,128]{1,0:T(8,128)(2,1)S(1)}, u32[]{:S(2)}, u32[]{:S(2)}) collective-permute-start(bf16[800,128]{1,0:T(8,128)(2,1)S(1)} %reduce-precision_convert_fusion.1), channel_id=1, source_target_pairs={{0,2},{1,9},{2,0},{3,11},{4,6},{5,13},{6,4},{7,15},{8,10},{9,1},{1... | collective-permute-start | bytes 614408 | tf_op jit(solution)/shard_map/ppermute | solution.py:401
  61.5 6.1 %collective-permute-start.11 = (bf16[800,128]{1,0:T(8,128)(2,1)S(1)}, bf16[800,128]{1,0:T(8,128)(2,1)S(1)}, u32[]{:S(2)}, u32[]{:S(2)}) collective-permute-start(bf16[800,128]{1,0:T(8,128)(2,1)S(1)} %reduce-precision_convert_fusion.1), channel_id=1, source_target_pairs={{0,16},{1,5},{2,18},{3,7},{4,20},{5,9},{6,22},{7,11},{8,24},{9,13}... | collective-permute-start | bytes 614408 | tf_op jit(solution)/shard_map/ppermute | solution.py:402
  62.2 5.6 %collective-permute-start.12 = (bf16[800,128]{1,0:T(8,128)(2,1)S(1)}, bf16[800,128]{1,0:T(8,128)(2,1)S(1)}, u32[]{:S(2)}, u32[]{:S(2)}) collective-permute-start(bf16[800,128]{1,0:T(8,128)(2,1)S(1)} %reduce-precision_convert_fusion.1), channel_id=1, source_target_pairs={{0,18},{1,13},{2,16},{3,15},{4,22},{5,1},{6,20},{7,3},{8,26},{9,5}... | collective-permute-start | bytes 614408 | tf_op jit(solution)/shard_map/ppermute | solution.py:403
  67.9 7.9 %collective-permute-start.13 = (bf16[800,128]{1,0:T(8,128)(2,1)S(1)}, bf16[800,128]{1,0:T(8,128)(2,1)S(1)}, u32[]{:S(2)}, u32[]{:S(2)}) collective-permute-start(bf16[800,128]{1,0:T(8,128)(2,1)S(1)} %reduce-precision_convert_fusion.refs_0_), channel_id=1, source_target_pairs={{0,12},{1,97},{2,14},{3,99},{4,0},{5,101},{6,2},{7,103},{8,4},{9,1... | collective-permute-start | bytes 614408 | tf_op jit(solution)/shard_map/ppermute | solution.py:403
  71.0 6.2 %collective-permute-start.14 = (bf16[800,128]{1,0:T(8,128)(2,1)S(1)}, bf16[800,128]{1,0:T(8,128)(2,1)S(1)}, u32[]{:S(2)}, u32[]{:S(2)}) collective-permute-start(bf16[800,128]{1,0:T(8,128)(2,1)S(1)} %reduce-precision_convert_fusion.refs_0_), channel_id=1, source_target_pairs={{0,8},{1,65},{2,10},{3,67},{4,12},{5,69},{6,14},{7,71},{8,0},{9,73... | collective-permute-start | bytes 614408 | tf_op jit(solution)/shard_map/ppermute | solution.py:401
  71.1 8.3 %collective-permute-start.15 = (bf16[800,128]{1,0:T(8,128)(2,1)S(1)}, bf16[800,128]{1,0:T(8,128)(2,1)S(1)}, u32[]{:S(2)}, u32[]{:S(2)}) collective-permute-start(bf16[800,128]{1,0:T(8,128)(2,1)S(1)} %reduce-precision_convert_fusion.refs_0_), channel_id=1, source_target_pairs={{0,4},{1,33},{2,6},{3,35},{4,8},{5,37},{6,10},{7,39},{8,12},{9,41}... | collective-permute-start | bytes 614408 | tf_op jit(solution)/shard_map/ppermute | solution.py:402
  79.5 6.6 %collective-permute-start.16 = (bf16[4,800,128]{2,1,0:T(8,128)(2,1)S(1)}, bf16[4,800,128]{2,1,0:T(8,128)(2,1)S(1)}, u32[]{:S(2)}, u32[]{:S(2)}) collective-permute-start(bf16[4,800,128]{2,1,0:T(8,128)(2,1)S(1)} %pad_maximum_fusion), channel_id=1, source_target_pairs={{0,1},{1,0},{2,3},{3,2},{4,5},{5,4},{6,7},{7,6},{8,9},{9,8},{10,11... | collective-permute-start | bytes 2457608 | tf_op jit(solution)/shard_map/ppermute | solution.py:397

commit v3 on v2

--- a/solution.py
+++ b/solution.py
@@ -57,9 +57,7 @@
         copy.wait()
 
 
-def second_kernel(lat, w1, w2, ker, _, act, slope, ft, taps, w1t, w2t):
-    n_px = act.shape[0]
-    project(lat[n_px : 2 * n_px], w1, w2, act, slope, ft)
+def turn(w1, w2, ker, taps, w1t, w2t):
     w1t[...] = w1[...].T
     w2t[...] = w2[...].T
     for t in range(6):
@@ -96,19 +94,6 @@
     )(*in_hbm(latent, w1, w2, kernel.reshape(18, 128, 128), cotangent))
 
 
-def second(lat, w1, w2, ker, after):
-    n = lat.shape[0]
-    shapes = frame_shapes(n // 2) + [(6, 512, 256), (512, 512), (512, 512)]
-    return pl.pallas_call(
-        second_kernel,
-        in_specs=[VMEM_SPEC] * 4 + [ANY_SPEC],
-        out_specs=[VMEM_SPEC] * len(shapes),
-        out_shape=[pltpu.VMEM(shape, BF) for shape in shapes],
-        cost_estimate=pl.CostEstimate(flops=4 * n * 512 * 512, bytes_accessed=8 * MIB, transcendentals=n * 256),
-        compiler_params=pltpu.CompilerParams(vmem_limit_bytes=16 * MIB),
-    )(*in_vmem(lat, w1, w2, ker, after))
-
-
 def border_kernel(first, second, _, __, cot_a, cot_b):
     odd = lax.axis_index("ha") % 2
     for upper, lower, here in ((second, first, odd == 0), (first, second, odd == 1)):
@@ -143,16 +128,12 @@
 
 def split_all(cells, planes, spread):
     zero = jnp.zeros((8, 128), F32)
-    for s in range(2):
+    for s in range(spread.shape[0]):
         spread[s, 0:8, :] = zero
         spread[s, 264:272, :] = zero
 
-    def body(r, carry):
-        for s in range(2):
-            split(cells, planes, spread, 2 * r + s, s)
-        return carry
-
-    lax.fori_loop(0, ROWS // 2 + 1, body, 0)
+    for row in range(ROWS + 2):
+        split(cells, planes, spread, row, row % spread.shape[0])
 
 
 def conv(taps, dt, planes, y):
@@ -177,7 +158,7 @@
 
 
 def rows_of(k, count):
-    return pl.ds(pl.multiple_of(k * count, count), count)
+    return slice(k * count, (k + 1) * count)
 
 
 def add_taps(gk, ft, dt, planes, before):
@@ -193,42 +174,35 @@
 
 def add_weights(gw, pairs, before):
     for n, (left, right) in enumerate(pairs):
-        for m in range(2):
-            part = lax.dot_general(
-                left[:, 256 * m : 256 * (m + 1)], right[...], (((0,), (0,)), ((), ())), preferred_element_type=F32
-            )
-            where = slice(512 * n + 256 * m, 512 * n + 256 * (m + 1))
-            gw[where] = part if before is None else before[where] + part
-
-
-def early_kernel(lat, act, slope, ft_a, ft_b, taps, w1t, w2t, cot_a, cot_b, gl_h, part, gk, gw, *scratch):
-    planes_a, planes_b, spread, gm, gp, gl, sem = scratch
+        part = lax.dot_general(left[...], right[...], (((0,), (0,)), ((), ())), preferred_element_type=F32)
+        where = slice(512 * n, 512 * (n + 1))
+        gw[where] = part if before is None else before[where] + part
+
+
+def early_kernel(lat, w1, w2, ker, act, slope, ft_a, cot_a, cot_b, *refs):
+    gl_h, part, gk, gw, act_b, slope_b, ft_b, taps, w1t, w2t = refs[:10]
+    planes_a, planes_b, spread, gm, gp, gl, sem = refs[10:]
     n_px = gm.shape[0]
     mine = pl.ds(0, n_px)
+    turn(w1, w2, ker, taps, w1t, w2t)
     split_all(cot_a, planes_a, spread)
+    add_taps(gk, ft_a, 1, planes_a, None)
     split_all(cot_b, planes_b, spread)
-
-    def back(k, carry):
+    for k in range(ROWS // STEP):
         y = k * STEP
         total = own_cells(planes_a, y) + conv(taps, 1, planes_a, y) + conv(taps, 0, planes_b, y)
         gm[rows_of(k, STEP * 64)] = analyze(total)
-        return carry
-
-    def ahead(k, carry):
+    for k in range(ROWS // STEP):
         y = k * STEP
         part[rows_of(k, STEP * 128)] = own_cells(planes_b, y) + conv(taps, 1, planes_b, y)
-        return carry
-
-    lax.fori_loop(0, ROWS // STEP, back, 0)
-    lax.fori_loop(0, ROWS // STEP, ahead, 0)
     gp[...] = (dot(gm[...], w2t[...]) * slope[...].astype(F32)).astype(BF)
     gl[...] = (gm[...].astype(F32) + dot(gp[...], w1t[...])).astype(BF)
     out = pltpu.make_async_copy(gl, gl_h.at[mine], sem)
     out.start()
-    add_taps(gk, ft_a, 1, planes_a, None)
+    add_weights(gw, ((lat.at[mine], gp), (act, gm)), None)
+    project(lat[n_px : 2 * n_px], w1, w2, act_b, slope_b, ft_b)
     add_taps(gk, ft_a, 0, planes_b, None)
     add_taps(gk, ft_b, 1, planes_b, gk)
-    add_weights(gw, ((lat.at[mine], gp), (act, gm)), None)
     out.wait()
 
 
@@ -238,12 +212,9 @@
     mine = pl.ds(n_px, n_px)
     split_all(cells, planes, spread)
 
-    def back(k, carry):
+    for k in range(ROWS // STEP):
         total = part[rows_of(k, STEP * 128)] + conv(taps, 0, planes, k * STEP)
         gm[rows_of(k, STEP * 64)] = analyze(total)
-        return carry
-
-    lax.fori_loop(0, ROWS // STEP, back, 0)
     gp[...] = (dot(gm[...], w2t[...]) * slope[...].astype(F32)).astype(BF)
     gk[128 * 9 :] = sumk[128 * 9 :]
     add_taps(gk, ft, 0, planes, sumk)
@@ -274,18 +245,19 @@
 
 def early(lat, *rest):
     n_px = lat.shape[0] // 2
-    sums = [pltpu.VMEM(shape, F32) for shape in SUMS]
     ops = in_vmem(lat, *rest)
+    shapes = [pltpu.VMEM(shape, F32) for shape in [(ROWS * 128, 256)] + SUMS]
+    shapes += [pltpu.VMEM(shape, BF) for shape in frame_shapes(n_px) + [(6, 512, 256), (512, 512), (512, 512)]]
     return pl.pallas_call(
         early_kernel,
         in_specs=[VMEM_SPEC] * len(ops),
-        out_specs=[ANY_SPEC] + [VMEM_SPEC] * 3,
-        out_shape=[pltpu.HBM(lat.shape, BF), pltpu.VMEM((ROWS * 128, 256), F32)] + sums,
+        out_specs=[ANY_SPEC] + [VMEM_SPEC] * len(shapes),
+        out_shape=[pltpu.HBM(lat.shape, BF)] + shapes,
         scratch_shapes=[pltpu.VMEM(PLANES, BF)] * 2
         + [pltpu.VMEM(SPREAD, F32)]
         + [pltpu.VMEM((n_px, 512), BF)] * 3
         + [pltpu.SemaphoreType.DMA],
-        cost_estimate=pl.CostEstimate(flops=10 << 30, bytes_accessed=16 * MIB, transcendentals=0),
+        cost_estimate=pl.CostEstimate(flops=12 << 30, bytes_accessed=16 * MIB, transcendentals=0),
         compiler_params=pltpu.CompilerParams(vmem_limit_bytes=24 * MIB),
     )(*ops)
 
@@ -460,8 +432,8 @@
     lat, w1, w2, ker, cot_a, cot_b, act_a, slope_a, ft_a = first(flat, w_first, w_second, kernel, cotangent)
     cot_a, cot_b = border(inner, outer, cot_a, cot_b)
     later = neighbour(cot_a, "ta", -1)
-    act_b, slope_b, ft_b, taps, w1t, w2t = second(lat, w1, w2, ker, cot_b)
-    grad, part, gk, gw = early(lat, act_a, slope_a, ft_a, ft_b, taps, w1t, w2t, cot_a, cot_b)
+    middle = early(lat, w1, w2, ker, act_a, slope_a, ft_a, cot_a, cot_b)
+    grad, part, gk, gw, act_b, slope_b, ft_b, taps, w1t, w2t = middle
     gm, gp, keep, send = late(lat, act_b, slope_b, ft_b, taps, w2t, later, part, gk, gw)
     got = swap(send)
     grad = last(gm, gp, w1t, grad)

time: 87.8 us -> 86.5 us (0.985)
  Pallas kernels: 30.3 us -> 28 us
  waiting for transfers between devices: 19.3 us -> 21.2 us
    pallas_call x1 -> x0, Pallas kernels: 2.02 us -> none  [second(): pl.pallas_call(second_kernel, in_specs=[VMEM_SPEC] * 4 + [ANY_SPEC], out_...]
    ppermute x1, waiting for transfers between devices: 0.01 us -> 1.55 us  [neighbour(): lax.ppermute(value, axis, [(i, i + step) for i in range(count) if 0 <= i...]
  transfers between devices with their start and end apart: 17 -> 17, of which waited for: 12 -> 13; matrix products, arithmetic and copies ran while one was open for 0% -> 0% of each run, Pallas kernels for 26% -> 24%
where the time goes in v3:
time: 86.5 us; the launch traced here: 86.3 us
  starting transfers between devices  34.6 us (40%)
  Pallas kernels  28 us (32%)
  waiting for transfers between devices  21.2 us (25%)
  other arithmetic  1.64 us (2%)
  between operations  0.95 us (1%)
    pallas_call x1, Pallas kernels, early(): pl.pallas_call(early_kernel, in_specs=[VMEM_SPEC] * len(ops), out_specs=[...  14.5 us
    ppermute x4, starting transfers between devices, trade(): across = lax.ppermute(far, BOTH, along(axes, step_by(2)))  12.5 us
    ppermute x4, waiting for transfers between devices, trade(): before = lax.ppermute(near, BOTH, along(axes, step_by(1)))  10.3 us
    ppermute x4, starting transfers between devices, trade(): after = lax.ppermute(last, BOTH, along(axes, step_by(3)))  9.16 us
    pallas_call x1, Pallas kernels, late(): pl.pallas_call(late_kernel, in_specs=[VMEM_SPEC] * len(ops), out_specs=[V...  5.81 us
    ppermute x2, starting transfers between devices, swap(): return lax.ppermute(value, BOTH, [(i, i ^ 1) for i in range(128)])  4.74 us
    ppermute x4, waiting for transfers between devices, trade(): after = lax.ppermute(last, BOTH, along(axes, step_by(3)))  4.42 us
    ppermute x4, waiting for transfers between devices, trade(): across = lax.ppermute(far, BOTH, along(axes, step_by(2)))  3.58 us
  transfers between devices with their start and end apart: 17, of which 13 were waited for; matrix products, arithmetic and copies ran while one was open for 0% of the time, Pallas kernels for 24%

profile of v3, /device:TPU:1, one launch (start us, length us, event | category | flops | bytes accessed | tf_op | source)
XLA Modules:
  0.0 86.3 jit_solution(10327933609454674201)
XLA Ops:
  0.6 1.0 %fusion.8 = (bf16[2,256,128]{2,1,0:T(8,128)(2,1)S(1)}, bf16[2,256,128]{2,1,0:T(8,128)(2,1)S(1)}) fusion(pred[]{:T(512)S(6)} %eq.6, bf16[2,16,256,128]{3,2,1,0:T(8,128)(2,1)} %cot_h.1), kind=kLoop, calls=%fused_computation.18 | loop fusion | flops 131072 | bytes 524289 | tf_op jit(solution)/shard_map/jit(_where)/select_n | solution.py:431
  1.6 2.1 %collective-permute-start = (bf16[2,256,128]{2,1,0:T(8,128)(2,1)S(1)}, bf16[2,256,128]{2,1,0:T(8,128)(2,1)S(1)}, u32[]{:S(2)}, u32[]{:S(2)}) collective-permute-start(bf16[2,256,128]{2,1,0:T(8,128)(2,1)S(1)} %get-tuple-element.71), channel_id=1, source_target_pairs={{0,16},{16,0},{32,48},{48,32},{64,80},{80,64},{96,112},{112,96},{1... | collective-permute-start | bytes 393224 | tf_op jit(solution)/shard_map/ppermute | solution.py:430
  3.8 0.7 collective-permute-start.1
  4.4 3.4 %shard_map.84 = (bf16[2048,512]{1,0:T(8,128)(2,1)S(1)}, bf16[512,512]{1,0:T(8,128)(2,1)S(1)}, bf16[512,512]{1,0:T(8,128)(2,1)S(1)}, bf16[18,128,128]{2,1,0:T(8,1...) custom-call(bf16[2048,512]{1,0:T(8,128)(2,1)} %bitcast.39, ...), custom_call_target="tpu_custom_call" | custom-call | flops 2147483648 | bytes 8388608 | tf_op jit(solution)/shard_map/pallas_call | solution.py:86
  7.9 3.0 %collective-permute-start.2 = (bf16[18,256,128]{2,1,0:T(8,128)(2,1)S(1)}, bf16[18,256,128]{2,1,0:T(8,128)(2,1)S(1)}, u32[]{:S(2)}, u32[]{:S(2)}) collective-permute-start(bf16[18,256,128]{2,1,0:T(8,128)(2,1)S(1)} %get-tuple-element.46.cot_a), channel_id=1, source_target_pairs={{1,0},{2,1},{3,2},{4,3},{5,4},{6,5},{7,6},{8,7},{9,8},{10,9},{11,1... | collective-permute-start | bytes 3538952 | tf_op jit(solution)/shard_map/ppermute | solution.py:415
  11.0 14.5 %shard_map.86 = (bf16[2048,512]{1,0:T(8,128)(2,1)}, f32[2048,256]{1,0:T(8,128)S(1)}, f32[2304,128]{1,0:T(8,128)S(1)}, f32[1024,512]{1,0:T(8,128)S(1)}, bf16[1024...) custom-call(bf16[2048,512]{1,0:T(8,128)(2,1)S(1)} %get-tuple-element, ...), custom_call_target="tpu_custom_call" | custom-call | flops 12884901888 | bytes 16777216 | tf_op jit(solution)/shard_map/pallas_call | solution.py:251
  25.5 1.5 %collective-permute-done.2.cells = bf16[18,256,128]{2,1,0:T(8,128)(2,1)S(1)} collective-permute-done((bf16[18,256,128]{2,1,0:T(8,128)(2,1)S(1)}, bf16[18,256,128]{2,1,0:T(8,128)(2,1)S(1)}, u32[]{:S(2)}, u32[]{:S(2)}) %collective-permute-start.2) | collective-permute-done | bytes 1179680 | tf_op jit(solution)/shard_map/ppermute | solution.py:415
  27.0 5.8 %shard_map.87 = (bf16[1024,512]{1,0:T(8,128)(2,1)S(1)}, bf16[1024,512]{1,0:T(8,128)(2,1)S(1)}, bf16[4,800,128]{2,1,0:T(8,128)(2,1)S(1)}, bf16[4,800,128]{2,1,0:T(8,128)(2,1)S(1)}) custom-call(bf16[2048,512]{1,0:T(8,128)(2,1)S(1)} %get-tuple-element.37.lat, bf16[1024,512]{1,0:T(8,128)(2,1)S(1)} %get-tuple-element.48.act, ...), custom_call_target="tpu_custom_call" | custom-call | flops 6442450944 | bytes 16777216 | tf_op jit(solution)/shard_map/pallas_call | solution.py:268
  32.9 1.7 %shard_map.88 = bf16[2048,512]{1,0:T(8,128)(2,1)} custom-call(bf16[1024,512]{1,0:T(8,128)(2,1)S(1)} %get-tuple-element.57.gm, bf16[1024,512]{1,0:T(8,128)(2,1)S(1)} %get-tuple-element.58.gp, bf16[512,512]{1,0:T(8,128)(2,1)S(1)} %get-tuple-element.59.w1t, bf16[2048,512]{1,0:T(8,128)(2,1)} %get-tuple-element.60._), custom_call_target="tpu_custom_call", output_to_operand_aliasing={{}: (3, {})} | custom-call | flops 536870912 | bytes 4194304 | tf_op jit(solution)/shard_map/pallas_call | solution.py:281
  34.6 0.6 collective-permute-done.3
  35.4 6.6 %collective-permute-start.4 = (bf16[800,128]{1,0:T(8,128)(2,1)S(1)}, bf16[800,128]{1,0:T(8,128)(2,1)S(1)}, u32[]{:S(2)}, u32[]{:S(2)}) collective-permute-start(bf16[800,128]{1,0:T(8,128)(2,1)S(1)} %get-tuple-element.72), channel_id=1, source_target_pairs={{0,8},{1,65},{2,10},{3,67},{4,12},{5,69},{6,14},{7,71},{8,0},{9,73... | collective-permute-start | bytes 614408 | tf_op jit(solution)/shard_map/ppermute | solution.py:373
  42.4 2.3 %collective-permute-start.6 = (bf16[800,128]{1,0:T(8,128)(2,1)S(1)}, bf16[800,128]{1,0:T(8,128)(2,1)S(1)}, u32[]{:S(2)}, u32[]{:S(2)}) collective-permute-start(bf16[800,128]{1,0:T(8,128)(2,1)S(1)} %get-tuple-element.73), channel_id=1, source_target_pairs={{0,12},{1,97},{2,14},{3,99},{4,0},{5,101},{6,2},{7,103},{8,4},{9,1... | collective-permute-start | bytes 614408 | tf_op jit(solution)/shard_map/ppermute | solution.py:375
  44.7 0.5 collective-permute-done.4
  45.1 2.7 %collective-permute-done.5 = bf16[800,128]{1,0:T(8,128)(2,1)S(1)} collective-permute-done((bf16[800,128]{1,0:T(8,128)(2,1)S(1)}, bf16[800,128]{1,0:T(8,128)(2,1)S(1)}, u32[]{:S(2)}, u32[]{:S(2)}) %collective-permute-start.5) | collective-permute-done | bytes 204832 | tf_op jit(solution)/shard_map/ppermute | solution.py:374
  48.0 2.2 %collective-permute-start.7 = (bf16[800,128]{1,0:T(8,128)(2,1)S(1)}, bf16[800,128]{1,0:T(8,128)(2,1)S(1)}, u32[]{:S(2)}, u32[]{:S(2)}) collective-permute-start(bf16[800,128]{1,0:T(8,128)(2,1)S(1)} %fusion.2), channel_id=1, source_target_pairs={{0,64},{1,3},{2,66},{3,1},{4,68},{5,7},{6,70},{7,5},{8,72},{9,11},... | collective-permute-start | bytes 614408 | tf_op jit(solution)/shard_map/ppermute | solution.py:373
  50.2 1.0 %collective-permute-start.8 = (bf16[800,128]{1,0:T(8,128)(2,1)S(1)}, bf16[800,128]{1,0:T(8,128)(2,1)S(1)}, u32[]{:S(2)}, u32[]{:S(2)}) collective-permute-start(bf16[800,128]{1,0:T(8,128)(2,1)S(1)} %fusion.2), channel_id=1, source_target_pairs={{0,32},{1,17},{2,34},{3,19},{4,36},{5,21},{6,38},{7,23},{8,40},{9,... | collective-permute-start | bytes 614408 | tf_op jit(solution)/shard_map/ppermute | solution.py:374
  51.2 1.7 %collective-permute-start.9 = (bf16[800,128]{1,0:T(8,128)(2,1)S(1)}, bf16[800,128]{1,0:T(8,128)(2,1)S(1)}, u32[]{:S(2)}, u32[]{:S(2)}) collective-permute-start(bf16[800,128]{1,0:T(8,128)(2,1)S(1)} %fusion.2), channel_id=1, source_target_pairs={{0,96},{1,19},{2,98},{3,17},{4,100},{5,23},{6,102},{7,21},{8,104},... | collective-permute-start | bytes 614408 | tf_op jit(solution)/shard_map/ppermute | solution.py:375
  52.9 1.3 %collective-permute-done.7 = bf16[800,128]{1,0:T(8,128)(2,1)S(1)} collective-permute-done((bf16[800,128]{1,0:T(8,128)(2,1)S(1)}, bf16[800,128]{1,0:T(8,128)(2,1)S(1)}, u32[]{:S(2)}, u32[]{:S(2)}) %collective-permute-start.7) | collective-permute-done | bytes 204832 | tf_op jit(solution)/shard_map/ppermute | solution.py:373
  54.2 2.5 %collective-permute-done.8 = bf16[800,128]{1,0:T(8,128)(2,1)S(1)} collective-permute-done((bf16[800,128]{1,0:T(8,128)(2,1)S(1)}, bf16[800,128]{1,0:T(8,128)(2,1)S(1)}, u32[]{:S(2)}, u32[]{:S(2)}) %collective-permute-start.8) | collective-permute-done | bytes 204832 | tf_op jit(solution)/shard_map/ppermute | solution.py:374
  57.0 3.5 %collective-permute-start.10 = (bf16[800,128]{1,0:T(8,128)(2,1)S(1)}, bf16[800,128]{1,0:T(8,128)(2,1)S(1)}, u32[]{:S(2)}, u32[]{:S(2)}) collective-permute-start(bf16[800,128]{1,0:T(8,128)(2,1)S(1)} %reduce-precision_convert_fusion.1), channel_id=1, source_target_pairs={{0,2},{1,9},{2,0},{3,11},{4,6},{5,13},{6,4},{7,15},{8,10},{9,1},{1... | collective-permute-start | bytes 614408 | tf_op jit(solution)/shard_map/ppermute | solution.py:373
  60.9 2.2 %collective-permute-start.12 = (bf16[800,128]{1,0:T(8,128)(2,1)S(1)}, bf16[800,128]{1,0:T(8,128)(2,1)S(1)}, u32[]{:S(2)}, u32[]{:S(2)}) collective-permute-start(bf16[800,128]{1,0:T(8,128)(2,1)S(1)} %reduce-precision_convert_fusion.1), channel_id=1, source_target_pairs={{0,18},{1,13},{2,16},{3,15},{4,22},{5,1},{6,20},{7,3},{8,26},{9,5}... | collective-permute-start | bytes 614408 | tf_op jit(solution)/shard_map/ppermute | solution.py:375
  63.1 0.5 collective-permute-done.10
  63.6 3.0 %collective-permute-done.11 = bf16[800,128]{1,0:T(8,128)(2,1)S(1)} collective-permute-done((bf16[800,128]{1,0:T(8,128)(2,1)S(1)}, bf16[800,128]{1,0:T(8,128)(2,1)S(1)}, u32[]{:S(2)}, u32[]{:S(2)}) %collective-permute-start.11) | collective-permute-done | bytes 204832 | tf_op jit(solution)/shard_map/ppermute | solution.py:374
  66.7 3.0 %collective-permute-start.13 = (bf16[800,128]{1,0:T(8,128)(2,1)S(1)}, bf16[800,128]{1,0:T(8,128)(2,1)S(1)}, u32[]{:S(2)}, u32[]{:S(2)}) collective-permute-start(bf16[800,128]{1,0:T(8,128)(2,1)S(1)} %reduce-precision_convert_fusion.refs_0_), channel_id=1, source_target_pairs={{0,12},{1,97},{2,14},{3,99},{4,0},{5,101},{6,2},{7,103},{8,4},{9,1... | collective-permute-start | bytes 614408 | tf_op jit(solution)/shard_map/ppermute | solution.py:375
  69.8 0.5 collective-permute-start.15
  70.4 4.2 %collective-permute-done.13.refs_1_ = bf16[800,128]{1,0:T(8,128)(2,1)S(1)} collective-permute-done((bf16[800,128]{1,0:T(8,128)(2,1)S(1)}, bf16[800,128]{1,0:T(8,128)(2,1)S(1)}, u32[]{:S(2)}, u32[]{:S(2)}) %collective-permute-start.13) | collective-permute-done | bytes 204832 | tf_op jit(solution)/shard_map/ppermute | solution.py:375
  74.6 1.3 %collective-permute-done.14.refs_2_ = bf16[800,128]{1,0:T(8,128)(2,1)S(1)} collective-permute-done((bf16[800,128]{1,0:T(8,128)(2,1)S(1)}, bf16[800,128]{1,0:T(8,128)(2,1)S(1)}, u32[]{:S(2)}, u32[]{:S(2)}) %collective-permute-start.14) | collective-permute-done | bytes 204832 | tf_op jit(solution)/shard_map/ppermute | solution.py:373
  75.9 2.2 %collective-permute-done.15.refs_3_ = bf16[800,128]{1,0:T(8,128)(2,1)S(1)} collective-permute-done((bf16[800,128]{1,0:T(8,128)(2,1)S(1)}, bf16[800,128]{1,0:T(8,128)(2,1)S(1)}, u32[]{:S(2)}, u32[]{:S(2)}) %collective-permute-start.15) | collective-permute-done | bytes 204832 | tf_op jit(solution)/shard_map/ppermute | solution.py:374
  78.2 4.7 %collective-permute-start.16 = (bf16[4,800,128]{2,1,0:T(8,128)(2,1)S(1)}, bf16[4,800,128]{2,1,0:T(8,128)(2,1)S(1)}, u32[]{:S(2)}, u32[]{:S(2)}) collective-permute-start(bf16[4,800,128]{2,1,0:T(8,128)(2,1)S(1)} %pad_maximum_fusion), channel_id=1, source_target_pairs={{0,1},{1,0},{2,3},{3,2},{4,5},{5,4},{6,7},{7,6},{8,9},{9,8},{10,11... | collective-permute-start | bytes 2457608 | tf_op jit(solution)/shard_map/ppermute | solution.py:369
  82.9 1.3 %shard_map.89 = (f32[512,512]{1,0:T(8,128)}, f32[512,512]{1,0:T(8,128)}, f32[2304,128]{1,0:T(8,128)}) custom-call(bf16[800,128]{1,0:T(8,128)(2,1)S(1)} %reduce-precision_convert_fusion.refs_0_, bf16[800,128]{1,0:T(8,128)(2,1)S(1)} %collective-permute-done.13.refs_1_, bf16[800,128]{1,0:T(8,128)(2,1)S(1)} %collective-permute-done.14.refs_2_, ...), custom_call_target="tpu_custom_call" | custom-call | flops 1048576 | bytes 3145728 | tf_op jit(solution)/shard_map/pallas_call | solution.py:322
  84.2 0.7 collective-permute-done.16.refs_0_
  84.9 1.3 %shard_map.90 = (f32[512,512]{1,0:T(8,128)}, f32[512,512]{1,0:T(8,128)}, f32[2304,128]{1,0:T(8,128)}) custom-call(bf16[4,800,128]{2,1,0:T(8,128)(2,1)S(1)} %collective-permute-done.16.refs_0_, f32[512,512]{1,0:T(8,128)} %get-tuple-element.64.refs_1_, ...), custom_call_target="tpu_custom_call", output_to_operand_aliasing={{0}: (1, {}), {1}: (2, {}), {2}: (3, {})} | custom-call | flops 1048576 | bytes 3145728 | tf_op jit(solution)/shard_map/pallas_call | solution.py:322
  (15 shorter events, 1.9 us)
Async XLA Ops:
  1.6 6.2 %collective-permute-start = (bf16[2,256,128]{2,1,0:T(8,128)(2,1)S(1)}, bf16[2,256,128]{2,1,0:T(8,128)(2,1)S(1)}, u32[]{:S(2)}, u32[]{:S(2)}) collective-permute-start(bf16[2,256,128]{2,1,0:T(8,128)(2,1)S(1)} %get-tuple-element.71), channel_id=1, source_target_pairs={{0,16},{16,0},{32,48},{48,32},{64,80},{80,64},{96,112},{112,96},{1... | collective-permute-start | bytes 393224 | tf_op jit(solution)/shard_map/ppermute | solution.py:430
  3.8 4.1 %collective-permute-start.1 = (bf16[2,256,128]{2,1,0:T(8,128)(2,1)S(1)}, bf16[2,256,128]{2,1,0:T(8,128)(2,1)S(1)}, u32[]{:S(2)}, u32[]{:S(2)}) collective-permute-start(bf16[2,256,128]{2,1,0:T(8,128)(2,1)S(1)} %get-tuple-element.70), channel_id=1, source_target_pairs={{16,32},{32,16},{48,64},{64,48},{80,96},{96,80},{17,33},{33,17},{4... | collective-permute-start | bytes 393224 | tf_op jit(solution)/shard_map/ppermute | solution.py:431
  7.9 19.1 %collective-permute-start.2 = (bf16[18,256,128]{2,1,0:T(8,128)(2,1)S(1)}, bf16[18,256,128]{2,1,0:T(8,128)(2,1)S(1)}, u32[]{:S(2)}, u32[]{:S(2)}) collective-permute-start(bf16[18,256,128]{2,1,0:T(8,128)(2,1)S(1)} %get-tuple-element.46.cot_a), channel_id=1, source_target_pairs={{1,0},{2,1},{3,2},{4,3},{5,4},{6,5},{7,6},{8,7},{9,8},{10,9},{11,1... | collective-permute-start | bytes 3538952 | tf_op jit(solution)/shard_map/ppermute | solution.py:415
  32.8 2.4 %collective-permute-start.3 = (bf16[4,800,128]{2,1,0:T(8,128)(2,1)S(1)}, bf16[4,800,128]{2,1,0:T(8,128)(2,1)S(1)}, u32[]{:S(2)}, u32[]{:S(2)}) collective-permute-start(bf16[4,800,128]{2,1,0:T(8,128)(2,1)S(1)} %get-tuple-element.56), channel_id=1, source_target_pairs={{0,1},{1,0},{2,3},{3,2},{4,5},{5,4},{6,7},{7,6},{8,9},{9,8},{10,11... | collective-permute-start | bytes 2457608 | tf_op jit(solution)/shard_map/ppermute | solution.py:369
  35.4 9.8 %collective-permute-start.4 = (bf16[800,128]{1,0:T(8,128)(2,1)S(1)}, bf16[800,128]{1,0:T(8,128)(2,1)S(1)}, u32[]{:S(2)}, u32[]{:S(2)}) collective-permute-start(bf16[800,128]{1,0:T(8,128)(2,1)S(1)} %get-tuple-element.72), channel_id=1, source_target_pairs={{0,8},{1,65},{2,10},{3,67},{4,12},{5,69},{6,14},{7,71},{8,0},{9,73... | collective-permute-start | bytes 614408 | tf_op jit(solution)/shard_map/ppermute | solution.py:373
  42.0 5.8 %collective-permute-start.5 = (bf16[800,128]{1,0:T(8,128)(2,1)S(1)}, bf16[800,128]{1,0:T(8,128)(2,1)S(1)}, u32[]{:S(2)}, u32[]{:S(2)}) collective-permute-start(bf16[800,128]{1,0:T(8,128)(2,1)S(1)} %get-tuple-element.74), channel_id=1, source_target_pairs={{0,4},{1,33},{2,6},{3,35},{4,8},{5,37},{6,10},{7,39},{8,12},{9,41}... | collective-permute-start | bytes 614408 | tf_op jit(solution)/shard_map/ppermute | solution.py:374
  42.4 5.4 %collective-permute-start.6 = (bf16[800,128]{1,0:T(8,128)(2,1)S(1)}, bf16[800,128]{1,0:T(8,128)(2,1)S(1)}, u32[]{:S(2)}, u32[]{:S(2)}) collective-permute-start(bf16[800,128]{1,0:T(8,128)(2,1)S(1)} %get-tuple-element.73), channel_id=1, source_target_pairs={{0,12},{1,97},{2,14},{3,99},{4,0},{5,101},{6,2},{7,103},{8,4},{9,1... | collective-permute-start | bytes 614408 | tf_op jit(solution)/shard_map/ppermute | solution.py:375
  48.0 6.2 %collective-permute-start.7 = (bf16[800,128]{1,0:T(8,128)(2,1)S(1)}, bf16[800,128]{1,0:T(8,128)(2,1)S(1)}, u32[]{:S(2)}, u32[]{:S(2)}) collective-permute-start(bf16[800,128]{1,0:T(8,128)(2,1)S(1)} %fusion.2), channel_id=1, source_target_pairs={{0,64},{1,3},{2,66},{3,1},{4,68},{5,7},{6,70},{7,5},{8,72},{9,11},... | collective-permute-start | bytes 614408 | tf_op jit(solution)/shard_map/ppermute | solution.py:373
  50.2 6.5 %collective-permute-start.8 = (bf16[800,128]{1,0:T(8,128)(2,1)S(1)}, bf16[800,128]{1,0:T(8,128)(2,1)S(1)}, u32[]{:S(2)}, u32[]{:S(2)}) collective-permute-start(bf16[800,128]{1,0:T(8,128)(2,1)S(1)} %fusion.2), channel_id=1, source_target_pairs={{0,32},{1,17},{2,34},{3,19},{4,36},{5,21},{6,38},{7,23},{8,40},{9,... | collective-permute-start | bytes 614408 | tf_op jit(solution)/shard_map/ppermute | solution.py:374
  51.2 5.6 %collective-permute-start.9 = (bf16[800,128]{1,0:T(8,128)(2,1)S(1)}, bf16[800,128]{1,0:T(8,128)(2,1)S(1)}, u32[]{:S(2)}, u32[]{:S(2)}) collective-permute-start(bf16[800,128]{1,0:T(8,128)(2,1)S(1)} %fusion.2), channel_id=1, source_target_pairs={{0,96},{1,19},{2,98},{3,17},{4,100},{5,23},{6,102},{7,21},{8,104},... | collective-permute-start | bytes 614408 | tf_op jit(solution)/shard_map/ppermute | solution.py:375
  57.0 6.6 %collective-permute-start.10 = (bf16[800,128]{1,0:T(8,128)(2,1)S(1)}, bf16[800,128]{1,0:T(8,128)(2,1)S(1)}, u32[]{:S(2)}, u32[]{:S(2)}) collective-permute-start(bf16[800,128]{1,0:T(8,128)(2,1)S(1)} %reduce-precision_convert_fusion.1), channel_id=1, source_target_pairs={{0,2},{1,9},{2,0},{3,11},{4,6},{5,13},{6,4},{7,15},{8,10},{9,1},{1... | collective-permute-start | bytes 614408 | tf_op jit(solution)/shard_map/ppermute | solution.py:373
  60.5 6.1 %collective-permute-start.11 = (bf16[800,128]{1,0:T(8,128)(2,1)S(1)}, bf16[800,128]{1,0:T(8,128)(2,1)S(1)}, u32[]{:S(2)}, u32[]{:S(2)}) collective-permute-start(bf16[800,128]{1,0:T(8,128)(2,1)S(1)} %reduce-precision_convert_fusion.1), channel_id=1, source_target_pairs={{0,16},{1,5},{2,18},{3,7},{4,20},{5,9},{6,22},{7,11},{8,24},{9,13}... | collective-permute-start | bytes 614408 | tf_op jit(solution)/shard_map/ppermute | solution.py:374
  60.9 5.7 %collective-permute-start.12 = (bf16[800,128]{1,0:T(8,128)(2,1)S(1)}, bf16[800,128]{1,0:T(8,128)(2,1)S(1)}, u32[]{:S(2)}, u32[]{:S(2)}) collective-permute-start(bf16[800,128]{1,0:T(8,128)(2,1)S(1)} %reduce-precision_convert_fusion.1), channel_id=1, source_target_pairs={{0,18},{1,13},{2,16},{3,15},{4,22},{5,1},{6,20},{7,3},{8,26},{9,5}... | collective-permute-start | bytes 614408 | tf_op jit(solution)/shard_map/ppermute | solution.py:375
  66.7 7.9 %collective-permute-start.13 = (bf16[800,128]{1,0:T(8,128)(2,1)S(1)}, bf16[800,128]{1,0:T(8,128)(2,1)S(1)}, u32[]{:S(2)}, u32[]{:S(2)}) collective-permute-start(bf16[800,128]{1,0:T(8,128)(2,1)S(1)} %reduce-precision_convert_fusion.refs_0_), channel_id=1, source_target_pairs={{0,12},{1,97},{2,14},{3,99},{4,0},{5,101},{6,2},{7,103},{8,4},{9,1... | collective-permute-start | bytes 614408 | tf_op jit(solution)/shard_map/ppermute | solution.py:375
  69.7 6.2 %collective-permute-start.14 = (bf16[800,128]{1,0:T(8,128)(2,1)S(1)}, bf16[800,128]{1,0:T(8,128)(2,1)S(1)}, u32[]{:S(2)}, u32[]{:S(2)}) collective-permute-start(bf16[800,128]{1,0:T(8,128)(2,1)S(1)} %reduce-precision_convert_fusion.refs_0_), channel_id=1, source_target_pairs={{0,8},{1,65},{2,10},{3,67},{4,12},{5,69},{6,14},{7,71},{8,0},{9,73... | collective-permute-start | bytes 614408 | tf_op jit(solution)/shard_map/ppermute | solution.py:373
  69.8 8.3 %collective-permute-start.15 = (bf16[800,128]{1,0:T(8,128)(2,1)S(1)}, bf16[800,128]{1,0:T(8,128)(2,1)S(1)}, u32[]{:S(2)}, u32[]{:S(2)}) collective-permute-start(bf16[800,128]{1,0:T(8,128)(2,1)S(1)} %reduce-precision_convert_fusion.refs_0_), channel_id=1, source_target_pairs={{0,4},{1,33},{2,6},{3,35},{4,8},{5,37},{6,10},{7,39},{8,12},{9,41}... | collective-permute-start | bytes 614408 | tf_op jit(solution)/shard_map/ppermute | solution.py:374
  78.2 6.6 %collective-permute-start.16 = (bf16[4,800,128]{2,1,0:T(8,128)(2,1)S(1)}, bf16[4,800,128]{2,1,0:T(8,128)(2,1)S(1)}, u32[]{:S(2)}, u32[]{:S(2)}) collective-permute-start(bf16[4,800,128]{2,1,0:T(8,128)(2,1)S(1)} %pad_maximum_fusion), channel_id=1, source_target_pairs={{0,1},{1,0},{2,3},{3,2},{4,5},{5,4},{6,7},{7,6},{8,9},{9,8},{10,11... | collective-permute-start | bytes 2457608 | tf_op jit(solution)/shard_map/ppermute | solution.py:369

commit v4 on v3

--- a/solution.py
+++ b/solution.py
@@ -117,7 +117,7 @@
     )(*in_vmem(first, second, cot_a, cot_b))
 
 
-STEP = 8
+STEP = 4
 
 
 def split(cells, planes, spread, row, s):
@@ -216,7 +216,6 @@
         total = part[rows_of(k, STEP * 128)] + conv(taps, 0, planes, k * STEP)
         gm[rows_of(k, STEP * 64)] = analyze(total)
     gp[...] = (dot(gm[...], w2t[...]) * slope[...].astype(F32)).astype(BF)
-    gk[128 * 9 :] = sumk[128 * 9 :]
     add_taps(gk, ft, 0, planes, sumk)
     add_weights(gw, ((lat.at[mine], gp), (act, gm)), sumw)
     ids = block_ids()
@@ -227,7 +226,9 @@
             packed[128 * lane : 128 * (lane + 1), :] = gw[
                 pl.ds(pl.multiple_of(b * 128, 128), 128), 128 * lane : 128 * (lane + 1)
             ].astype(BF)
-        packed[512:800, :] = gk[pl.ds(pl.multiple_of(b * 288, 32), 288), :].astype(BF)
+        new = gk[pl.ds(pl.multiple_of((b % 4) * 288, 32), 288), :]
+        old = sumk[pl.ds(pl.multiple_of(b * 288, 32), 288), :]
+        packed[512:800, :] = jnp.where(b < 4, new, old).astype(BF)
 
 
 def last_kernel(gm, gp, w1t, _, gl_h, gl, sem):

time: 86.5 us -> 86.6 us (level)
  no operation moved by 1% of the time
where the time goes in v4:
time: 86.6 us; the launch traced here: 86.4 us
  starting transfers between devices  34.6 us (40%)
  Pallas kernels  28 us (32%)
  waiting for transfers between devices  21.3 us (25%)
  other arithmetic  1.64 us (2%)
  between operations  0.95 us (1%)
    pallas_call x1, Pallas kernels, early(): pl.pallas_call(early_kernel, in_specs=[VMEM_SPEC] * len(ops), out_specs=[...  14.4 us
    ppermute x4, starting transfers between devices, trade(): across = lax.ppermute(far, BOTH, along(axes, step_by(2)))  12.5 us
    ppermute x4, waiting for transfers between devices, trade(): before = lax.ppermute(near, BOTH, along(axes, step_by(1)))  10.3 us
    ppermute x4, starting transfers between devices, trade(): after = lax.ppermute(last, BOTH, along(axes, step_by(3)))  9.16 us
    pallas_call x1, Pallas kernels, late(): pl.pallas_call(late_kernel, in_specs=[VMEM_SPEC] * len(ops), out_specs=[V...  5.91 us
    ppermute x2, starting transfers between devices, swap(): return lax.ppermute(value, BOTH, [(i, i ^ 1) for i in range(128)])  4.75 us
    ppermute x4, waiting for transfers between devices, trade(): after = lax.ppermute(last, BOTH, along(axes, step_by(3)))  4.41 us
    ppermute x4, waiting for transfers between devices, trade(): across = lax.ppermute(far, BOTH, along(axes, step_by(2)))  3.59 us
  transfers between devices with their start and end apart: 17, of which 13 were waited for; matrix products, arithmetic and copies ran while one was open for 0% of the time, Pallas kernels for 24%

profile of v4, /device:TPU:1, one launch (start us, length us, event | category | flops | bytes accessed | tf_op | source)
XLA Modules:
  0.0 86.4 jit_solution(10578744206429040835)
XLA Ops:
  0.6 1.0 %fusion.8 = (bf16[2,256,128]{2,1,0:T(8,128)(2,1)S(1)}, bf16[2,256,128]{2,1,0:T(8,128)(2,1)S(1)}) fusion(pred[]{:T(512)S(6)} %eq.6, bf16[2,16,256,128]{3,2,1,0:T(8,128)(2,1)} %cot_h.1), kind=kLoop, calls=%fused_computation.18 | loop fusion | flops 131072 | bytes 524289 | tf_op jit(solution)/shard_map/jit(_where)/select_n | solution.py:432
  1.6 2.1 %collective-permute-start = (bf16[2,256,128]{2,1,0:T(8,128)(2,1)S(1)}, bf16[2,256,128]{2,1,0:T(8,128)(2,1)S(1)}, u32[]{:S(2)}, u32[]{:S(2)}) collective-permute-start(bf16[2,256,128]{2,1,0:T(8,128)(2,1)S(1)} %get-tuple-element.71), channel_id=1, source_target_pairs={{0,16},{16,0},{32,48},{48,32},{64,80},{80,64},{96,112},{112,96},{1... | collective-permute-start | bytes 393224 | tf_op jit(solution)/shard_map/ppermute | solution.py:431
  3.8 0.7 collective-permute-start.1
  4.4 3.4 %shard_map.84 = (bf16[2048,512]{1,0:T(8,128)(2,1)S(1)}, bf16[512,512]{1,0:T(8,128)(2,1)S(1)}, bf16[512,512]{1,0:T(8,128)(2,1)S(1)}, bf16[18,128,128]{2,1,0:T(8,1...) custom-call(bf16[2048,512]{1,0:T(8,128)(2,1)} %bitcast.39, ...), custom_call_target="tpu_custom_call" | custom-call | flops 2147483648 | bytes 8388608 | tf_op jit(solution)/shard_map/pallas_call | solution.py:86
  7.9 3.0 %collective-permute-start.2 = (bf16[18,256,128]{2,1,0:T(8,128)(2,1)S(1)}, bf16[18,256,128]{2,1,0:T(8,128)(2,1)S(1)}, u32[]{:S(2)}, u32[]{:S(2)}) collective-permute-start(bf16[18,256,128]{2,1,0:T(8,128)(2,1)S(1)} %get-tuple-element.46.cot_a), channel_id=1, source_target_pairs={{1,0},{2,1},{3,2},{4,3},{5,4},{6,5},{7,6},{8,7},{9,8},{10,9},{11,1... | collective-permute-start | bytes 3538952 | tf_op jit(solution)/shard_map/ppermute | solution.py:416
  11.0 14.4 %shard_map.86 = (bf16[2048,512]{1,0:T(8,128)(2,1)}, f32[2048,256]{1,0:T(8,128)S(1)}, f32[2304,128]{1,0:T(8,128)S(1)}, f32[1024,512]{1,0:T(8,128)S(1)}, bf16[1024...) custom-call(bf16[2048,512]{1,0:T(8,128)(2,1)S(1)} %get-tuple-element, ...), custom_call_target="tpu_custom_call" | custom-call | flops 12884901888 | bytes 16777216 | tf_op jit(solution)/shard_map/pallas_call | solution.py:252
  25.4 1.6 %collective-permute-done.2.cells = bf16[18,256,128]{2,1,0:T(8,128)(2,1)S(1)} collective-permute-done((bf16[18,256,128]{2,1,0:T(8,128)(2,1)S(1)}, bf16[18,256,128]{2,1,0:T(8,128)(2,1)S(1)}, u32[]{:S(2)}, u32[]{:S(2)}) %collective-permute-start.2) | collective-permute-done | bytes 1179680 | tf_op jit(solution)/shard_map/ppermute | solution.py:416
  27.0 5.9 %shard_map.87 = (bf16[1024,512]{1,0:T(8,128)(2,1)S(1)}, bf16[1024,512]{1,0:T(8,128)(2,1)S(1)}, bf16[4,800,128]{2,1,0:T(8,128)(2,1)S(1)}, bf16[4,800,128]{2,1,0:T(8,128)(2,1)S(1)}) custom-call(bf16[2048,512]{1,0:T(8,128)(2,1)S(1)} %get-tuple-element.37.lat, bf16[1024,512]{1,0:T(8,128)(2,1)S(1)} %get-tuple-element.48.act, ...), custom_call_target="tpu_custom_call" | custom-call | flops 6442450944 | bytes 16777216 | tf_op jit(solution)/shard_map/pallas_call | solution.py:269
  33.0 1.7 %shard_map.88 = bf16[2048,512]{1,0:T(8,128)(2,1)} custom-call(bf16[1024,512]{1,0:T(8,128)(2,1)S(1)} %get-tuple-element.57.gm, bf16[1024,512]{1,0:T(8,128)(2,1)S(1)} %get-tuple-element.58.gp, bf16[512,512]{1,0:T(8,128)(2,1)S(1)} %get-tuple-element.59.w1t, bf16[2048,512]{1,0:T(8,128)(2,1)} %get-tuple-element.60._), custom_call_target="tpu_custom_call", output_to_operand_aliasing={{}: (3, {})} | custom-call | flops 536870912 | bytes 4194304 | tf_op jit(solution)/shard_map/pallas_call | solution.py:282
  34.7 0.6 collective-permute-done.3
  35.5 6.6 %collective-permute-start.4 = (bf16[800,128]{1,0:T(8,128)(2,1)S(1)}, bf16[800,128]{1,0:T(8,128)(2,1)S(1)}, u32[]{:S(2)}, u32[]{:S(2)}) collective-permute-start(bf16[800,128]{1,0:T(8,128)(2,1)S(1)} %get-tuple-element.72), channel_id=1, source_target_pairs={{0,8},{1,65},{2,10},{3,67},{4,12},{5,69},{6,14},{7,71},{8,0},{9,73... | collective-permute-start | bytes 614408 | tf_op jit(solution)/shard_map/ppermute | solution.py:374
  42.5 2.3 %collective-permute-start.6 = (bf16[800,128]{1,0:T(8,128)(2,1)S(1)}, bf16[800,128]{1,0:T(8,128)(2,1)S(1)}, u32[]{:S(2)}, u32[]{:S(2)}) collective-permute-start(bf16[800,128]{1,0:T(8,128)(2,1)S(1)} %get-tuple-element.73), channel_id=1, source_target_pairs={{0,12},{1,97},{2,14},{3,99},{4,0},{5,101},{6,2},{7,103},{8,4},{9,1... | collective-permute-start | bytes 614408 | tf_op jit(solution)/shard_map/ppermute | solution.py:376
  44.8 0.5 collective-permute-done.4
  45.3 2.7 %collective-permute-done.5 = bf16[800,128]{1,0:T(8,128)(2,1)S(1)} collective-permute-done((bf16[800,128]{1,0:T(8,128)(2,1)S(1)}, bf16[800,128]{1,0:T(8,128)(2,1)S(1)}, u32[]{:S(2)}, u32[]{:S(2)}) %collective-permute-start.5) | collective-permute-done | bytes 204832 | tf_op jit(solution)/shard_map/ppermute | solution.py:375
  48.1 2.2 %collective-permute-start.7 = (bf16[800,128]{1,0:T(8,128)(2,1)S(1)}, bf16[800,128]{1,0:T(8,128)(2,1)S(1)}, u32[]{:S(2)}, u32[]{:S(2)}) collective-permute-start(bf16[800,128]{1,0:T(8,128)(2,1)S(1)} %fusion.2), channel_id=1, source_target_pairs={{0,64},{1,3},{2,66},{3,1},{4,68},{5,7},{6,70},{7,5},{8,72},{9,11},... | collective-permute-start | bytes 614408 | tf_op jit(solution)/shard_map/ppermute | solution.py:374
  50.3 1.0 %collective-permute-start.8 = (bf16[800,128]{1,0:T(8,128)(2,1)S(1)}, bf16[800,128]{1,0:T(8,128)(2,1)S(1)}, u32[]{:S(2)}, u32[]{:S(2)}) collective-permute-start(bf16[800,128]{1,0:T(8,128)(2,1)S(1)} %fusion.2), channel_id=1, source_target_pairs={{0,32},{1,17},{2,34},{3,19},{4,36},{5,21},{6,38},{7,23},{8,40},{9,... | collective-permute-start | bytes 614408 | tf_op jit(solution)/shard_map/ppermute | solution.py:375
  51.3 1.7 %collective-permute-start.9 = (bf16[800,128]{1,0:T(8,128)(2,1)S(1)}, bf16[800,128]{1,0:T(8,128)(2,1)S(1)}, u32[]{:S(2)}, u32[]{:S(2)}) collective-permute-start(bf16[800,128]{1,0:T(8,128)(2,1)S(1)} %fusion.2), channel_id=1, source_target_pairs={{0,96},{1,19},{2,98},{3,17},{4,100},{5,23},{6,102},{7,21},{8,104},... | collective-permute-start | bytes 614408 | tf_op jit(solution)/shard_map/ppermute | solution.py:376
  53.0 1.3 %collective-permute-done.7 = bf16[800,128]{1,0:T(8,128)(2,1)S(1)} collective-permute-done((bf16[800,128]{1,0:T(8,128)(2,1)S(1)}, bf16[800,128]{1,0:T(8,128)(2,1)S(1)}, u32[]{:S(2)}, u32[]{:S(2)}) %collective-permute-start.7) | collective-permute-done | bytes 204832 | tf_op jit(solution)/shard_map/ppermute | solution.py:374
  54.3 2.5 %collective-permute-done.8 = bf16[800,128]{1,0:T(8,128)(2,1)S(1)} collective-permute-done((bf16[800,128]{1,0:T(8,128)(2,1)S(1)}, bf16[800,128]{1,0:T(8,128)(2,1)S(1)}, u32[]{:S(2)}, u32[]{:S(2)}) %collective-permute-start.8) | collective-permute-done | bytes 204832 | tf_op jit(solution)/shard_map/ppermute | solution.py:375
  57.1 3.5 %collective-permute-start.10 = (bf16[800,128]{1,0:T(8,128)(2,1)S(1)}, bf16[800,128]{1,0:T(8,128)(2,1)S(1)}, u32[]{:S(2)}, u32[]{:S(2)}) collective-permute-start(bf16[800,128]{1,0:T(8,128)(2,1)S(1)} %reduce-precision_convert_fusion.1), channel_id=1, source_target_pairs={{0,2},{1,9},{2,0},{3,11},{4,6},{5,13},{6,4},{7,15},{8,10},{9,1},{1... | collective-permute-start | bytes 614408 | tf_op jit(solution)/shard_map/ppermute | solution.py:374
  61.0 2.2 %collective-permute-start.12 = (bf16[800,128]{1,0:T(8,128)(2,1)S(1)}, bf16[800,128]{1,0:T(8,128)(2,1)S(1)}, u32[]{:S(2)}, u32[]{:S(2)}) collective-permute-start(bf16[800,128]{1,0:T(8,128)(2,1)S(1)} %reduce-precision_convert_fusion.1), channel_id=1, source_target_pairs={{0,18},{1,13},{2,16},{3,15},{4,22},{5,1},{6,20},{7,3},{8,26},{9,5}... | collective-permute-start | bytes 614408 | tf_op jit(solution)/shard_map/ppermute | solution.py:376
  63.2 0.5 collective-permute-done.10
  63.7 3.0 %collective-permute-done.11 = bf16[800,128]{1,0:T(8,128)(2,1)S(1)} collective-permute-done((bf16[800,128]{1,0:T(8,128)(2,1)S(1)}, bf16[800,128]{1,0:T(8,128)(2,1)S(1)}, u32[]{:S(2)}, u32[]{:S(2)}) %collective-permute-start.11) | collective-permute-done | bytes 204832 | tf_op jit(solution)/shard_map/ppermute | solution.py:375
  66.8 3.0 %collective-permute-start.13 = (bf16[800,128]{1,0:T(8,128)(2,1)S(1)}, bf16[800,128]{1,0:T(8,128)(2,1)S(1)}, u32[]{:S(2)}, u32[]{:S(2)}) collective-permute-start(bf16[800,128]{1,0:T(8,128)(2,1)S(1)} %reduce-precision_convert_fusion.refs_0_), channel_id=1, source_target_pairs={{0,12},{1,97},{2,14},{3,99},{4,0},{5,101},{6,2},{7,103},{8,4},{9,1... | collective-permute-start | bytes 614408 | tf_op jit(solution)/shard_map/ppermute | solution.py:376
  69.9 0.5 collective-permute-start.15
  70.4 4.2 %collective-permute-done.13.refs_1_ = bf16[800,128]{1,0:T(8,128)(2,1)S(1)} collective-permute-done((bf16[800,128]{1,0:T(8,128)(2,1)S(1)}, bf16[800,128]{1,0:T(8,128)(2,1)S(1)}, u32[]{:S(2)}, u32[]{:S(2)}) %collective-permute-start.13) | collective-permute-done | bytes 204832 | tf_op jit(solution)/shard_map/ppermute | solution.py:376
  74.7 1.3 %collective-permute-done.14.refs_2_ = bf16[800,128]{1,0:T(8,128)(2,1)S(1)} collective-permute-done((bf16[800,128]{1,0:T(8,128)(2,1)S(1)}, bf16[800,128]{1,0:T(8,128)(2,1)S(1)}, u32[]{:S(2)}, u32[]{:S(2)}) %collective-permute-start.14) | collective-permute-done | bytes 204832 | tf_op jit(solution)/shard_map/ppermute | solution.py:374
  76.0 2.2 %collective-permute-done.15.refs_3_ = bf16[800,128]{1,0:T(8,128)(2,1)S(1)} collective-permute-done((bf16[800,128]{1,0:T(8,128)(2,1)S(1)}, bf16[800,128]{1,0:T(8,128)(2,1)S(1)}, u32[]{:S(2)}, u32[]{:S(2)}) %collective-permute-start.15) | collective-permute-done | bytes 204832 | tf_op jit(solution)/shard_map/ppermute | solution.py:375
  78.3 4.7 %collective-permute-start.16 = (bf16[4,800,128]{2,1,0:T(8,128)(2,1)S(1)}, bf16[4,800,128]{2,1,0:T(8,128)(2,1)S(1)}, u32[]{:S(2)}, u32[]{:S(2)}) collective-permute-start(bf16[4,800,128]{2,1,0:T(8,128)(2,1)S(1)} %pad_maximum_fusion), channel_id=1, source_target_pairs={{0,1},{1,0},{2,3},{3,2},{4,5},{5,4},{6,7},{7,6},{8,9},{9,8},{10,11... | collective-permute-start | bytes 2457608 | tf_op jit(solution)/shard_map/ppermute | solution.py:370
  83.0 1.3 %shard_map.89 = (f32[512,512]{1,0:T(8,128)}, f32[512,512]{1,0:T(8,128)}, f32[2304,128]{1,0:T(8,128)}) custom-call(bf16[800,128]{1,0:T(8,128)(2,1)S(1)} %reduce-precision_convert_fusion.refs_0_, bf16[800,128]{1,0:T(8,128)(2,1)S(1)} %collective-permute-done.13.refs_1_, bf16[800,128]{1,0:T(8,128)(2,1)S(1)} %collective-permute-done.14.refs_2_, ...), custom_call_target="tpu_custom_call" | custom-call | flops 1048576 | bytes 3145728 | tf_op jit(solution)/shard_map/pallas_call | solution.py:323
  84.3 0.7 collective-permute-done.16.refs_0_
  85.0 1.3 %shard_map.90 = (f32[512,512]{1,0:T(8,128)}, f32[512,512]{1,0:T(8,128)}, f32[2304,128]{1,0:T(8,128)}) custom-call(bf16[4,800,128]{2,1,0:T(8,128)(2,1)S(1)} %collective-permute-done.16.refs_0_, f32[512,512]{1,0:T(8,128)} %get-tuple-element.64.refs_1_, ...), custom_call_target="tpu_custom_call", output_to_operand_aliasing={{0}: (1, {}), {1}: (2, {}), {2}: (3, {})} | custom-call | flops 1048576 | bytes 3145728 | tf_op jit(solution)/shard_map/pallas_call | solution.py:323
  (15 shorter events, 1.9 us)
Async XLA Ops:
  1.6 6.2 %collective-permute-start = (bf16[2,256,128]{2,1,0:T(8,128)(2,1)S(1)}, bf16[2,256,128]{2,1,0:T(8,128)(2,1)S(1)}, u32[]{:S(2)}, u32[]{:S(2)}) collective-permute-start(bf16[2,256,128]{2,1,0:T(8,128)(2,1)S(1)} %get-tuple-element.71), channel_id=1, source_target_pairs={{0,16},{16,0},{32,48},{48,32},{64,80},{80,64},{96,112},{112,96},{1... | collective-permute-start | bytes 393224 | tf_op jit(solution)/shard_map/ppermute | solution.py:431
  3.8 4.1 %collective-permute-start.1 = (bf16[2,256,128]{2,1,0:T(8,128)(2,1)S(1)}, bf16[2,256,128]{2,1,0:T(8,128)(2,1)S(1)}, u32[]{:S(2)}, u32[]{:S(2)}) collective-permute-start(bf16[2,256,128]{2,1,0:T(8,128)(2,1)S(1)} %get-tuple-element.70), channel_id=1, source_target_pairs={{16,32},{32,16},{48,64},{64,48},{80,96},{96,80},{17,33},{33,17},{4... | collective-permute-start | bytes 393224 | tf_op jit(solution)/shard_map/ppermute | solution.py:432
  7.9 19.1 %collective-permute-start.2 = (bf16[18,256,128]{2,1,0:T(8,128)(2,1)S(1)}, bf16[18,256,128]{2,1,0:T(8,128)(2,1)S(1)}, u32[]{:S(2)}, u32[]{:S(2)}) collective-permute-start(bf16[18,256,128]{2,1,0:T(8,128)(2,1)S(1)} %get-tuple-element.46.cot_a), channel_id=1, source_target_pairs={{1,0},{2,1},{3,2},{4,3},{5,4},{6,5},{7,6},{8,7},{9,8},{10,9},{11,1... | collective-permute-start | bytes 3538952 | tf_op jit(solution)/shard_map/ppermute | solution.py:416
  32.9 2.4 %collective-permute-start.3 = (bf16[4,800,128]{2,1,0:T(8,128)(2,1)S(1)}, bf16[4,800,128]{2,1,0:T(8,128)(2,1)S(1)}, u32[]{:S(2)}, u32[]{:S(2)}) collective-permute-start(bf16[4,800,128]{2,1,0:T(8,128)(2,1)S(1)} %get-tuple-element.56), channel_id=1, source_target_pairs={{0,1},{1,0},{2,3},{3,2},{4,5},{5,4},{6,7},{7,6},{8,9},{9,8},{10,11... | collective-permute-start | bytes 2457608 | tf_op jit(solution)/shard_map/ppermute | solution.py:370
  35.5 9.8 %collective-permute-start.4 = (bf16[800,128]{1,0:T(8,128)(2,1)S(1)}, bf16[800,128]{1,0:T(8,128)(2,1)S(1)}, u32[]{:S(2)}, u32[]{:S(2)}) collective-permute-start(bf16[800,128]{1,0:T(8,128)(2,1)S(1)} %get-tuple-element.72), channel_id=1, source_target_pairs={{0,8},{1,65},{2,10},{3,67},{4,12},{5,69},{6,14},{7,71},{8,0},{9,73... | collective-permute-start | bytes 614408 | tf_op jit(solution)/shard_map/ppermute | solution.py:374
  42.1 5.8 %collective-permute-start.5 = (bf16[800,128]{1,0:T(8,128)(2,1)S(1)}, bf16[800,128]{1,0:T(8,128)(2,1)S(1)}, u32[]{:S(2)}, u32[]{:S(2)}) collective-permute-start(bf16[800,128]{1,0:T(8,128)(2,1)S(1)} %get-tuple-element.74), channel_id=1, source_target_pairs={{0,4},{1,33},{2,6},{3,35},{4,8},{5,37},{6,10},{7,39},{8,12},{9,41}... | collective-permute-start | bytes 614408 | tf_op jit(solution)/shard_map/ppermute | solution.py:375
  42.5 5.4 %collective-permute-start.6 = (bf16[800,128]{1,0:T(8,128)(2,1)S(1)}, bf16[800,128]{1,0:T(8,128)(2,1)S(1)}, u32[]{:S(2)}, u32[]{:S(2)}) collective-permute-start(bf16[800,128]{1,0:T(8,128)(2,1)S(1)} %get-tuple-element.73), channel_id=1, source_target_pairs={{0,12},{1,97},{2,14},{3,99},{4,0},{5,101},{6,2},{7,103},{8,4},{9,1... | collective-permute-start | bytes 614408 | tf_op jit(solution)/shard_map/ppermute | solution.py:376
  48.1 6.2 %collective-permute-start.7 = (bf16[800,128]{1,0:T(8,128)(2,1)S(1)}, bf16[800,128]{1,0:T(8,128)(2,1)S(1)}, u32[]{:S(2)}, u32[]{:S(2)}) collective-permute-start(bf16[800,128]{1,0:T(8,128)(2,1)S(1)} %fusion.2), channel_id=1, source_target_pairs={{0,64},{1,3},{2,66},{3,1},{4,68},{5,7},{6,70},{7,5},{8,72},{9,11},... | collective-permute-start | bytes 614408 | tf_op jit(solution)/shard_map/ppermute | solution.py:374
  50.3 6.5 %collective-permute-start.8 = (bf16[800,128]{1,0:T(8,128)(2,1)S(1)}, bf16[800,128]{1,0:T(8,128)(2,1)S(1)}, u32[]{:S(2)}, u32[]{:S(2)}) collective-permute-start(bf16[800,128]{1,0:T(8,128)(2,1)S(1)} %fusion.2), channel_id=1, source_target_pairs={{0,32},{1,17},{2,34},{3,19},{4,36},{5,21},{6,38},{7,23},{8,40},{9,... | collective-permute-start | bytes 614408 | tf_op jit(solution)/shard_map/ppermute | solution.py:375
  51.3 5.6 %collective-permute-start.9 = (bf16[800,128]{1,0:T(8,128)(2,1)S(1)}, bf16[800,128]{1,0:T(8,128)(2,1)S(1)}, u32[]{:S(2)}, u32[]{:S(2)}) collective-permute-start(bf16[800,128]{1,0:T(8,128)(2,1)S(1)} %fusion.2), channel_id=1, source_target_pairs={{0,96},{1,19},{2,98},{3,17},{4,100},{5,23},{6,102},{7,21},{8,104},... | collective-permute-start | bytes 614408 | tf_op jit(solution)/shard_map/ppermute | solution.py:376
  57.1 6.6 %collective-permute-start.10 = (bf16[800,128]{1,0:T(8,128)(2,1)S(1)}, bf16[800,128]{1,0:T(8,128)(2,1)S(1)}, u32[]{:S(2)}, u32[]{:S(2)}) collective-permute-start(bf16[800,128]{1,0:T(8,128)(2,1)S(1)} %reduce-precision_convert_fusion.1), channel_id=1, source_target_pairs={{0,2},{1,9},{2,0},{3,11},{4,6},{5,13},{6,4},{7,15},{8,10},{9,1},{1... | collective-permute-start | bytes 614408 | tf_op jit(solution)/shard_map/ppermute | solution.py:374
  60.6 6.1 %collective-permute-start.11 = (bf16[800,128]{1,0:T(8,128)(2,1)S(1)}, bf16[800,128]{1,0:T(8,128)(2,1)S(1)}, u32[]{:S(2)}, u32[]{:S(2)}) collective-permute-start(bf16[800,128]{1,0:T(8,128)(2,1)S(1)} %reduce-precision_convert_fusion.1), channel_id=1, source_target_pairs={{0,16},{1,5},{2,18},{3,7},{4,20},{5,9},{6,22},{7,11},{8,24},{9,13}... | collective-permute-start | bytes 614408 | tf_op jit(solution)/shard_map/ppermute | solution.py:375
  61.0 5.7 %collective-permute-start.12 = (bf16[800,128]{1,0:T(8,128)(2,1)S(1)}, bf16[800,128]{1,0:T(8,128)(2,1)S(1)}, u32[]{:S(2)}, u32[]{:S(2)}) collective-permute-start(bf16[800,128]{1,0:T(8,128)(2,1)S(1)} %reduce-precision_convert_fusion.1), channel_id=1, source_target_pairs={{0,18},{1,13},{2,16},{3,15},{4,22},{5,1},{6,20},{7,3},{8,26},{9,5}... | collective-permute-start | bytes 614408 | tf_op jit(solution)/shard_map/ppermute | solution.py:376
  66.8 7.9 %collective-permute-start.13 = (bf16[800,128]{1,0:T(8,128)(2,1)S(1)}, bf16[800,128]{1,0:T(8,128)(2,1)S(1)}, u32[]{:S(2)}, u32[]{:S(2)}) collective-permute-start(bf16[800,128]{1,0:T(8,128)(2,1)S(1)} %reduce-precision_convert_fusion.refs_0_), channel_id=1, source_target_pairs={{0,12},{1,97},{2,14},{3,99},{4,0},{5,101},{6,2},{7,103},{8,4},{9,1... | collective-permute-start | bytes 614408 | tf_op jit(solution)/shard_map/ppermute | solution.py:376
  69.8 6.2 %collective-permute-start.14 = (bf16[800,128]{1,0:T(8,128)(2,1)S(1)}, bf16[800,128]{1,0:T(8,128)(2,1)S(1)}, u32[]{:S(2)}, u32[]{:S(2)}) collective-permute-start(bf16[800,128]{1,0:T(8,128)(2,1)S(1)} %reduce-precision_convert_fusion.refs_0_), channel_id=1, source_target_pairs={{0,8},{1,65},{2,10},{3,67},{4,12},{5,69},{6,14},{7,71},{8,0},{9,73... | collective-permute-start | bytes 614408 | tf_op jit(solution)/shard_map/ppermute | solution.py:374
  69.9 8.3 %collective-permute-start.15 = (bf16[800,128]{1,0:T(8,128)(2,1)S(1)}, bf16[800,128]{1,0:T(8,128)(2,1)S(1)}, u32[]{:S(2)}, u32[]{:S(2)}) collective-permute-start(bf16[800,128]{1,0:T(8,128)(2,1)S(1)} %reduce-precision_convert_fusion.refs_0_), channel_id=1, source_target_pairs={{0,4},{1,33},{2,6},{3,35},{4,8},{5,37},{6,10},{7,39},{8,12},{9,41}... | collective-permute-start | bytes 614408 | tf_op jit(solution)/shard_map/ppermute | solution.py:375
  78.3 6.6 %collective-permute-start.16 = (bf16[4,800,128]{2,1,0:T(8,128)(2,1)S(1)}, bf16[4,800,128]{2,1,0:T(8,128)(2,1)S(1)}, u32[]{:S(2)}, u32[]{:S(2)}) collective-permute-start(bf16[4,800,128]{2,1,0:T(8,128)(2,1)S(1)} %pad_maximum_fusion), channel_id=1, source_target_pairs={{0,1},{1,0},{2,3},{3,2},{4,5},{5,4},{6,7},{7,6},{8,9},{9,8},{10,11... | collective-permute-start | bytes 2457608 | tf_op jit(solution)/shard_map/ppermute | solution.py:370

commit v5 on v4

--- a/solution.py
+++ b/solution.py
@@ -180,8 +180,7 @@
 
 
 def early_kernel(lat, w1, w2, ker, act, slope, ft_a, cot_a, cot_b, *refs):
-    gl_h, part, gk, gw, act_b, slope_b, ft_b, taps, w1t, w2t = refs[:10]
-    planes_a, planes_b, spread, gm, gp, gl, sem = refs[10:]
+    part, gk, gw, act_b, slope_b, ft_b, taps, w1t, w2t, gm, gp, planes_a, planes_b, spread = refs
     n_px = gm.shape[0]
     mine = pl.ds(0, n_px)
     turn(w1, w2, ker, taps, w1t, w2t)
@@ -196,14 +195,10 @@
         y = k * STEP
         part[rows_of(k, STEP * 128)] = own_cells(planes_b, y) + conv(taps, 1, planes_b, y)
     gp[...] = (dot(gm[...], w2t[...]) * slope[...].astype(F32)).astype(BF)
-    gl[...] = (gm[...].astype(F32) + dot(gp[...], w1t[...])).astype(BF)
-    out = pltpu.make_async_copy(gl, gl_h.at[mine], sem)
-    out.start()
     add_weights(gw, ((lat.at[mine], gp), (act, gm)), None)
     project(lat[n_px : 2 * n_px], w1, w2, act_b, slope_b, ft_b)
     add_taps(gk, ft_a, 0, planes_b, None)
     add_taps(gk, ft_b, 1, planes_b, gk)
-    out.wait()
 
 
 def late_kernel(lat, act, slope, ft, taps, w2t, cells, part, sumk, sumw, gm, gp, keep, send, *scratch):
@@ -231,12 +226,16 @@
         packed[512:800, :] = jnp.where(b < 4, new, old).astype(BF)
 
 
-def last_kernel(gm, gp, w1t, _, gl_h, gl, sem):
-    n_px = gm.shape[0]
-    gl[...] = (gm[...].astype(F32) + dot(gp[...], w1t[...])).astype(BF)
-    out = pltpu.make_async_copy(gl, gl_h.at[pl.ds(n_px, n_px)], sem)
-    out.start()
-    out.wait()
+def last_kernel(gm_a, gp_a, gm_b, gp_b, w1t, gl_h, gl, sems):
+    n_px = gm_a.shape[0]
+    copies = []
+    for n, (gm, gp) in enumerate(((gm_a, gp_a), (gm_b, gp_b))):
+        here = pl.ds(n * n_px, n_px)
+        gl[here] = (gm[...].astype(F32) + dot(gp[...], w1t[...])).astype(BF)
+        copies.append(pltpu.make_async_copy(gl.at[here], gl_h.at[here], sems.at[n]))
+        copies[-1].start()
+    for copy in copies:
+        copy.wait()
 
 
 PLANES = (ROWS + 2, 128, 512)
@@ -249,15 +248,14 @@
     ops = in_vmem(lat, *rest)
     shapes = [pltpu.VMEM(shape, F32) for shape in [(ROWS * 128, 256)] + SUMS]
     shapes += [pltpu.VMEM(shape, BF) for shape in frame_shapes(n_px) + [(6, 512, 256), (512, 512), (512, 512)]]
+    shapes += [pltpu.VMEM((n_px, 512), BF)] * 2
     return pl.pallas_call(
         early_kernel,
         in_specs=[VMEM_SPEC] * len(ops),
-        out_specs=[ANY_SPEC] + [VMEM_SPEC] * len(shapes),
-        out_shape=[pltpu.HBM(lat.shape, BF)] + shapes,
+        out_specs=[VMEM_SPEC] * len(shapes),
+        out_shape=shapes,
         scratch_shapes=[pltpu.VMEM(PLANES, BF)] * 2
-        + [pltpu.VMEM(SPREAD, F32)]
-        + [pltpu.VMEM((n_px, 512), BF)] * 3
-        + [pltpu.SemaphoreType.DMA],
+        + [pltpu.VMEM(SPREAD, F32)],
         cost_estimate=pl.CostEstimate(flops=12 << 30, bytes_accessed=16 * MIB, transcendentals=0),
         compiler_params=pltpu.CompilerParams(vmem_limit_bytes=24 * MIB),
     )(*ops)
@@ -278,17 +276,17 @@
     )(*ops)
 
 
-def last(gm, gp, w1t, grad):
+def last(*ops):
+    shape = (2 * ops[0].shape[0], 512)
     return pl.pallas_call(
         last_kernel,
-        in_specs=[VMEM_SPEC] * 3 + [ANY_SPEC],
+        in_specs=[VMEM_SPEC] * 5,
         out_specs=ANY_SPEC,
-        out_shape=pltpu.HBM(grad.shape, BF),
-        input_output_aliases={3: 0},
-        scratch_shapes=[pltpu.VMEM(gm.shape, BF), pltpu.SemaphoreType.DMA],
-        cost_estimate=pl.CostEstimate(flops=1 << 29, bytes_accessed=4 * MIB, transcendentals=0),
+        out_shape=pltpu.HBM(shape, BF),
+        scratch_shapes=[pltpu.VMEM(shape, BF), pltpu.SemaphoreType.DMA((2,))],
+        cost_estimate=pl.CostEstimate(flops=1 << 30, bytes_accessed=8 * MIB, transcendentals=0),
         compiler_params=pltpu.CompilerParams(vmem_limit_bytes=8 * MIB),
-    )(*in_vmem(gm, gp, w1t), *in_hbm(grad))
+    )(*in_vmem(*ops))
 
 
 def unpack_kernel(side, *refs):
@@ -434,10 +432,10 @@
     cot_a, cot_b = border(inner, outer, cot_a, cot_b)
     later = neighbour(cot_a, "ta", -1)
     middle = early(lat, w1, w2, ker, act_a, slope_a, ft_a, cot_a, cot_b)
-    grad, part, gk, gw, act_b, slope_b, ft_b, taps, w1t, w2t = middle
+    part, gk, gw, act_b, slope_b, ft_b, taps, w1t, w2t, gm_a, gp_a = middle
     gm, gp, keep, send = late(lat, act_b, slope_b, ft_b, taps, w2t, later, part, gk, gw)
     got = swap(send)
-    grad = last(gm, gp, w1t, grad)
+    grad = last(gm_a, gp_a, gm, gp, w1t)
     got, grad = lax.optimization_barrier((got, grad))
     grad_first, grad_second, gk = sum_all(keep, got)
     return grad.reshape(latent.shape), grad_first, grad_second, gk.reshape(kernel.shape)

time: 86.6 us -> 86.9 us (level)
  transfers between devices with their start and end apart: 17 -> 17, of which waited for: 13 -> 12; matrix products, arithmetic and copies ran while one was open for 0% -> 0% of each run, Pallas kernels for 24% -> 24%
where the time goes in v5:
time: 86.9 us; the launch traced here: 86.7 us
  starting transfers between devices  35 us (40%)
  Pallas kernels  28 us (32%)
  waiting for transfers between devices  21.1 us (24%)
  other arithmetic  1.64 us (2%)
  between operations  0.95 us (1%)
    pallas_call x1, Pallas kernels, early(): pl.pallas_call(early_kernel, in_specs=[VMEM_SPEC] * len(ops), out_specs=[...  13.9 us
    ppermute x4, starting transfers between devices, trade(): across = lax.ppermute(far, BOTH, along(axes, step_by(2)))  12.7 us
    ppermute x4, waiting for transfers between devices, trade(): before = lax.ppermute(near, BOTH, along(axes, step_by(1)))  10.4 us
    ppermute x4, starting transfers between devices, trade(): after = lax.ppermute(last, BOTH, along(axes, step_by(3)))  9.52 us
    pallas_call x1, Pallas kernels, late(): pl.pallas_call(late_kernel, in_specs=[VMEM_SPEC] * len(ops), out_specs=[V...  5.91 us
    ppermute x2, starting transfers between devices, swap(): return lax.ppermute(value, BOTH, [(i, i ^ 1) for i in range(128)])  4.91 us
    ppermute x4, waiting for transfers between devices, trade(): after = lax.ppermute(last, BOTH, along(axes, step_by(3)))  4.23 us
    ppermute x4, waiting for transfers between devices, trade(): across = lax.ppermute(far, BOTH, along(axes, step_by(2)))  3.59 us
  transfers between devices with their start and end apart: 17, of which 12 were waited for; matrix products, arithmetic and copies ran while one was open for 0% of the time, Pallas kernels for 24%

profile of v5, /device:TPU:1, one launch (start us, length us, event | category | flops | bytes accessed | tf_op | source)
XLA Modules:
  0.0 86.7 jit_solution(10154395266221722445)
XLA Ops:
  0.6 1.0 %fusion.8 = (bf16[2,256,128]{2,1,0:T(8,128)(2,1)S(1)}, bf16[2,256,128]{2,1,0:T(8,128)(2,1)S(1)}) fusion(pred[]{:T(512)S(6)} %eq.6, bf16[2,16,256,128]{3,2,1,0:T(8,128)(2,1)} %cot_h.1), kind=kLoop, calls=%fused_computation.18 | loop fusion | flops 131072 | bytes 524289 | tf_op jit(solution)/shard_map/jit(_where)/select_n | solution.py:430
  1.6 2.1 %collective-permute-start = (bf16[2,256,128]{2,1,0:T(8,128)(2,1)S(1)}, bf16[2,256,128]{2,1,0:T(8,128)(2,1)S(1)}, u32[]{:S(2)}, u32[]{:S(2)}) collective-permute-start(bf16[2,256,128]{2,1,0:T(8,128)(2,1)S(1)} %get-tuple-element.73), channel_id=1, source_target_pairs={{0,16},{16,0},{32,48},{48,32},{64,80},{80,64},{96,112},{112,96},{1... | collective-permute-start | bytes 393224 | tf_op jit(solution)/shard_map/ppermute | solution.py:429
  3.8 0.7 collective-permute-start.1
  4.4 3.4 %shard_map.84 = (bf16[2048,512]{1,0:T(8,128)(2,1)S(1)}, bf16[512,512]{1,0:T(8,128)(2,1)S(1)}, bf16[512,512]{1,0:T(8,128)(2,1)S(1)}, bf16[18,128,128]{2,1,0:T(8,1...) custom-call(bf16[2048,512]{1,0:T(8,128)(2,1)} %bitcast.39, ...), custom_call_target="tpu_custom_call" | custom-call | flops 2147483648 | bytes 8388608 | tf_op jit(solution)/shard_map/pallas_call | solution.py:86
  7.9 3.0 %collective-permute-start.2 = (bf16[18,256,128]{2,1,0:T(8,128)(2,1)S(1)}, bf16[18,256,128]{2,1,0:T(8,128)(2,1)S(1)}, u32[]{:S(2)}, u32[]{:S(2)}) collective-permute-start(bf16[18,256,128]{2,1,0:T(8,128)(2,1)S(1)} %get-tuple-element.47.cot_a), channel_id=1, source_target_pairs={{1,0},{2,1},{3,2},{4,3},{5,4},{6,5},{7,6},{8,7},{9,8},{10,9},{11,1... | collective-permute-start | bytes 3538952 | tf_op jit(solution)/shard_map/ppermute | solution.py:414
  11.0 13.9 %shard_map.86 = (f32[2048,256]{1,0:T(8,128)S(1)}, f32[2304,128]{1,0:T(8,128)S(1)}, f32[1024,512]{1,0:T(8,128)S(1)}, bf16[1024,512]{1,0:T(8,128)(2,1)S(1)}, bf16[...) custom-call(bf16[2048,512]{1,0:T(8,128)(2,1)S(1)} %get-tuple-element, ...), custom_call_target="tpu_custom_call" | custom-call | flops 12884901888 | bytes 16777216 | tf_op jit(solution)/shard_map/pallas_call | solution.py:252
  24.8 2.1 %collective-permute-done.2.cells = bf16[18,256,128]{2,1,0:T(8,128)(2,1)S(1)} collective-permute-done((bf16[18,256,128]{2,1,0:T(8,128)(2,1)S(1)}, bf16[18,256,128]{2,1,0:T(8,128)(2,1)S(1)}, u32[]{:S(2)}, u32[]{:S(2)}) %collective-permute-start.2) | collective-permute-done | bytes 1179680 | tf_op jit(solution)/shard_map/ppermute | solution.py:414
  27.0 5.9 %shard_map.87 = (bf16[1024,512]{1,0:T(8,128)(2,1)S(1)}, bf16[1024,512]{1,0:T(8,128)(2,1)S(1)}, bf16[4,800,128]{2,1,0:T(8,128)(2,1)S(1)}, bf16[4,800,128]{2,1,0:T(8,128)(2,1)S(1)}) custom-call(bf16[2048,512]{1,0:T(8,128)(2,1)S(1)} %get-tuple-element.38.lat, bf16[1024,512]{1,0:T(8,128)(2,1)S(1)} %get-tuple-element.49.act, ...), custom_call_target="tpu_custom_call" | custom-call | flops 6442450944 | bytes 16777216 | tf_op jit(solution)/shard_map/pallas_call | solution.py:267
  33.0 2.2 %shard_map.88 = bf16[2048,512]{1,0:T(8,128)(2,1)} custom-call(bf16[1024,512]{1,0:T(8,128)(2,1)S(1)} %get-tuple-element.58.gm_a, bf16[1024,512]{1,0:T(8,128)(2,1)S(1)} %get-tuple-element.59.gp_a, bf16[1024,512]{1,0:T(8,128)(2,1)S(1)} %get-tuple-element.60.gm_b, bf16[1024,512]{1,0:T(8,128)(2,1)S(1)} %get-tuple-element.61.gp_b, ...), custom_call_target="tpu_custom_call" | custom-call | flops 1073741824 | bytes 8388608 | tf_op jit(solution)/shard_map/pallas_call | solution.py:281
  35.5 6.6 %collective-permute-start.4 = (bf16[800,128]{1,0:T(8,128)(2,1)S(1)}, bf16[800,128]{1,0:T(8,128)(2,1)S(1)}, u32[]{:S(2)}, u32[]{:S(2)}) collective-permute-start(bf16[800,128]{1,0:T(8,128)(2,1)S(1)} %get-tuple-element.74), channel_id=1, source_target_pairs={{0,8},{1,65},{2,10},{3,67},{4,12},{5,69},{6,14},{7,71},{8,0},{9,73... | collective-permute-start | bytes 614408 | tf_op jit(solution)/shard_map/ppermute | solution.py:372
  42.5 2.3 %collective-permute-start.6 = (bf16[800,128]{1,0:T(8,128)(2,1)S(1)}, bf16[800,128]{1,0:T(8,128)(2,1)S(1)}, u32[]{:S(2)}, u32[]{:S(2)}) collective-permute-start(bf16[800,128]{1,0:T(8,128)(2,1)S(1)} %get-tuple-element.75), channel_id=1, source_target_pairs={{0,12},{1,97},{2,14},{3,99},{4,0},{5,101},{6,2},{7,103},{8,4},{9,1... | collective-permute-start | bytes 614408 | tf_op jit(solution)/shard_map/ppermute | solution.py:374
  44.8 0.5 collective-permute-done.4
  45.3 2.7 %collective-permute-done.5 = bf16[800,128]{1,0:T(8,128)(2,1)S(1)} collective-permute-done((bf16[800,128]{1,0:T(8,128)(2,1)S(1)}, bf16[800,128]{1,0:T(8,128)(2,1)S(1)}, u32[]{:S(2)}, u32[]{:S(2)}) %collective-permute-start.5) | collective-permute-done | bytes 204832 | tf_op jit(solution)/shard_map/ppermute | solution.py:373
  48.1 2.2 %collective-permute-start.7 = (bf16[800,128]{1,0:T(8,128)(2,1)S(1)}, bf16[800,128]{1,0:T(8,128)(2,1)S(1)}, u32[]{:S(2)}, u32[]{:S(2)}) collective-permute-start(bf16[800,128]{1,0:T(8,128)(2,1)S(1)} %fusion.2), channel_id=1, source_target_pairs={{0,64},{1,3},{2,66},{3,1},{4,68},{5,7},{6,70},{7,5},{8,72},{9,11},... | collective-permute-start | bytes 614408 | tf_op jit(solution)/shard_map/ppermute | solution.py:372
  50.3 0.7 collective-permute-start.8
  51.0 1.9 %collective-permute-start.9 = (bf16[800,128]{1,0:T(8,128)(2,1)S(1)}, bf16[800,128]{1,0:T(8,128)(2,1)S(1)}, u32[]{:S(2)}, u32[]{:S(2)}) collective-permute-start(bf16[800,128]{1,0:T(8,128)(2,1)S(1)} %fusion.2), channel_id=1, source_target_pairs={{0,96},{1,19},{2,98},{3,17},{4,100},{5,23},{6,102},{7,21},{8,104},... | collective-permute-start | bytes 614408 | tf_op jit(solution)/shard_map/ppermute | solution.py:374
  53.0 1.3 %collective-permute-done.7 = bf16[800,128]{1,0:T(8,128)(2,1)S(1)} collective-permute-done((bf16[800,128]{1,0:T(8,128)(2,1)S(1)}, bf16[800,128]{1,0:T(8,128)(2,1)S(1)}, u32[]{:S(2)}, u32[]{:S(2)}) %collective-permute-start.7) | collective-permute-done | bytes 204832 | tf_op jit(solution)/shard_map/ppermute | solution.py:372
  54.3 2.5 %collective-permute-done.8 = bf16[800,128]{1,0:T(8,128)(2,1)S(1)} collective-permute-done((bf16[800,128]{1,0:T(8,128)(2,1)S(1)}, bf16[800,128]{1,0:T(8,128)(2,1)S(1)}, u32[]{:S(2)}, u32[]{:S(2)}) %collective-permute-start.8) | collective-permute-done | bytes 204832 | tf_op jit(solution)/shard_map/ppermute | solution.py:373
  56.9 3.7 %collective-permute-start.10 = (bf16[800,128]{1,0:T(8,128)(2,1)S(1)}, bf16[800,128]{1,0:T(8,128)(2,1)S(1)}, u32[]{:S(2)}, u32[]{:S(2)}) collective-permute-start(bf16[800,128]{1,0:T(8,128)(2,1)S(1)} %reduce-precision_convert_fusion.1), channel_id=1, source_target_pairs={{0,2},{1,9},{2,0},{3,11},{4,6},{5,13},{6,4},{7,15},{8,10},{9,1},{1... | collective-permute-start | bytes 614408 | tf_op jit(solution)/shard_map/ppermute | solution.py:372
  60.6 0.4 collective-permute-start.11
  61.0 2.2 %collective-permute-start.12 = (bf16[800,128]{1,0:T(8,128)(2,1)S(1)}, bf16[800,128]{1,0:T(8,128)(2,1)S(1)}, u32[]{:S(2)}, u32[]{:S(2)}) collective-permute-start(bf16[800,128]{1,0:T(8,128)(2,1)S(1)} %reduce-precision_convert_fusion.1), channel_id=1, source_target_pairs={{0,18},{1,13},{2,16},{3,15},{4,22},{5,1},{6,20},{7,3},{8,26},{9,5}... | collective-permute-start | bytes 614408 | tf_op jit(solution)/shard_map/ppermute | solution.py:374
  63.2 0.5 collective-permute-done.10
  63.7 3.0 %collective-permute-done.11 = bf16[800,128]{1,0:T(8,128)(2,1)S(1)} collective-permute-done((bf16[800,128]{1,0:T(8,128)(2,1)S(1)}, bf16[800,128]{1,0:T(8,128)(2,1)S(1)}, u32[]{:S(2)}, u32[]{:S(2)}) %collective-permute-start.11) | collective-permute-done | bytes 204832 | tf_op jit(solution)/shard_map/ppermute | solution.py:373
  66.8 3.1 %collective-permute-start.13 = (bf16[800,128]{1,0:T(8,128)(2,1)S(1)}, bf16[800,128]{1,0:T(8,128)(2,1)S(1)}, u32[]{:S(2)}, u32[]{:S(2)}) collective-permute-start(bf16[800,128]{1,0:T(8,128)(2,1)S(1)} %reduce-precision_convert_fusion.refs_0_), channel_id=1, source_target_pairs={{0,12},{1,97},{2,14},{3,99},{4,0},{5,101},{6,2},{7,103},{8,4},{9,1... | collective-permute-start | bytes 614408 | tf_op jit(solution)/shard_map/ppermute | solution.py:374
  70.1 0.5 collective-permute-start.15
  70.5 4.2 %collective-permute-done.13.refs_1_ = bf16[800,128]{1,0:T(8,128)(2,1)S(1)} collective-permute-done((bf16[800,128]{1,0:T(8,128)(2,1)S(1)}, bf16[800,128]{1,0:T(8,128)(2,1)S(1)}, u32[]{:S(2)}, u32[]{:S(2)}) %collective-permute-start.13) | collective-permute-done | bytes 204832 | tf_op jit(solution)/shard_map/ppermute | solution.py:374
  74.8 1.3 %collective-permute-done.14.refs_2_ = bf16[800,128]{1,0:T(8,128)(2,1)S(1)} collective-permute-done((bf16[800,128]{1,0:T(8,128)(2,1)S(1)}, bf16[800,128]{1,0:T(8,128)(2,1)S(1)}, u32[]{:S(2)}, u32[]{:S(2)}) %collective-permute-start.14) | collective-permute-done | bytes 204832 | tf_op jit(solution)/shard_map/ppermute | solution.py:372
  76.1 2.3 %collective-permute-done.15.refs_3_ = bf16[800,128]{1,0:T(8,128)(2,1)S(1)} collective-permute-done((bf16[800,128]{1,0:T(8,128)(2,1)S(1)}, bf16[800,128]{1,0:T(8,128)(2,1)S(1)}, u32[]{:S(2)}, u32[]{:S(2)}) %collective-permute-start.15) | collective-permute-done | bytes 204832 | tf_op jit(solution)/shard_map/ppermute | solution.py:373
  78.5 4.8 %collective-permute-start.16 = (bf16[4,800,128]{2,1,0:T(8,128)(2,1)S(1)}, bf16[4,800,128]{2,1,0:T(8,128)(2,1)S(1)}, u32[]{:S(2)}, u32[]{:S(2)}) collective-permute-start(bf16[4,800,128]{2,1,0:T(8,128)(2,1)S(1)} %pad_maximum_fusion), channel_id=1, source_target_pairs={{0,1},{1,0},{2,3},{3,2},{4,5},{5,4},{6,7},{7,6},{8,9},{9,8},{10,11... | collective-permute-start | bytes 2457608 | tf_op jit(solution)/shard_map/ppermute | solution.py:368
  83.3 1.3 %shard_map.89 = (f32[512,512]{1,0:T(8,128)}, f32[512,512]{1,0:T(8,128)}, f32[2304,128]{1,0:T(8,128)}) custom-call(bf16[800,128]{1,0:T(8,128)(2,1)S(1)} %reduce-precision_convert_fusion.refs_0_, bf16[800,128]{1,0:T(8,128)(2,1)S(1)} %collective-permute-done.13.refs_1_, bf16[800,128]{1,0:T(8,128)(2,1)S(1)} %collective-permute-done.14.refs_2_, ...), custom_call_target="tpu_custom_call" | custom-call | flops 1048576 | bytes 3145728 | tf_op jit(solution)/shard_map/pallas_call | solution.py:321
  84.6 0.7 collective-permute-done.16.refs_0_
  85.3 1.3 %shard_map.90 = (f32[512,512]{1,0:T(8,128)}, f32[512,512]{1,0:T(8,128)}, f32[2304,128]{1,0:T(8,128)}) custom-call(bf16[4,800,128]{2,1,0:T(8,128)(2,1)S(1)} %collective-permute-done.16.refs_0_, f32[512,512]{1,0:T(8,128)} %get-tuple-element.66.refs_1_, ...), custom_call_target="tpu_custom_call", output_to_operand_aliasing={{0}: (1, {}), {1}: (2, {}), {2}: (3, {})} | custom-call | flops 1048576 | bytes 3145728 | tf_op jit(solution)/shard_map/pallas_call | solution.py:321
  (15 shorter events, 1.4 us)
Async XLA Ops:
  1.6 6.2 %collective-permute-start = (bf16[2,256,128]{2,1,0:T(8,128)(2,1)S(1)}, bf16[2,256,128]{2,1,0:T(8,128)(2,1)S(1)}, u32[]{:S(2)}, u32[]{:S(2)}) collective-permute-start(bf16[2,256,128]{2,1,0:T(8,128)(2,1)S(1)} %get-tuple-element.73), channel_id=1, source_target_pairs={{0,16},{16,0},{32,48},{48,32},{64,80},{80,64},{96,112},{112,96},{1... | collective-permute-start | bytes 393224 | tf_op jit(solution)/shard_map/ppermute | solution.py:429
  3.8 4.1 %collective-permute-start.1 = (bf16[2,256,128]{2,1,0:T(8,128)(2,1)S(1)}, bf16[2,256,128]{2,1,0:T(8,128)(2,1)S(1)}, u32[]{:S(2)}, u32[]{:S(2)}) collective-permute-start(bf16[2,256,128]{2,1,0:T(8,128)(2,1)S(1)} %get-tuple-element.72), channel_id=1, source_target_pairs={{16,32},{32,16},{48,64},{64,48},{80,96},{96,80},{17,33},{33,17},{4... | collective-permute-start | bytes 393224 | tf_op jit(solution)/shard_map/ppermute | solution.py:430
  7.9 19.1 %collective-permute-start.2 = (bf16[18,256,128]{2,1,0:T(8,128)(2,1)S(1)}, bf16[18,256,128]{2,1,0:T(8,128)(2,1)S(1)}, u32[]{:S(2)}, u32[]{:S(2)}) collective-permute-start(bf16[18,256,128]{2,1,0:T(8,128)(2,1)S(1)} %get-tuple-element.47.cot_a), channel_id=1, source_target_pairs={{1,0},{2,1},{3,2},{4,3},{5,4},{6,5},{7,6},{8,7},{9,8},{10,9},{11,1... | collective-permute-start | bytes 3538952 | tf_op jit(solution)/shard_map/ppermute | solution.py:414
  32.9 2.4 %collective-permute-start.3 = (bf16[4,800,128]{2,1,0:T(8,128)(2,1)S(1)}, bf16[4,800,128]{2,1,0:T(8,128)(2,1)S(1)}, u32[]{:S(2)}, u32[]{:S(2)}) collective-permute-start(bf16[4,800,128]{2,1,0:T(8,128)(2,1)S(1)} %get-tuple-element.57), channel_id=1, source_target_pairs={{0,1},{1,0},{2,3},{3,2},{4,5},{5,4},{6,7},{7,6},{8,9},{9,8},{10,11... | collective-permute-start | bytes 2457608 | tf_op jit(solution)/shard_map/ppermute | solution.py:368
  35.5 9.8 %collective-permute-start.4 = (bf16[800,128]{1,0:T(8,128)(2,1)S(1)}, bf16[800,128]{1,0:T(8,128)(2,1)S(1)}, u32[]{:S(2)}, u32[]{:S(2)}) collective-permute-start(bf16[800,128]{1,0:T(8,128)(2,1)S(1)} %get-tuple-element.74), channel_id=1, source_target_pairs={{0,8},{1,65},{2,10},{3,67},{4,12},{5,69},{6,14},{7,71},{8,0},{9,73... | collective-permute-start | bytes 614408 | tf_op jit(solution)/shard_map/ppermute | solution.py:372
  42.1 5.8 %collective-permute-start.5 = (bf16[800,128]{1,0:T(8,128)(2,1)S(1)}, bf16[800,128]{1,0:T(8,128)(2,1)S(1)}, u32[]{:S(2)}, u32[]{:S(2)}) collective-permute-start(bf16[800,128]{1,0:T(8,128)(2,1)S(1)} %get-tuple-element.76), channel_id=1, source_target_pairs={{0,4},{1,33},{2,6},{3,35},{4,8},{5,37},{6,10},{7,39},{8,12},{9,41}... | collective-permute-start | bytes 614408 | tf_op jit(solution)/shard_map/ppermute | solution.py:373
  42.5 5.4 %collective-permute-start.6 = (bf16[800,128]{1,0:T(8,128)(2,1)S(1)}, bf16[800,128]{1,0:T(8,128)(2,1)S(1)}, u32[]{:S(2)}, u32[]{:S(2)}) collective-permute-start(bf16[800,128]{1,0:T(8,128)(2,1)S(1)} %get-tuple-element.75), channel_id=1, source_target_pairs={{0,12},{1,97},{2,14},{3,99},{4,0},{5,101},{6,2},{7,103},{8,4},{9,1... | collective-permute-start | bytes 614408 | tf_op jit(solution)/shard_map/ppermute | solution.py:374
  48.1 6.2 %collective-permute-start.7 = (bf16[800,128]{1,0:T(8,128)(2,1)S(1)}, bf16[800,128]{1,0:T(8,128)(2,1)S(1)}, u32[]{:S(2)}, u32[]{:S(2)}) collective-permute-start(bf16[800,128]{1,0:T(8,128)(2,1)S(1)} %fusion.2), channel_id=1, source_target_pairs={{0,64},{1,3},{2,66},{3,1},{4,68},{5,7},{6,70},{7,5},{8,72},{9,11},... | collective-permute-start | bytes 614408 | tf_op jit(solution)/shard_map/ppermute | solution.py:372
  50.3 6.5 %collective-permute-start.8 = (bf16[800,128]{1,0:T(8,128)(2,1)S(1)}, bf16[800,128]{1,0:T(8,128)(2,1)S(1)}, u32[]{:S(2)}, u32[]{:S(2)}) collective-permute-start(bf16[800,128]{1,0:T(8,128)(2,1)S(1)} %fusion.2), channel_id=1, source_target_pairs={{0,32},{1,17},{2,34},{3,19},{4,36},{5,21},{6,38},{7,23},{8,40},{9,... | collective-permute-start | bytes 614408 | tf_op jit(solution)/shard_map/ppermute | solution.py:373
  51.0 5.7 %collective-permute-start.9 = (bf16[800,128]{1,0:T(8,128)(2,1)S(1)}, bf16[800,128]{1,0:T(8,128)(2,1)S(1)}, u32[]{:S(2)}, u32[]{:S(2)}) collective-permute-start(bf16[800,128]{1,0:T(8,128)(2,1)S(1)} %fusion.2), channel_id=1, source_target_pairs={{0,96},{1,19},{2,98},{3,17},{4,100},{5,23},{6,102},{7,21},{8,104},... | collective-permute-start | bytes 614408 | tf_op jit(solution)/shard_map/ppermute | solution.py:374
  56.9 6.8 %collective-permute-start.10 = (bf16[800,128]{1,0:T(8,128)(2,1)S(1)}, bf16[800,128]{1,0:T(8,128)(2,1)S(1)}, u32[]{:S(2)}, u32[]{:S(2)}) collective-permute-start(bf16[800,128]{1,0:T(8,128)(2,1)S(1)} %reduce-precision_convert_fusion.1), channel_id=1, source_target_pairs={{0,2},{1,9},{2,0},{3,11},{4,6},{5,13},{6,4},{7,15},{8,10},{9,1},{1... | collective-permute-start | bytes 614408 | tf_op jit(solution)/shard_map/ppermute | solution.py:372
  60.6 6.1 %collective-permute-start.11 = (bf16[800,128]{1,0:T(8,128)(2,1)S(1)}, bf16[800,128]{1,0:T(8,128)(2,1)S(1)}, u32[]{:S(2)}, u32[]{:S(2)}) collective-permute-start(bf16[800,128]{1,0:T(8,128)(2,1)S(1)} %reduce-precision_convert_fusion.1), channel_id=1, source_target_pairs={{0,16},{1,5},{2,18},{3,7},{4,20},{5,9},{6,22},{7,11},{8,24},{9,13}... | collective-permute-start | bytes 614408 | tf_op jit(solution)/shard_map/ppermute | solution.py:373
  61.0 5.7 %collective-permute-start.12 = (bf16[800,128]{1,0:T(8,128)(2,1)S(1)}, bf16[800,128]{1,0:T(8,128)(2,1)S(1)}, u32[]{:S(2)}, u32[]{:S(2)}) collective-permute-start(bf16[800,128]{1,0:T(8,128)(2,1)S(1)} %reduce-precision_convert_fusion.1), channel_id=1, source_target_pairs={{0,18},{1,13},{2,16},{3,15},{4,22},{5,1},{6,20},{7,3},{8,26},{9,5}... | collective-permute-start | bytes 614408 | tf_op jit(solution)/shard_map/ppermute | solution.py:374
  66.8 8.0 %collective-permute-start.13 = (bf16[800,128]{1,0:T(8,128)(2,1)S(1)}, bf16[800,128]{1,0:T(8,128)(2,1)S(1)}, u32[]{:S(2)}, u32[]{:S(2)}) collective-permute-start(bf16[800,128]{1,0:T(8,128)(2,1)S(1)} %reduce-precision_convert_fusion.refs_0_), channel_id=1, source_target_pairs={{0,12},{1,97},{2,14},{3,99},{4,0},{5,101},{6,2},{7,103},{8,4},{9,1... | collective-permute-start | bytes 614408 | tf_op jit(solution)/shard_map/ppermute | solution.py:374
  69.9 6.2 %collective-permute-start.14 = (bf16[800,128]{1,0:T(8,128)(2,1)S(1)}, bf16[800,128]{1,0:T(8,128)(2,1)S(1)}, u32[]{:S(2)}, u32[]{:S(2)}) collective-permute-start(bf16[800,128]{1,0:T(8,128)(2,1)S(1)} %reduce-precision_convert_fusion.refs_0_), channel_id=1, source_target_pairs={{0,8},{1,65},{2,10},{3,67},{4,12},{5,69},{6,14},{7,71},{8,0},{9,73... | collective-permute-start | bytes 614408 | tf_op jit(solution)/shard_map/ppermute | solution.py:372
  70.1 8.3 %collective-permute-start.15 = (bf16[800,128]{1,0:T(8,128)(2,1)S(1)}, bf16[800,128]{1,0:T(8,128)(2,1)S(1)}, u32[]{:S(2)}, u32[]{:S(2)}) collective-permute-start(bf16[800,128]{1,0:T(8,128)(2,1)S(1)} %reduce-precision_convert_fusion.refs_0_), channel_id=1, source_target_pairs={{0,4},{1,33},{2,6},{3,35},{4,8},{5,37},{6,10},{7,39},{8,12},{9,41}... | collective-permute-start | bytes 614408 | tf_op jit(solution)/shard_map/ppermute | solution.py:373
  78.5 6.8 %collective-permute-start.16 = (bf16[4,800,128]{2,1,0:T(8,128)(2,1)S(1)}, bf16[4,800,128]{2,1,0:T(8,128)(2,1)S(1)}, u32[]{:S(2)}, u32[]{:S(2)}) collective-permute-start(bf16[4,800,128]{2,1,0:T(8,128)(2,1)S(1)} %pad_maximum_fusion), channel_id=1, source_target_pairs={{0,1},{1,0},{2,3},{3,2},{4,5},{5,4},{6,7},{7,6},{8,9},{9,8},{10,11... | collective-permute-start | bytes 2457608 | tf_op jit(solution)/shard_map/ppermute | solution.py:368
